TPU v7x, 32 devices: a whole 2x2x4 slice. The times are simulated.
32 devices in a mesh: dp: 2 (over core), gx: 4 (over y, x), gy: 4 (over z).
Axes of the slice: x: 2, y: 2, z: 4, core: 2. Of those that a mesh axis runs over, the one named last changes fastest.
Arguments:
- hidden_in: bfloat16 [2, 2048, 1088], P(None, ('dp', 'gy'), 'gx'), may hold values from -6 to 6
- segment_ids: int32 [2, 2048], P(None, 'dp'), may hold values from 0 to 31, as said below
- cotangent: bfloat16 [2, 2048, 1088], P(None, ('dp', 'gy'), 'gx'), may hold values from -6 to 6
- norm1_gain: bfloat16 [1088], replicated, may hold values from 0.5 to 1.5
- norm1_shift: bfloat16 [1088], replicated, may hold values from -1.75 to 1.75
- w_qkv: bfloat16 [1088, 3264], P('gx', 'gy'), may hold values from -0.1875 to 0.1875
- q_bias: bfloat16 [1088], replicated, may hold values from -1.75 to 1.75
- v_bias: bfloat16 [1088], replicated, may hold values from -0.1875 to 0.1875
- w_out: bfloat16 [1088, 1088], P('gy', 'gx'), may hold values from -1.5 to 1.5
- out_bias: bfloat16 [1088], replicated, may hold values from -1.75 to 1.75
- norm2_gain: bfloat16 [1088], replicated, may hold values from 0.5 to 1.5
- norm2_shift: bfloat16 [1088], replicated, may hold values from -1.75 to 1.75
- w_up: bfloat16 [1088, 4352], P('gx', 'gy'), may hold values from -0.1875 to 0.1875
- up_bias: bfloat16 [4352], replicated, may hold values from -1.75 to 1.75
- w_down: bfloat16 [4352, 1088], P('gy', 'gx'), may hold values from -0.09375 to 0.09375
- down_bias: bfloat16 [1088], replicated, may hold values from -1.75 to 1.75
Outputs:
- hidden_out: bfloat16 [2, 2048, 1088], P(None, ('dp', 'gy'), 'gx')
- grad_in: bfloat16 [2, 2048, 1088], P(None, ('dp', 'gy'), 'gx')
- grad_norm1_gain: float32 [1088], replicated
- grad_norm1_shift: float32 [1088], replicated
- grad_w_qkv: float32 [1088, 3264], P('gx', 'gy')
- grad_q_bias: float32 [1088], replicated
- grad_v_bias: float32 [1088], replicated
- grad_w_out: float32 [1088, 1088], P('gy', 'gx')
- grad_out_bias: float32 [1088], replicated
- grad_norm2_gain: float32 [1088], replicated
- grad_norm2_shift: float32 [1088], replicated
- grad_w_up: float32 [1088, 4352], P('gx', 'gy')
- grad_up_bias: float32 [4352], replicated
- grad_w_down: float32 [4352, 1088], P('gy', 'gx')
- grad_down_bias: float32 [1088], replicated
Inputs may be any that keep to these rules, and one draw needn't show every extreme that they name: `segment_ids`: documents never span two sequences of 1024 tokens; numbers rise along a sequence, its documents but the last are numbered upward from 8 times the sequence's place in the whole array, and its last document is numbered 8 times that place plus 7. Every document but the last of a sequence has 200 to 1000 tokens; the last is cut at the sequence's end, so a sequence holds 2 to 6 documents.
All inputs are finite; a program needn't handle non-finite values.
Results may differ from a plain program's by a relative error of at most 0.014.
Values may be sent and summed in bfloat16 or wider, within the bound.
No kernel may reach another device: no remote copies, remote signals or barrier semaphores. Data moves between devices by JAX's collectives and lax.ppermute only.
A program may use at most 128 MiB of HBM per device.

v0:
```python
from functools import partial

import jax
import jax.numpy as jnp
from jax import lax
from jax.sharding import PartitionSpec as P

D = 1088
HEAD_DIM = 64


epsilon = 1e-05
blocked_score = -1e30


def rows_over_gy(local_rows):
    return lax.all_gather(local_rows, "gy", axis=0, tiled=True)


def rows_over_gx(local_rows):
    return lax.all_gather(local_rows, "gx", axis=0, tiled=True)


def to_tokens(column_block):
    return lax.all_to_all(column_block, "gy", split_axis=0, concat_axis=1, tiled=True)


def to_columns(token_block):
    return lax.all_to_all(token_block, "gy", split_axis=1, concat_axis=0, tiled=True)


def multiply(piece, weight, flipped):
    if flipped:
        return lax.dot_general(
            piece, weight, (((1,), (1,)), ((), ())), preferred_element_type=jnp.float32
        )
    return jnp.dot(piece, weight, preferred_element_type=jnp.float32)


def contract_rows(left, right):
    return lax.dot_general(
        left, right, (((0,), (0,)), ((), ())), preferred_element_type=jnp.float32
    )


def summed_over_gx(whole, weight, flipped):
    own_rows = whole.shape[0] // lax.axis_size("gx")

    def partial_term(first_row, row_count):
        return multiply(whole, weight, flipped)

    return lax.psum_scatter(
        partial_term(jnp.int32(0), lax.axis_size("gx") * own_rows),
        "gx",
        scatter_dimension=0,
        tiled=True,
    )


def summed_over_gy(whole, weight, flipped):
    own_rows = whole.shape[0] // lax.axis_size("gy")

    def partial_term(first_row, row_count):
        return multiply(whole, weight, flipped)

    return lax.psum_scatter(
        partial_term(jnp.int32(0), lax.axis_size("gy") * own_rows),
        "gy",
        scatter_dimension=0,
        tiled=True,
    )


def column_sums(first_part, second_part):
    return lax.psum((first_part, second_part), "gx")


def norm_forward(values_in, gain_part, shift_part):
    totals = column_sums(jnp.sum(values_in, axis=1), jnp.sum(values_in * values_in, axis=1))
    average = totals[0] / D
    variance = totals[1] / D - average * average
    inverse = lax.rsqrt(variance + epsilon)
    centered = (values_in - average[:, None]) * inverse[:, None]
    return (centered * gain_part + shift_part, centered, inverse)


def norm_backward(upstream, centered, inverse, gain_part):
    scaled = upstream * gain_part
    totals = column_sums(jnp.sum(scaled, axis=1), jnp.sum(scaled * centered, axis=1))
    result = inverse[:, None] * (
        scaled - totals[0][:, None] / D - centered * (totals[1][:, None] / D)
    )
    return (result, jnp.sum(upstream * centered, axis=0), jnp.sum(upstream, axis=0))


def local_part(vector, index, parts):
    width = vector.shape[0] // parts
    return lax.dynamic_slice_in_dim(vector.astype(jnp.float32), index * width, width, 0)


def placed(part_vector, index, total_width):
    return lax.dynamic_update_slice_in_dim(
        jnp.zeros((total_width,), jnp.float32), part_vector, index * part_vector.shape[0], 0
    )


def head_groups(head_total):
    group_size = -(-head_total // 4)
    return [
        (first_head, min(group_size, head_total - first_head))
        for first_head in range(0, head_total, group_size)
    ]


def paired_heads(kv_local, head_total):
    row_total = kv_local.shape[0]
    width = head_total * HEAD_DIM
    key_part = kv_local[:, :width].reshape(row_total, head_total, 1, HEAD_DIM)
    value_part = kv_local[:, width:].reshape(row_total, head_total, 1, HEAD_DIM)
    return jnp.concatenate([key_part, value_part], axis=2).reshape(
        row_total, head_total * 2 * HEAD_DIM
    )


def gather_group(paired, first_head, head_count):
    chosen = lax.slice_in_dim(
        paired, first_head * 2 * HEAD_DIM, (first_head + head_count) * 2 * HEAD_DIM, axis=1
    )
    return lax.all_gather(chosen, ("gx", "gy"), axis=0, tiled=True)


def score_rows(query_head, key_head, allowed):
    scores = lax.dot_general(
        query_head, key_head, (((1,), (1,)), ((), ())), preferred_element_type=jnp.float32
    ) * HEAD_DIM ** (-0.5)
    return jnp.where(allowed, scores, blocked_score)


def heads_forward(queries, group_rows, first_head, head_count, allowed, carry):

    def one_head(offset, state):
        attended, log_totals = state
        head_index = first_head + offset
        query_head = lax.dynamic_slice_in_dim(queries, head_index * HEAD_DIM, HEAD_DIM, 1)
        key_head = lax.dynamic_slice_in_dim(group_rows, offset * 2 * HEAD_DIM, HEAD_DIM, 1)
        value_head = lax.dynamic_slice_in_dim(
            group_rows, offset * 2 * HEAD_DIM + HEAD_DIM, HEAD_DIM, 1
        )
        masked = score_rows(query_head, key_head, allowed)
        row_top = jnp.max(masked, axis=1, keepdims=True)
        weights = jnp.exp(masked - row_top)
        row_total = jnp.sum(weights, axis=1, keepdims=True)
        probabilities = (weights / row_total).astype(jnp.bfloat16)
        head_out = jnp.dot(probabilities, value_head, preferred_element_type=jnp.float32)
        attended = lax.dynamic_update_slice_in_dim(attended, head_out, head_index * HEAD_DIM, 1)
        log_totals = lax.dynamic_update_slice_in_dim(
            log_totals, (row_top + jnp.log(row_total)).T, head_index, 0
        )
        return (attended, log_totals)

    return lax.fori_loop(0, head_count, one_head, carry)


def heads_backward(
    queries, group_rows, first_head, head_count, allowed, log_totals, grad_out, grad_queries
):
    key_total = group_rows.shape[0]
    score_scale = HEAD_DIM ** (-0.5)

    def one_head(offset, state):
        grad_queries, grad_terms = state
        head_index = first_head + offset
        query_head = lax.dynamic_slice_in_dim(queries, head_index * HEAD_DIM, HEAD_DIM, 1)
        key_head = lax.dynamic_slice_in_dim(group_rows, offset * 2 * HEAD_DIM, HEAD_DIM, 1)
        value_head = lax.dynamic_slice_in_dim(
            group_rows, offset * 2 * HEAD_DIM + HEAD_DIM, HEAD_DIM, 1
        )
        grad_head = lax.dynamic_slice_in_dim(grad_out, head_index * HEAD_DIM, HEAD_DIM, 1)
        masked = score_rows(query_head, key_head, allowed)
        log_row = lax.dynamic_slice_in_dim(log_totals, head_index, 1, 0).T
        probabilities = jnp.exp(masked - log_row)
        rounded = probabilities.astype(jnp.bfloat16)
        grad_probs = lax.dot_general(
            grad_head, value_head, (((1,), (1,)), ((), ())), preferred_element_type=jnp.float32
        )
        inner = jnp.sum(probabilities * grad_probs, axis=1, keepdims=True)
        grad_scores = (probabilities * (grad_probs - inner)).astype(jnp.bfloat16)
        grad_query = (
            jnp.dot(grad_scores, key_head, preferred_element_type=jnp.float32) * score_scale
        )
        grad_key = contract_rows(grad_scores, query_head) * score_scale
        grad_value = contract_rows(rounded, grad_head)
        grad_queries = lax.dynamic_update_slice_in_dim(
            grad_queries, grad_query, head_index * HEAD_DIM, 1
        )
        grad_terms = lax.dynamic_update_slice_in_dim(
            grad_terms, jnp.concatenate([grad_key, grad_value], axis=1), offset * 2 * HEAD_DIM, 1
        )
        return (grad_queries, grad_terms)

    start_terms = jnp.zeros((key_total, head_count * 2 * HEAD_DIM), jnp.float32)
    return lax.fori_loop(0, head_count, one_head, (grad_queries, start_terms))


def shards(
    hidden_in,
    segment_ids,
    cotangent,
    norm1_gain,
    norm1_shift,
    w_qkv,
    q_bias,
    v_bias,
    w_out,
    out_bias,
    norm2_gain,
    norm2_shift,
    w_up,
    up_bias,
    w_down,
    down_bias,
):
    size_gx = lax.axis_size("gx")
    size_gy = lax.axis_size("gy")
    index_gx = lax.axis_index("gx")
    index_gy = lax.axis_index("gy")
    model_width = norm1_gain.shape[0]
    hidden_width = up_bias.shape[0]
    head_total = model_width // HEAD_DIM
    gain_one = local_part(norm1_gain, index_gx, size_gx)
    shift_one = local_part(norm1_shift, index_gx, size_gx)
    gain_two = local_part(norm2_gain, index_gx, size_gx)
    shift_two = local_part(norm2_shift, index_gx, size_gx)
    qkv_columns = w_qkv.shape[1]
    bias_full = jnp.concatenate(
        [
            q_bias.astype(jnp.float32),
            jnp.zeros((model_width,), jnp.float32),
            v_bias.astype(jnp.float32),
        ]
    )
    bias_qkv = lax.dynamic_slice_in_dim(bias_full, index_gy * qkv_columns, qkv_columns, 0)
    bias_out = local_part(out_bias, index_gx, size_gx)
    bias_up = local_part(up_bias, index_gy, size_gy)
    bias_down = local_part(down_bias, index_gx, size_gx)
    seq_length = segment_ids.shape[1]
    shard_rows = seq_length // (size_gx * size_gy)
    query_start = (index_gx * size_gy + index_gy) * shard_rows
    key_places = jnp.arange(seq_length, dtype=jnp.int32)
    query_places = query_start + jnp.arange(shard_rows, dtype=jnp.int32)
    groups = head_groups(head_total)
    total_qkv = jnp.zeros(w_qkv.shape, jnp.float32)
    total_out = jnp.zeros(w_out.shape, jnp.float32)
    total_up = jnp.zeros(w_up.shape, jnp.float32)
    total_down = jnp.zeros(w_down.shape, jnp.float32)
    sum_gain_one = jnp.zeros(gain_one.shape, jnp.float32)
    sum_shift_one = jnp.zeros(gain_one.shape, jnp.float32)
    sum_gain_two = jnp.zeros(gain_one.shape, jnp.float32)
    sum_shift_two = jnp.zeros(gain_one.shape, jnp.float32)
    sum_query_bias = jnp.zeros((model_width,), jnp.float32)
    sum_value_bias = jnp.zeros((model_width,), jnp.float32)
    sum_out_bias = jnp.zeros(bias_out.shape, jnp.float32)
    sum_up_bias = jnp.zeros(bias_up.shape, jnp.float32)
    sum_down_bias = jnp.zeros(bias_down.shape, jnp.float32)
    block_outs = []
    input_grads = []
    for micro_batch in range(hidden_in.shape[0]):
        residual_in = hidden_in[micro_batch].astype(jnp.float32)
        segments = segment_ids[micro_batch]
        query_segments = lax.dynamic_slice_in_dim(segments, query_start, shard_rows, 0)
        allowed = (query_segments[:, None] == segments[None, :]) & (
            key_places[None, :] <= query_places[:, None]
        )
        normed_one, centered_one, inverse_one = norm_forward(residual_in, gain_one, shift_one)
        normed_low = normed_one.astype(jnp.bfloat16)
        normed_whole = rows_over_gy(normed_low)
        projected = summed_over_gx(normed_whole, w_qkv, False) + bias_qkv
        token_rows = to_tokens(projected.astype(jnp.bfloat16))
        queries = token_rows[:, :model_width]
        paired = paired_heads(token_rows[:, model_width:], head_total)
        attended = jnp.zeros((shard_rows, model_width), jnp.float32)
        log_totals = jnp.zeros((head_total, shard_rows), jnp.float32)
        for first_head, head_count in groups:
            group_rows = gather_group(paired, first_head, head_count)
            attended, log_totals = heads_forward(
                queries, group_rows, first_head, head_count, allowed, (attended, log_totals)
            )
        attended_cols = to_columns(attended.astype(jnp.bfloat16))
        attended_whole = rows_over_gx(attended_cols)
        middle = residual_in + (summed_over_gy(attended_whole, w_out, False) + bias_out)
        normed_two, centered_two, inverse_two = norm_forward(middle, gain_two, shift_two)
        second_low = normed_two.astype(jnp.bfloat16)
        second_whole = rows_over_gy(second_low)
        hidden_pre = summed_over_gx(second_whole, w_up, False) + bias_up
        activated_low = jax.nn.gelu(hidden_pre, approximate=True).astype(jnp.bfloat16)
        activated_whole = rows_over_gx(activated_low)
        result = middle + (summed_over_gy(activated_whole, w_down, False) + bias_down)
        block_outs.append(result.astype(jnp.bfloat16))
        grad_low = cotangent[micro_batch]
        grad_result = grad_low.astype(jnp.float32)
        grad_whole = rows_over_gy(grad_low)
        down_input = rows_over_gx(activated_low)
        micro_down = contract_rows(down_input, grad_whole)
        grad_activated = summed_over_gx(grad_whole, w_down, True)
        gelu_pull = jax.vjp(partial(jax.nn.gelu, approximate=True), hidden_pre)[1]
        grad_pre_low = gelu_pull(grad_activated)[0].astype(jnp.bfloat16)
        grad_pre_whole = rows_over_gx(grad_pre_low)
        up_input = rows_over_gy(second_low)
        micro_up = contract_rows(up_input, grad_pre_whole)
        grad_second = summed_over_gy(grad_pre_whole, w_up, True)
        grad_from_norm, gain_two_term, shift_two_term = norm_backward(
            grad_second, centered_two, inverse_two, gain_two
        )
        grad_middle = grad_result + grad_from_norm
        grad_branch_low = grad_middle.astype(jnp.bfloat16)
        branch_whole = rows_over_gy(grad_branch_low)
        out_input = rows_over_gx(attended_cols)
        micro_out = contract_rows(out_input, branch_whole)
        grad_attended = summed_over_gx(branch_whole, w_out, True)
        grad_attended_tokens = to_tokens(grad_attended.astype(jnp.bfloat16))
        grad_queries = jnp.zeros((shard_rows, model_width), jnp.float32)
        key_pieces = []
        for first_head, head_count in groups:
            group_rows = gather_group(paired, first_head, head_count)
            grad_queries, grad_terms = heads_backward(
                queries,
                group_rows,
                first_head,
                head_count,
                allowed,
                log_totals,
                grad_attended_tokens,
                grad_queries,
            )
            key_pieces.append(
                lax.psum_scatter(
                    grad_terms.astype(jnp.bfloat16), ("gx", "gy"), scatter_dimension=0, tiled=True
                ).astype(jnp.float32)
            )
        grad_pairs = jnp.concatenate(key_pieces, axis=1).reshape(
            shard_rows, head_total, 2, HEAD_DIM
        )
        grad_keys = grad_pairs[:, :, 0, :].reshape(shard_rows, model_width)
        grad_values = grad_pairs[:, :, 1, :].reshape(shard_rows, model_width)
        grad_tokens_low = jnp.concatenate([grad_queries, grad_keys, grad_values], axis=1).astype(
            jnp.bfloat16
        )
        grad_cols = to_columns(grad_tokens_low)
        grad_cols_whole = rows_over_gx(grad_cols)
        qkv_input = rows_over_gy(normed_low)
        micro_qkv = contract_rows(qkv_input, grad_cols_whole)
        grad_first = summed_over_gy(grad_cols_whole, w_qkv, True)
        grad_from_first, gain_one_term, shift_one_term = norm_backward(
            grad_first, centered_one, inverse_one, gain_one
        )
        input_grads.append((grad_middle + grad_from_first).astype(jnp.bfloat16))
        sum_gain_one = sum_gain_one + gain_one_term
        sum_shift_one = sum_shift_one + shift_one_term
        sum_gain_two = sum_gain_two + gain_two_term
        sum_shift_two = sum_shift_two + shift_two_term
        sum_query_bias = sum_query_bias + jnp.sum(
            grad_tokens_low[:, :model_width].astype(jnp.float32), axis=0
        )
        sum_value_bias = sum_value_bias + jnp.sum(
            grad_tokens_low[:, 2 * model_width :].astype(jnp.float32), axis=0
        )
        sum_out_bias = sum_out_bias + jnp.sum(grad_branch_low.astype(jnp.float32), axis=0)
        sum_up_bias = sum_up_bias + jnp.sum(grad_pre_low.astype(jnp.float32), axis=0)
        sum_down_bias = sum_down_bias + jnp.sum(grad_result, axis=0)
        summed = (
            lax.psum(micro_qkv.astype(jnp.bfloat16), "dp").astype(jnp.float32),
            lax.psum(micro_out.astype(jnp.bfloat16), "dp").astype(jnp.float32),
            lax.psum(micro_up.astype(jnp.bfloat16), "dp").astype(jnp.float32),
            lax.psum(micro_down.astype(jnp.bfloat16), "dp").astype(jnp.float32),
        )
        total_qkv = total_qkv + summed[0]
        total_out = total_out + summed[1]
        total_up = total_up + summed[2]
        total_down = total_down + summed[3]
    smalls = lax.psum(
        (
            placed(sum_gain_one, index_gx, model_width),
            placed(sum_shift_one, index_gx, model_width),
            sum_query_bias,
            sum_value_bias,
            placed(sum_out_bias, index_gx, model_width),
            placed(sum_gain_two, index_gx, model_width),
            placed(sum_shift_two, index_gx, model_width),
            placed(sum_up_bias, index_gy, hidden_width),
            placed(sum_down_bias, index_gx, model_width),
        ),
        ("dp", "gx", "gy"),
    )
    return (
        jnp.stack(block_outs),
        jnp.stack(input_grads),
        smalls[0],
        smalls[1],
        total_qkv,
        smalls[2],
        smalls[3],
        total_out,
        smalls[4],
        smalls[5],
        smalls[6],
        total_up,
        smalls[7],
        total_down,
        smalls[8],
    )


def solution(mesh):
    return jax.shard_map(
        shards,
        mesh=mesh,
        in_specs=(
            P(None, ("dp", "gy"), "gx"),
            P(None, "dp"),
            P(None, ("dp", "gy"), "gx"),
            P(),
            P(),
            P("gx", "gy"),
            P(),
            P(),
            P("gy", "gx"),
            P(),
            P(),
            P(),
            P("gx", "gy"),
            P(),
            P("gy", "gx"),
            P(),
        ),
        out_specs=(
            P(None, ("dp", "gy"), "gx"),
            P(None, ("dp", "gy"), "gx"),
            P(),
            P(),
            P("gx", "gy"),
            P(),
            P(),
            P("gy", "gx"),
            P(),
            P(),
            P(),
            P("gx", "gy"),
            P(),
            P("gy", "gx"),
            P(),
        ),
        check_vma=False,
    )
```

profile of v0, /device:TPU:0, one launch (start us, length us, event | category | flops | bytes accessed | tf_op | source)
XLA Modules:
  0.0 2146.1 jit_solution(2652059781082269257)
XLA Ops:
  10.2 11.3 all-reduce.4
  22.8 16.2 all_gather.88
  41.8 16.1 all_gather.96
  61.6 24.1 %reduce-scatter.41.cloned.1.call-done = f32[256,816]{0,1:T(8,128)} async-done(((f32[1024,816]{0,1:T(8,128)}), f32[256,816]{0,1:T(8,128)}) %reduce-scatter.41.cloned.1.call-update) | async-done | bytes 835600 | tf_op jit(solution)/shard_map/reduce_scatter | solution.py:52
  85.8 48.6 %reduce-scatter.49.cloned.1.call-done = f32[256,816]{0,1:T(8,128)} async-done(((f32[1024,816]{0,1:T(8,128)}), f32[256,816]{0,1:T(8,128)}) %reduce-scatter.49.cloned.1.call-update) | async-done | bytes 835600 | tf_op jit(solution)/shard_map/reduce_scatter | solution.py:52
  136.2 17.5 all_to_all.146
  158.4 16.3 all_to_all.147
  179.4 44.0 %all_gather.92 = bf16[1024,256]{1,0:T(8,128)(2,1)S(1)} all-gather(bf16[64,256]{1,0:T(8,128)(2,1)S(1)} %slice-done), channel_id=1, replica_groups=mesh['dp'=2,'gx'=4,'gy'=4] {'gx','gy'}, dimensions={0}, use_global_device_ids=true | all-gather | bytes 557056 | tf_op jit(solution)/shard_map/all_gather | solution.py:129
  223.4 42.9 %all_gather.100 = bf16[1024,256]{1,0:T(8,128)(2,1)S(1)} all-gather(bf16[64,256]{1,0:T(8,128)(2,1)S(1)} %slice.139), channel_id=1, replica_groups=mesh['dp'=2,'gx'=4,'gy'=4] {'gx','gy'}, dimensions={0}, use_global_device_ids=true | all-gather | bytes 557056 | tf_op jit(solution)/shard_map/all_gather | solution.py:129
  266.5 15.9 while.288
  282.4 16.1 while.289
  298.5 34.8 %all-gather.19.cloned.1.call-done = bf16[1024,640]{1,0:T(8,128)(2,1)} async-done(((bf16[64,640]{1,0:T(8,128)(2,1)}), bf16[1024,640]{1,0:T(8,128)(2,1)}) %all-gather.19.cloned.1.call-update) | async-done | bytes 1310736 | tf_op jit(solution)/shard_map/all_gather | solution.py:129
  333.3 15.9 while.290
  356.4 35.4 %all-gather.23.cloned.1.call-done = bf16[1024,640]{1,0:T(8,128)(2,1)} async-done(((bf16[64,640]{1,0:T(8,128)(2,1)}), bf16[1024,640]{1,0:T(8,128)(2,1)}) %all-gather.23.cloned.1.call-update) | async-done | bytes 1310736 | tf_op jit(solution)/shard_map/all_gather | solution.py:129
  392.4 22.0 %while.292 = (s32[]{:T(128)}, bf16[64,1088]{1,0:T(8,128)(2,1)S(1)}, f32[17,64]{1,0:T(8,128)}, bf16[64,1088]{1,0:T(8,128)(2,1)S(1)}, bf16[1024,640]{1,0:T(8,128)(...) while((s32[]{:T(128)}, bf16[64,1088]{1,0:T(8,128)(2,1)S(1)}, ...), condition=%wide.region_36.37_spmd.clone, body=%wide.region_33.36_spmd.clone.sunk | while | flops 17498060 | bytes 1359667 | solution.py:161
  414.4 36.4 %all-gather.25.cloned.1.call-done = bf16[1024,640]{1,0:T(8,128)(2,1)} async-done(((bf16[64,640]{1,0:T(8,128)(2,1)}), bf16[1024,640]{1,0:T(8,128)(2,1)}) %all-gather.25.cloned.1.call-update) | async-done | bytes 1310736 | tf_op jit(solution)/shard_map/all_gather | solution.py:129
  450.8 22.3 %while.293 = (s32[]{:T(128)}, bf16[64,1088]{1,0:T(8,128)(2,1)S(1)}, f32[17,64]{1,0:T(8,128)}, bf16[64,1088]{1,0:T(8,128)(2,1)S(1)}, bf16[1024,640]{1,0:T(8,128)(...) while((s32[]{:T(128)}, bf16[64,1088]{1,0:T(8,128)(2,1)S(1)}, ...), condition=%wide.region_40.41_spmd.clone, body=%wide.region_37.0_spmd.clone.sunk | while | flops 17498064 | bytes 1359729 | solution.py:161
  473.8 13.6 all_gather.93
  489.0 21.4 all-gather.27.cloned.1.call-done
  510.4 22.1 %while.294 = (s32[]{:T(128)}, bf16[64,1088]{1,0:T(8,128)(2,1)S(1)}, f32[17,64]{1,0:T(8,128)}, bf16[64,1088]{1,0:T(8,128)(2,1)S(1)}, bf16[1024,640]{1,0:T(8,128)(...) while((s32[]{:T(128)}, bf16[64,1088]{1,0:T(8,128)(2,1)S(1)}, ...), condition=%wide.region_44.45_spmd.clone, body=%wide.region_41.0_spmd.clone.sunk | while | flops 17498064 | bytes 1359729 | solution.py:161
  539.0 10.1 all_to_all.148
  549.1 11.1 all_gather.101
  562.7 19.1 all-gather
  586.6 18.8 all-gather.1
  622.7 15.6 all_gather.94
  641.9 15.0 all_gather.102
  661.6 51.7 %reduce-scatter.65.cloned.1.call-done = f32[256,1088]{0,1:T(8,128)} async-done(((f32[1024,1088]{0,1:T(8,128)}), f32[256,1088]{0,1:T(8,128)}) %reduce-scatter.65.cloned.1.call-update) | async-done | bytes 1114128 | tf_op jit(solution)/shard_map/reduce_scatter | solution.py:52
  713.3 57.9 %reduce-scatter.45.cloned.1.call-done = f32[256,1088]{0,1:T(8,128)} async-done(((f32[1024,1088]{0,1:T(8,128)}), f32[256,1088]{0,1:T(8,128)}) %reduce-scatter.45.cloned.1.call-update) | async-done | bytes 1114128 | tf_op jit(solution)/shard_map/reduce_scatter | solution.py:52
  771.2 57.8 %reduce-scatter.53.cloned.1.call-done = f32[256,1088]{0,1:T(8,128)} async-done(((f32[1024,1088]{0,1:T(8,128)}), f32[256,1088]{0,1:T(8,128)}) %reduce-scatter.53.cloned.1.call-update) | async-done | bytes 1114128 | tf_op jit(solution)/shard_map/reduce_scatter | solution.py:52
  836.5 34.6 %all-gather.31.cloned.1.call-done = bf16[1024,1088]{0,1:T(8,128)(2,1)} async-done(((bf16[256,1088]{0,1:T(8,128)(2,1)}), bf16[1024,1088]{0,1:T(8,128)(2,1)}) %all-gather.31.cloned.1.call-update) | async-done | bytes 2228240 | tf_op jit(solution)/shard_map/all_gather | solution.py:21
  874.7 35.0 %all-gather.35.cloned.1.call-done = bf16[1024,1088]{0,1:T(8,128)(2,1)} async-done(((bf16[256,1088]{0,1:T(8,128)(2,1)}), bf16[1024,1088]{0,1:T(8,128)(2,1)}) %all-gather.35.cloned.1.call-update) | async-done | bytes 2228240 | tf_op jit(solution)/shard_map/all_gather | solution.py:21
  913.2 34.4 %all-gather.29.cloned.1.call-done = bf16[1024,1088]{0,1:T(8,128)(2,1)} async-done(((bf16[256,1088]{0,1:T(8,128)(2,1)}), bf16[1024,1088]{0,1:T(8,128)(2,1)}) %all-gather.29.cloned.1.call-update) | async-done | bytes 2228240 | tf_op jit(solution)/shard_map/all_gather | solution.py:21
  951.4 34.2 %all-gather.21.cloned.1.call-done = bf16[1024,1088]{0,1:T(8,128)(2,1)} async-done(((bf16[256,1088]{0,1:T(8,128)(2,1)}), bf16[1024,1088]{0,1:T(8,128)(2,1)}) %all-gather.21.cloned.1.call-update) | async-done | bytes 2228240 | tf_op jit(solution)/shard_map/all_gather | solution.py:21
  989.9 26.7 %reduce-scatter.59.cloned.1.call-done = f32[256,272]{0,1:T(8,128)} async-done(((f32[1024,272]{0,1:T(8,128)}), f32[256,272]{0,1:T(8,128)}) %reduce-scatter.59.cloned.1.call-update) | async-done | bytes 278544 | tf_op jit(solution)/shard_map/reduce_scatter | solution.py:66
  1016.7 29.7 %reduce-scatter.67.cloned.1.call-done = f32[256,272]{0,1:T(8,128)} async-done(((f32[1024,272]{0,1:T(8,128)}), f32[256,272]{0,1:T(8,128)}) %reduce-scatter.67.cloned.1.call-update) | async-done | bytes 278544 | tf_op jit(solution)/shard_map/reduce_scatter | solution.py:66
  1048.4 9.9 all-reduce.2
  1058.4 17.2 reduce-scatter.55.cloned.1.call-done
  1075.6 29.3 %reduce-scatter.47.cloned.1.call-done = f32[256,272]{0,1:T(8,128)} async-done(((f32[1024,272]{0,1:T(8,128)}), f32[256,272]{0,1:T(8,128)}) %reduce-scatter.47.cloned.1.call-update) | async-done | bytes 278544 | tf_op jit(solution)/shard_map/reduce_scatter | solution.py:66
  1107.5 16.4 all_gather.110
  1125.5 15.4 all_gather.106
  1142.4 9.6 reduce-scatter.69.cloned.1.call-done
  1158.5 25.2 %reduce-scatter.61.cloned.1.call-done = f32[256,272]{0,1:T(8,128)} async-done(((f32[1024,272]{0,1:T(8,128)}), f32[256,272]{0,1:T(8,128)}) %reduce-scatter.61.cloned.1.call-update) | async-done | bytes 278544 | tf_op jit(solution)/shard_map/reduce_scatter | solution.py:52
  1193.2 37.4 %while.300 = (s32[]{:T(128)}, bf16[64,1088]{1,0:T(8,128)(2,1)}, bf16[1024,640]{0,1:T(8,128)(2,1)}, bf16[64,1088]{1,0:T(8,128)(2,1)}, bf16[1024,640]{1,0:T(8,128)...) while((s32[]{:T(128)}, bf16[64,1088]{1,0:T(8,128)(2,1)}, ...), condition=%wide.region_93.94_spmd.clone, body=%wide.region_91.0_spmd.clone.sunk | while | flops 43392972 | bytes 3636055 | solution.py:202
  1232.5 37.7 %while.301 = (s32[]{:T(128)}, bf16[64,1088]{1,0:T(8,128)(2,1)}, bf16[1024,640]{0,1:T(8,128)(2,1)}, bf16[64,1088]{1,0:T(8,128)(2,1)}, bf16[1024,640]{1,0:T(8,128)...) while((s32[]{:T(128)}, bf16[64,1088]{1,0:T(8,128)(2,1)}, ...), condition=%wide.region_96.97_spmd.clone, body=%wide.region_94.0_spmd.clone.sunk | while | flops 43392976 | bytes 3636117 | solution.py:202
  1271.9 37.4 %while.302 = (s32[]{:T(128)}, bf16[64,1088]{1,0:T(8,128)(2,1)}, bf16[1024,640]{0,1:T(8,128)(2,1)}, bf16[64,1088]{1,0:T(8,128)(2,1)}, bf16[1024,640]{1,0:T(8,128)...) while((s32[]{:T(128)}, bf16[64,1088]{1,0:T(8,128)(2,1)}, ...), condition=%wide.region_99.100_spmd.clone, body=%wide.region_97.0_spmd.clone.sunk | while | flops 43392976 | bytes 3636117 | solution.py:202
  1309.4 13.4 while.303
  1327.1 23.0 %while.296 = (s32[]{:T(128)}, bf16[64,1088]{1,0:T(8,128)(2,1)}, bf16[1024,640]{0,1:T(8,128)(2,1)}, bf16[64,1088]{1,0:T(8,128)(2,1)S(1)}, bf16[1024,640]{1,0:T(8,...) while((s32[]{:T(128)}, bf16[64,1088]{1,0:T(8,128)(2,1)}, ...), condition=%wide.region_65.66_spmd.clone, body=%wide.region_63.0_spmd.clone.sunk | while | flops 43392972 | bytes 3636055 | solution.py:202
  1354.3 23.3 %while.297 = (s32[]{:T(128)}, bf16[64,1088]{1,0:T(8,128)(2,1)}, bf16[1024,640]{0,1:T(8,128)(2,1)}, bf16[64,1088]{1,0:T(8,128)(2,1)S(1)}, bf16[1024,640]{1,0:T(8,...) while((s32[]{:T(128)}, bf16[64,1088]{1,0:T(8,128)(2,1)}, ...), condition=%wide.region_68.69_spmd.clone, body=%wide.region_66.0_spmd.clone.sunk | while | flops 43392976 | bytes 3636117 | solution.py:202
  1381.6 23.0 %while.298 = (s32[]{:T(128)}, bf16[64,1088]{1,0:T(8,128)(2,1)}, bf16[1024,640]{0,1:T(8,128)(2,1)}, bf16[64,1088]{1,0:T(8,128)(2,1)S(1)}, bf16[1024,640]{1,0:T(8,...) while((s32[]{:T(128)}, bf16[64,1088]{1,0:T(8,128)(2,1)}, ...), condition=%wide.region_71.72_spmd.clone, body=%wide.region_69.0_spmd.clone.sunk | while | flops 43392976 | bytes 3636117 | solution.py:202
  1425.3 54.8 %reduce-scatter.85.cloned.1.call-done = bf16[64,640]{1,0:T(8,128)(2,1)} async-done(((bf16[1024,640]{1,0:T(8,128)(2,1)}), bf16[64,640]{1,0:T(8,128)(2,1)}) %reduce-scatter.85.cloned.1.call-update) | async-done | bytes 81936
  1481.1 77.7 %reduce-scatter.83.cloned.1.call-done = bf16[64,640]{1,0:T(8,128)(2,1)} async-done(((bf16[1024,640]{1,0:T(8,128)(2,1)}), bf16[64,640]{1,0:T(8,128)(2,1)}) %reduce-scatter.83.cloned.1.call-update) | async-done | bytes 81936
  1559.8 77.8 %reduce-scatter.81.cloned.1.call-done = bf16[64,640]{1,0:T(8,128)(2,1)} async-done(((bf16[1024,640]{1,0:T(8,128)(2,1)}), bf16[64,640]{1,0:T(8,128)(2,1)}) %reduce-scatter.81.cloned.1.call-update) | async-done | bytes 81936
  1639.4 13.8 all_to_all.149
  1654.3 59.6 %reduce-scatter.79.cloned.1.call-done = bf16[64,256]{1,0:T(8,128)(2,1)} async-done(((bf16[1024,256]{1,0:T(8,128)(2,1)}), bf16[64,256]{1,0:T(8,128)(2,1)}) %reduce-scatter.79.cloned.1.call-update) | async-done | bytes 32784
  1714.8 78.1 %reduce-scatter.77.cloned.1.call-done = bf16[64,640]{1,0:T(8,128)(2,1)} async-done(((bf16[1024,640]{1,0:T(8,128)(2,1)}), bf16[64,640]{1,0:T(8,128)(2,1)}) %reduce-scatter.77.cloned.1.call-update) | async-done | bytes 81936
  1794.0 78.0 %reduce-scatter.75.cloned.1.call-done = bf16[64,640]{1,0:T(8,128)(2,1)} async-done(((bf16[1024,640]{1,0:T(8,128)(2,1)}), bf16[64,640]{1,0:T(8,128)(2,1)}) %reduce-scatter.75.cloned.1.call-update) | async-done | bytes 81936
  1873.1 77.7 %reduce-scatter.73.cloned.1.call-done = bf16[64,640]{1,0:T(8,128)(2,1)} async-done(((bf16[1024,640]{1,0:T(8,128)(2,1)}), bf16[64,640]{1,0:T(8,128)(2,1)}) %reduce-scatter.73.cloned.1.call-update) | async-done | bytes 81936
  1952.5 12.7 all_to_all.150
  1965.3 16.9 all-gather.37.cloned.1.call-done
  1985.7 31.5 %all-gather.33.cloned.1.call-done = bf16[1024,816]{1,0:T(8,128)(2,1)} async-done(((bf16[256,816]{1,0:T(8,128)(2,1)}), bf16[1024,816]{1,0:T(8,128)(2,1)}) %all-gather.33.cloned.1.call-update) | async-done | bytes 1671184 | tf_op jit(solution)/shard_map/all_gather | solution.py:21
  2038.4 9.9 reduce-scatter.71.cloned.1.call-done
  2048.3 29.7 %reduce-scatter.63.cloned.1.call-done = f32[256,272]{0,1:T(8,128)} async-done(((f32[1024,272]{0,1:T(8,128)}), f32[256,272]{0,1:T(8,128)}) %reduce-scatter.63.cloned.1.call-update) | async-done | bytes 278544 | tf_op jit(solution)/shard_map/reduce_scatter | solution.py:66
  2079.5 9.9 all-reduce.1
  2089.6 40.8 %all-reduce = (f32[1088]{0:T(1024)}, f32[1088]{0:T(1024)}, f32[1088]{0:T(1024)}, f32[1088]{0:T(1024)}, f32[1088]{0:T(1024)}, /*index=5*/f32[1088]{0:T(1024)}, f32[1088]{0:T(1024)}, f32[4352]{0:T(1024)}, f32[1088]{0:T(1024)}) all-reduce(f32[1088]{0:T(1024)S(1)} %add_dynamic-update-slice_fusio, ...), channel_id=1, replica_groups=mesh['dp'=2,'gx'=4,'gy'=4] {'dp','gx','gy'}, use_global_device_ids=true, to_apply=%region_114.115 | all-reduce | flops 13056 | bytes 104448 | tf_op jit(solution)/shard_map/psum | solution.py:380
  (977 shorter events, 520.4 us)
Async XLA Ops:
  7.2 631.1 %copy-start = (bf16[272,1088]{1,0:T(8,128)(2,1)S(1)}, bf16[272,1088]{1,0:T(8,128)(2,1)}, u32[]{:S(2)}) copy-start(bf16[272,1088]{1,0:T(8,128)(2,1)} %param.60) | copy-start | bytes 1775620
  7.2 78.6 %reduce-scatter.41.cloned.1.call-start = ((), (), s32[]{:S(2)}) async-start(), calls=%async_computation.32 | async-start | bytes 4177920 | tf_op jit(solution)/shard_map/reduce_scatter | solution.py:52
  41.8 92.7 %reduce-scatter.49.cloned.1.call-start = ((), (), s32[]{:S(2)}) async-start(), calls=%async_computation.40 | async-start | bytes 4177920 | tf_op jit(solution)/shard_map/reduce_scatter | solution.py:52
  60.8 205.6 %all-gather.15.cloned.1.call-start = ((), (), s32[]{:S(2)}) async-start(), calls=%async_computation.33 | async-start | bytes 1392640 | tf_op jit(solution)/shard_map/all_gather | solution.py:129
  156.9 125.5 %all-gather.17.cloned.1.call-start = ((), (), s32[]{:S(2)}) async-start(), calls=%async_computation.34 | async-start | bytes 1392640 | tf_op jit(solution)/shard_map/all_gather | solution.py:129
  157.5 175.8 %all-gather.19.cloned.1.call-start = ((), (), s32[]{:S(2)}) async-start(), calls=%async_computation.35 | async-start | bytes 1392640 | tf_op jit(solution)/shard_map/all_gather | solution.py:129
  158.1 233.7 %all-gather.23.cloned.1.call-start = ((), (), s32[]{:S(2)}) async-start(), calls=%async_computation.41 | async-start | bytes 1392640 | tf_op jit(solution)/shard_map/all_gather | solution.py:129
  177.8 273.0 %all-gather.25.cloned.1.call-start = ((), (), s32[]{:S(2)}) async-start(), calls=%async_computation.42 | async-start | bytes 1392640 | tf_op jit(solution)/shard_map/all_gather | solution.py:129
  178.6 331.8 %all-gather.27.cloned.1.call-start = ((), (), s32[]{:S(2)}) async-start(), calls=%async_computation.43 | async-start | bytes 1392640 | tf_op jit(solution)/shard_map/all_gather | solution.py:129
  352.7 120.4 %all-to-all-start.1 = ((bf16[64,4,272]{2,0,1:T(8,128)(2,1)}), bf16[64,4,272]{2,0,1:T(8,128)(2,1)S(1)}, u32[]{:S(2)}, u32[]{:S(2)}) async-start(bf16[64,4,272]{2,0,1:T(8,128)(2,1)} %copy.102), calls=%async_computation.2 | async-start | bytes 393216 | tf_op jit(solution)/shard_map/all_to_all | solution.py:29
  356.2 255.7 %reduce-scatter.43.cloned.1.call-start = ((), (), s32[]{:S(2)}) async-start(), calls=%async_computation.36 | async-start | bytes 1392640 | tf_op jit(solution)/shard_map/reduce_scatter | solution.py:66
  489.0 122.9 %reduce-scatter.51.cloned.1.call-start = ((), (), s32[]{:S(2)}) async-start(), calls=%async_computation.44 | async-start | bytes 1392640 | tf_op jit(solution)/shard_map/reduce_scatter | solution.py:66
  562.6 99.0 %reduce-scatter.57.cloned.1.call-start = ((), (), s32[]{:S(2)}) async-start(), calls=%async_computation.48 | async-start | bytes 5570560 | tf_op jit(solution)/shard_map/reduce_scatter | solution.py:52
  586.6 126.8 %reduce-scatter.65.cloned.1.call-start = ((), (), s32[]{:S(2)}) async-start(), calls=%async_computation.54 | async-start | bytes 5570560 | tf_op jit(solution)/shard_map/reduce_scatter | solution.py:52
  610.2 161.0 %reduce-scatter.45.cloned.1.call-start = ((), (), s32[]{:S(2)}) async-start(), calls=%async_computation.37 | async-start | bytes 5570560 | tf_op jit(solution)/shard_map/reduce_scatter | solution.py:52
  611.8 493.0 %copy-start.65 = (f32[272]{0:T(512)}, f32[272]{0:T(512)S(1)}, u32[]{:S(2)}) copy-start(f32[272]{0:T(512)S(1)} %get-tuple-element.3865) | copy-start | bytes 3268
  613.1 491.7 %copy-start.11 = (f32[256,272]{0,1:T(8,128)}, f32[256,272]{0,1:T(8,128)S(1)}, u32[]{:S(2)}) copy-start(f32[256,272]{0,1:T(8,128)S(1)} %get-tuple-element.3780) | copy-start | bytes 835588
  613.1 491.7 %copy-start.13 = (f32[256,272]{0,1:T(8,128)}, f32[256,272]{0,1:T(8,128)S(1)}, u32[]{:S(2)}) copy-start(f32[256,272]{0,1:T(8,128)S(1)} %get-tuple-element.3832) | copy-start | bytes 835588
  621.8 483.0 %copy-start.71 = (f32[256]{0:T(256)}, f32[256]{0:T(256)S(1)}, u32[]{:S(2)}) copy-start(f32[256]{0:T(256)S(1)} %get-tuple-element.3856) | copy-start | bytes 3076
  621.8 483.0 %copy-start.73 = (f32[256]{0:T(256)}, f32[256]{0:T(256)S(1)}, u32[]{:S(2)}) copy-start(f32[256]{0:T(256)S(1)} %get-tuple-element.3857) | copy-start | bytes 3076
  621.8 483.0 %copy-start.75 = (f32[256]{0:T(256)}, f32[256]{0:T(256)S(1)}, u32[]{:S(2)}) copy-start(f32[256]{0:T(256)S(1)} %get-tuple-element.3858) | copy-start | bytes 3076
  621.9 483.0 %copy-start.77 = (f32[256]{0:T(256)}, f32[256]{0:T(256)S(1)}, u32[]{:S(2)}) copy-start(f32[256]{0:T(256)S(1)} %get-tuple-element.3859) | copy-start | bytes 3076
  641.9 187.1 %reduce-scatter.53.cloned.1.call-start = ((), (), s32[]{:S(2)}) async-start(), calls=%async_computation.45 | async-start | bytes 5570560 | tf_op jit(solution)/shard_map/reduce_scatter | solution.py:52
  660.4 210.7 %all-gather.31.cloned.1.call-start = ((), (), s32[]{:S(2)}) async-start(), calls=%async_computation.49 | async-start | bytes 2785280 | tf_op jit(solution)/shard_map/all_gather | solution.py:21
  834.7 74.9 %all-gather.35.cloned.1.call-start = ((), (), s32[]{:S(2)}) async-start(), calls=%async_computation.55 | async-start | bytes 2785280 | tf_op jit(solution)/shard_map/all_gather | solution.py:21
  835.3 112.3 %all-gather.29.cloned.1.call-start = ((), (), s32[]{:S(2)}) async-start(), calls=%async_computation.46 | async-start | bytes 2785280 | tf_op jit(solution)/shard_map/all_gather | solution.py:21
  835.9 149.7 %all-gather.21.cloned.1.call-start = ((), (), s32[]{:S(2)}) async-start(), calls=%async_computation.38 | async-start | bytes 2785280 | tf_op jit(solution)/shard_map/all_gather | solution.py:21
  836.5 180.2 %reduce-scatter.59.cloned.1.call-start = ((), (), s32[]{:S(2)}) async-start(), calls=%async_computation.50 | async-start | bytes 1392640 | tf_op jit(solution)/shard_map/reduce_scatter | solution.py:66
  874.6 171.7 %reduce-scatter.67.cloned.1.call-start = ((), (), s32[]{:S(2)}) async-start(), calls=%async_computation.56 | async-start | bytes 1392640 | tf_op jit(solution)/shard_map/reduce_scatter | solution.py:66
  913.2 72.4 %copy-start.40 = (bf16[1088,272]{0,1:T(8,128)(2,1)S(1)}, bf16[1088,272]{0,1:T(8,128)(2,1)}, u32[]{:S(2)}) copy-start(bf16[1088,272]{0,1:T(8,128)(2,1)} %param.62) | copy-start | bytes 1775620
  913.2 162.4 %reduce-scatter.55.cloned.1.call-start = ((), (), s32[]{:S(2)}) async-start(), calls=%async_computation.47 | async-start | bytes 1392640 | tf_op jit(solution)/shard_map/reduce_scatter | solution.py:66
  951.3 153.5 %reduce-scatter.47.cloned.1.call-start = ((), (), s32[]{:S(2)}) async-start(), calls=%async_computation.39 | async-start | bytes 1392640 | tf_op jit(solution)/shard_map/reduce_scatter | solution.py:66
  989.1 162.9 %reduce-scatter.69.cloned.1.call-start = ((), (), s32[]{:S(2)}) async-start(), calls=%async_computation.57 | async-start | bytes 1392640 | tf_op jit(solution)/shard_map/reduce_scatter | solution.py:52
  1016.7 88.2 %copy-start.36 = (f32[256,272]{0,1:T(8,128)S(1)}, f32[256,272]{0,1:T(8,128)}, u32[]{:S(2)}) copy-start(f32[256,272]{0,1:T(8,128)} %reduce-scatter.59.cloned.1.call-done) | copy-start | bytes 835588
  1058.3 65.6 %copy-start.88 = (f32[256]{0:T(256)}, f32[256]{0:T(256)S(1)}, u32[]{:S(2)}) copy-start(f32[256]{0:T(256)S(1)} %broadcast_multiply_fusion.6) | copy-start | bytes 3076
  1125.5 58.2 %reduce-scatter.61.cloned.1.call-start = ((), (), s32[]{:S(2)}) async-start(), calls=%async_computation.51 | async-start | bytes 1392640 | tf_op jit(solution)/shard_map/reduce_scatter | solution.py:52
  1153.9 31.6 %all-to-all-start.6 = ((bf16[4,64,272]{2,1,0:T(8,128)(2,1)}), bf16[4,64,272]{2,1,0:T(8,128)(2,1)S(1)}, u32[]{:S(2)}, u32[]{:S(2)}) async-start(bf16[4,64,272]{2,1,0:T(8,128)(2,1)} %bitcast.34), calls=%async_computation.21 | async-start | bytes 393216 | tf_op jit(solution)/shard_map/all_to_all | solution.py:25
  1185.4 138.4 %all-to-all-start.4 = ((bf16[4,64,272]{2,1,0:T(8,128)(2,1)}), bf16[4,64,272]{2,1,0:T(8,128)(2,1)}, u32[]{:S(2)}, u32[]{:S(2)}) async-start(bf16[4,64,272]{2,1,0:T(8,128)(2,1)} %bitcast.22), calls=%async_computation.15 | async-start | bytes 393216 | tf_op jit(solution)/shard_map/all_to_all | solution.py:25
  1190.2 234.2 %reduce-scatter.87.cloned.1.call-start = ((), (), s32[]{:S(2)}) async-start(), calls=%async_computation.67 | async-start | bytes 557056
  1323.8 156.2 %reduce-scatter.85.cloned.1.call-start = ((), (), s32[]{:S(2)}) async-start(), calls=%async_computation.66 | async-start | bytes 1392640
  1352.6 206.1 %reduce-scatter.83.cloned.1.call-start = ((), (), s32[]{:S(2)}) async-start(), calls=%async_computation.65 | async-start | bytes 1392640
  1380.0 257.7 %reduce-scatter.81.cloned.1.call-start = ((), (), s32[]{:S(2)}) async-start(), calls=%async_computation.64 | async-start | bytes 1392640
  1407.1 306.9 %reduce-scatter.79.cloned.1.call-start = ((), (), s32[]{:S(2)}) async-start(), calls=%async_computation.63 | async-start | bytes 557056
  1415.8 377.2 %reduce-scatter.77.cloned.1.call-start = ((), (), s32[]{:S(2)}) async-start(), calls=%async_computation.62 | async-start | bytes 1392640
  1417.7 454.3 %reduce-scatter.75.cloned.1.call-start = ((), (), s32[]{:S(2)}) async-start(), calls=%async_computation.61 | async-start | bytes 1392640
  1420.5 530.3 %reduce-scatter.73.cloned.1.call-start = ((), (), s32[]{:S(2)}) async-start(), calls=%async_computation.60 | async-start | bytes 1392640
  1423.3 558.9 %all-gather.37.cloned.1.call-start = ((), (), s32[]{:S(2)}) async-start(), calls=%async_computation.58 | async-start | bytes 2293760 | tf_op jit(solution)/shard_map/all_gather | solution.py:21
  1653.2 364.0 %all-gather.33.cloned.1.call-start = ((), (), s32[]{:S(2)}) async-start(), calls=%async_computation.52 | async-start | bytes 2293760 | tf_op jit(solution)/shard_map/all_gather | solution.py:21
  1965.3 83.0 %reduce-scatter.71.cloned.1.call-start = ((), (), s32[]{:S(2)}) async-start(), calls=%async_computation.59 | async-start | bytes 1392640 | tf_op jit(solution)/shard_map/reduce_scatter | solution.py:66
  1985.5 92.5 %reduce-scatter.63.cloned.1.call-start = ((), (), s32[]{:S(2)}) async-start(), calls=%async_computation.53 | async-start | bytes 1392640 | tf_op jit(solution)/shard_map/reduce_scatter | solution.py:66
  2020.5 112.2 %all-reduce.8.cloned.1.call-start = ((), (), s32[]{:S(2)}) async-start(), calls=%async_computation.68 | async-start | bytes 7798784 | tf_op jit(solution)/shard_map/psum | solution.py:371
  2036.6 93.8 %copy-start.14 = (f32[256,272]{0,1:T(8,128)S(1)}, f32[256,272]{0,1:T(8,128)}, u32[]{:S(2)}) copy-start(f32[256,272]{0,1:T(8,128)} %copy-done.13) | copy-start | bytes 835588
  2036.6 93.8 %copy-start.39 = (f32[256,272]{0,1:T(8,128)S(1)}, f32[256,272]{0,1:T(8,128)}, u32[]{:S(2)}) copy-start(f32[256,272]{0,1:T(8,128)} %reduce-scatter.67.cloned.1.call-done) | copy-start | bytes 835588
  2036.6 93.9 %copy-start.66 = (f32[272]{0:T(512)S(1)}, f32[272]{0:T(512)}, u32[]{:S(2)}) copy-start(f32[272]{0:T(512)} %copy-done.65) | copy-start | bytes 3268
  2036.6 93.9 %copy-start.76 = (f32[256]{0:T(256)S(1)}, f32[256]{0:T(256)}, u32[]{:S(2)}) copy-start(f32[256]{0:T(256)} %copy-done.75) | copy-start | bytes 3076
  2036.6 93.9 %copy-start.78 = (f32[256]{0:T(256)S(1)}, f32[256]{0:T(256)}, u32[]{:S(2)}) copy-start(f32[256]{0:T(256)} %copy-done.77) | copy-start | bytes 3076
  2036.7 93.9 %copy-start.93 = (f32[256]{0:T(256)S(1)}, f32[256]{0:T(256)}, u32[]{:S(2)}) copy-start(f32[256]{0:T(256)} %copy-done.92) | copy-start | bytes 3076
  2036.7 93.9 %copy-start.95 = (f32[256]{0:T(256)S(1)}, f32[256]{0:T(256)}, u32[]{:S(2)}) copy-start(f32[256]{0:T(256)} %copy-done.94) | copy-start | bytes 3076
  2038.0 93.7 %copy-start.12 = (f32[256,272]{0,1:T(8,128)S(1)}, f32[256,272]{0,1:T(8,128)}, u32[]{:S(2)}) copy-start(f32[256,272]{0,1:T(8,128)} %copy-done.11) | copy-start | bytes 835588
  2038.0 93.7 %copy-start.37 = (f32[256,272]{0,1:T(8,128)S(1)}, f32[256,272]{0,1:T(8,128)}, u32[]{:S(2)}) copy-start(f32[256,272]{0,1:T(8,128)} %reduce-scatter.59.cloned.1.call-done) | copy-start | bytes 835588
  2038.0 93.7 %copy-start.72 = (f32[256]{0:T(256)S(1)}, f32[256]{0:T(256)}, u32[]{:S(2)}) copy-start(f32[256]{0:T(256)} %copy-done.71) | copy-start | bytes 3076
  2038.1 93.7 %copy-start.74 = (f32[256]{0:T(256)S(1)}, f32[256]{0:T(256)}, u32[]{:S(2)}) copy-start(f32[256]{0:T(256)} %copy-done.73) | copy-start | bytes 3076
  2038.1 93.7 %copy-start.89 = (f32[256]{0:T(256)S(1)}, f32[256]{0:T(256)}, u32[]{:S(2)}) copy-start(f32[256]{0:T(256)} %copy-done.88) | copy-start | bytes 3076
  2038.1 93.7 %copy-start.91 = (f32[256]{0:T(256)S(1)}, f32[256]{0:T(256)}, u32[]{:S(2)}) copy-start(f32[256]{0:T(256)} %copy-done.90) | copy-start | bytes 3076
  (85 other events, 922.5 us)
Sparse Core Ops, SparseCore 0:
  41.9 43.8 reduce-scatter.40
  88.8 45.5 reduce-scatter.48
  157.0 57.3 all-gather.14
  217.6 56.7 all-gather.16
  277.5 55.7 all-gather.18
  335.9 55.8 all-gather.22
  395.0 55.7 all-gather.24
  454.1 56.2 all-gather.26
  513.3 27.0 reduce-scatter.42
  562.7 34.7 reduce-scatter.50
  600.5 54.9 reduce-scatter.56
  658.4 54.8 reduce-scatter.64
  716.4 54.8 reduce-scatter.44
  774.1 54.8 reduce-scatter.52
  834.8 36.2 all-gather.30
  873.4 36.2 all-gather.34
  911.3 36.2 all-gather.28
  949.3 36.2 all-gather.20
  988.5 28.1 reduce-scatter.58
  1019.5 26.8 reduce-scatter.66
  1048.7 26.8 reduce-scatter.54
  1078.0 26.8 reduce-scatter.46
  1125.6 26.4 reduce-scatter.68
  1155.4 28.1 reduce-scatter.60
  1323.9 77.5 reduce-scatter.86
  1403.8 76.2 reduce-scatter.84
  1482.3 76.4 reduce-scatter.82
  1561.1 76.4 reduce-scatter.80
  1640.5 73.3 reduce-scatter.78
  1716.1 76.8 reduce-scatter.76
  1795.3 76.7 reduce-scatter.74
  1874.3 76.4 reduce-scatter.72
  1952.5 29.6 all-gather.36
  1984.0 33.1 all-gather.32
  2020.1 28.1 reduce-scatter.70
  2051.1 26.8 reduce-scatter.62
  2081.3 23.8 all-reduce.7
where the time goes:
time: 2170 us; the launch traced here: 2150 us
  waiting for transfers between devices  1240 us (57%)
  blocking collectives  395 us (18%)
  matrix products  247 us (11%)
  local copies, waits for them, and re-layouts  160 us (7%)
  other arithmetic  68.4 us (3%)
    unnamed x45, waiting for transfers between devices  508 us
    reduce_scatter x8, waiting for transfers between devices, summed_over_gx(): lax.psum_scatter(partial_term(jnp.int32(0), lax.axis_size('gx') * own_row...  275 us
    all_gather x6, waiting for transfers between devices, rows_over_gx(): return lax.all_gather(local_rows, 'gx', axis=0, tiled=True)  186 us
    reduce_scatter x8, waiting for transfers between devices, summed_over_gy(): lax.psum_scatter(partial_term(jnp.int32(0), lax.axis_size('gy') * own_row...  142 us
    all_gather x8, blocking collectives, rows_over_gy(): return lax.all_gather(local_rows, 'gy', axis=0, tiled=True)  133 us
    all_gather x6, waiting for transfers between devices, gather_group(): return lax.all_gather(chosen, ('gx', 'gy'), axis=0, tiled=True)  128 us
    all_gather x2, blocking collectives, gather_group(): return lax.all_gather(chosen, ('gx', 'gy'), axis=0, tiled=True)  87 us
    dot_general x68, matrix products, score_rows(): lax.dot_general(query_head, key_head, (((1,), (1,)), ((), ())), preferred...  69.7 us
  transfers between devices with their start and end apart: 40, of which 30 were waited for; matrix products, arithmetic and copies ran while one was open for 20% of the time, Pallas kernels for 0%

commit v1 on v0

v1 whole, which is shorter than its diff:
```python
import math

import jax
import jax.numpy as jnp
from jax import lax
from jax.sharding import Mesh
from jax.sharding import PartitionSpec as P

HEAD_DIM = 64
PAIR = 2 * HEAD_DIM
EPSILON = 1e-05
BLOCKED = -1e30
BF = jnp.bfloat16
F32 = jnp.float32
PLANE = ("c", "gx")
ROOT = math.sqrt(2.0 / math.pi)


def dot(left, right, dims):
    return lax.dot_general(left, right, (dims, ((), ())), preferred_element_type=F32)


def swap_core(value):
    return lax.ppermute(value, "c", [(0, 1), (1, 0)])


def from_peer(value, step):
    return lax.ppermute(value, "gx", [(i, i ^ step) for i in range(4)])


def reordered(blocks, mask):
    return jnp.stack(
        [lax.dynamic_index_in_dim(blocks, i ^ mask, 0, False) for i in range(blocks.shape[0])]
    )


def exchange_gx(blocks, g):
    sent = [lax.dynamic_index_in_dim(blocks, g ^ k, 0, False) for k in range(4)]
    got = jnp.stack([sent[0]] + [from_peer(sent[k], k) for k in range(1, 4)])
    return reordered(got, g)


def gather_plane(own):
    near = jnp.stack([own] + [from_peer(own, k) for k in range(1, 4)])
    return jnp.concatenate([near, swap_core(near)], 0)


def scatter_plane(partial):
    other = swap_core(partial[4:].astype(BF))
    summed = partial[:4].astype(F32) + other.astype(F32)
    total = summed[0]
    for k in range(1, 4):
        total = total + from_peer(summed[k].astype(BF), k).astype(F32)
    return total


def plane_of(core, z, second):
    half = z % 2 if not second else 1 - z % 2
    return (z // 2) * 4 + 2 * half + core


FORWARD = [[(c * 4 + z, plane_of(c, z, second)) for c in range(2) for z in range(4)] for second in (False, True)]
BACKWARD = [[(b, a) for a, b in perm] for perm in FORWARD]


def to_plane(local, z):
    first = lax.ppermute(lax.dynamic_index_in_dim(local, z % 2, 0, False), ("c", "gy"), FORWARD[0])
    second = lax.ppermute(lax.dynamic_index_in_dim(local, 1 - z % 2, 0, False), ("c", "gy"), FORWARD[1])
    low = z // 2 == 0
    return jnp.concatenate([jnp.where(low, first, second), jnp.where(low, second, first)], 0)


def from_plane(half, z):
    rows = half.shape[0] // 2
    parts = half.reshape(2, rows, half.shape[1])
    first = lax.ppermute(lax.dynamic_index_in_dim(parts, z // 2, 0, False), ("c", "gy"), BACKWARD[0])
    second = lax.ppermute(lax.dynamic_index_in_dim(parts, 1 - z // 2, 0, False), ("c", "gy"), BACKWARD[1])
    even = z % 2 == 0
    return jnp.stack([jnp.where(even, first, second), jnp.where(even, second, first)])


def whole_width(half, g):
    near = jnp.stack([half] + [from_peer(half, k) for k in range(1, 4)])
    ordered = reordered(near, g)
    return jnp.concatenate([ordered[i] for i in range(4)], 1)


def norm_parts(rows):
    average = jnp.mean(rows, axis=1, keepdims=True)
    centered = rows - average
    inverse = lax.rsqrt(jnp.mean(centered * centered, axis=1, keepdims=True) + EPSILON)
    return centered * inverse, inverse


def norm_pull(upstream, centered, inverse, gain):
    scaled = upstream * gain
    return inverse * (
        scaled
        - jnp.mean(scaled, axis=1, keepdims=True)
        - centered * jnp.mean(scaled * centered, axis=1, keepdims=True)
    )


def head_forward(query, key, value, allowed):
    scores = dot(query, key, ((1,), (1,))) * HEAD_DIM**-0.5
    masked = jnp.where(allowed, scores, BLOCKED)
    top = jnp.max(masked, axis=1, keepdims=True)
    weights = jnp.exp(masked - top)
    probs = weights / jnp.sum(weights, axis=1, keepdims=True)
    return probs, dot(probs.astype(BF), value, ((1,), (0,))).astype(BF)


def head_backward(query, key, value, probs, grad_out):
    grad_probs = dot(grad_out, value, ((1,), (1,)))
    inner = jnp.sum(probs * grad_probs, axis=1, keepdims=True)
    grad_scores = (probs * (grad_probs - inner)).astype(BF)
    grad_query = dot(grad_scores, key, ((1,), (0,))) * HEAD_DIM**-0.5
    grad_key = dot(grad_scores, query, ((0,), (0,))) * HEAD_DIM**-0.5
    grad_value = dot(probs.astype(BF), grad_out, ((0,), (0,)))
    return grad_query, grad_key, grad_value


def shards(
    hidden_in,
    segment_ids,
    cotangent,
    norm1_gain,
    norm1_shift,
    w_qkv,
    q_bias,
    v_bias,
    w_out,
    out_bias,
    norm2_gain,
    norm2_shift,
    w_up,
    up_bias,
    w_down,
    down_bias,
):
    c = lax.axis_index("c")
    g = lax.axis_index("gx")
    z = lax.axis_index("gy")
    d = c * 4 + g
    width = norm1_gain.shape[0]
    hidden = up_bias.shape[0]
    block = w_qkv.shape[0] // 2
    part = hidden // 32
    qkv_cols = w_qkv.shape[1]
    seq = segment_ids.shape[1]
    rows = seq // 8
    shared_at = 8 * PAIR
    gain1, shift1 = norm1_gain.astype(F32), norm1_shift.astype(F32)
    gain2, shift2 = norm2_gain.astype(F32), norm2_shift.astype(F32)

    x_half = whole_width(to_plane(hidden_in, z), g)
    x_own = lax.dynamic_slice_in_dim(x_half, g * rows, rows, 0).astype(F32)
    normed1_half = (norm_parts(x_half.astype(F32))[0] * gain1 + shift1).astype(BF)
    normed1_other = swap_core(normed1_half)
    low = c == 0
    normed1 = jnp.concatenate(
        [jnp.where(low, normed1_half, normed1_other), jnp.where(low, normed1_other, normed1_half)], 0
    )
    g_half = whole_width(to_plane(cotangent, z), g)
    g_half = reordered(g_half.reshape(4, rows, width), g)
    g_own = g_half[0].astype(F32)
    g_rel = jnp.concatenate([g_half, swap_core(g_half)], 0).reshape(seq, width)

    swapped_ids = swap_core(segment_ids)
    ids = jnp.where(z % 2 == c, segment_ids, swapped_ids)
    segments = lax.dynamic_index_in_dim(ids, z // 2, 0, False)

    qkv_half = lax.dynamic_slice_in_dim(w_qkv, c * block, block, 0)
    qkv_all = lax.all_gather(qkv_half, "gy", axis=1, tiled=True)
    pieces = []
    for t in range(3):
        third = qkv_all[:, t * width : (t + 1) * width]
        pieces.append(third[:, :shared_at].reshape(block, 8, PAIR).transpose(1, 0, 2))
    for t in range(3):
        shared = qkv_all[:, t * width + shared_at : (t + 1) * width]
        pieces.append(jnp.broadcast_to(shared[None], (8, block, HEAD_DIM)))
    qkv_own = lax.all_to_all(jnp.concatenate(pieces, 2), PLANE, split_axis=0, concat_axis=0, tiled=True)
    own_cols = qkv_own.shape[2]
    qkv_own = qkv_own.reshape(2, 4, block, own_cols).transpose(1, 0, 2, 3).reshape(width, own_cols)

    out_half = lax.dynamic_slice_in_dim(w_out, c * block, block, 1)
    out_all = lax.all_gather(out_half, "gy", axis=0, tiled=True)
    out_pieces = jnp.concatenate(
        [
            out_all[:shared_at].reshape(8, PAIR, block),
            jnp.broadcast_to(out_all[None, shared_at:], (8, HEAD_DIM, block)),
        ],
        1,
    )
    out_own = lax.all_to_all(out_pieces, PLANE, split_axis=0, concat_axis=0, tiled=True)
    out_own = out_own.reshape(2, 4, PAIR + HEAD_DIM, block).transpose(2, 1, 0, 3).reshape(-1, width)

    up_half = lax.dynamic_slice_in_dim(w_up, c * 4 * part, 4 * part, 1)
    up_half = up_half.reshape(2 * block, 4, part).transpose(1, 2, 0)
    down_half = lax.dynamic_slice_in_dim(w_down, c * 4 * part, 4 * part, 0).reshape(4, part, 2 * block)
    mlp = exchange_gx(jnp.concatenate([up_half, down_half], 1), g)
    mlp = lax.all_gather(mlp, "gy", axis=0, tiled=False)
    mlp = mlp.reshape(4, 4, 2, part, 2 * block).transpose(2, 0, 3, 1, 4).reshape(2, 4 * part, width)
    up_own, down_own = mlp[0], mlp[1]
    up_bias_own = lax.dynamic_index_in_dim(up_bias.reshape(4, 8, part), d, 1, False).reshape(1, -1).astype(F32)

    bias_pair = jnp.concatenate(
        [
            lax.dynamic_slice_in_dim(q_bias, d * PAIR, PAIR, 0),
            jnp.zeros((PAIR,), BF),
            lax.dynamic_slice_in_dim(v_bias, d * PAIR, PAIR, 0),
            q_bias[shared_at:],
            jnp.zeros((HEAD_DIM,), BF),
            v_bias[shared_at:],
        ]
    ).astype(F32)
    projected = (dot(normed1, qkv_own, ((1,), (0,))) + bias_pair).astype(BF)
    places = jnp.arange(seq, dtype=jnp.int32)
    allowed = (segments[:, None] == segments[None, :]) & (places[None, :] <= places[:, None])
    first_row = d * rows
    allowed_own = lax.dynamic_slice_in_dim(allowed, first_row, rows, 0)
    heads = []
    for h in range(2):
        heads.append([projected[:, t * PAIR + h * HEAD_DIM :][:, :HEAD_DIM] for t in range(3)])
    shared = [projected[:, 3 * PAIR + t * HEAD_DIM :][:, :HEAD_DIM] for t in range(3)]
    shared[0] = lax.dynamic_slice_in_dim(shared[0], first_row, rows, 0)
    kept = [head_forward(*heads[h], allowed) for h in range(2)]
    kept_shared = head_forward(*shared, allowed_own)
    attended = jnp.concatenate([kept[0][1], kept[1][1]], 1)
    attended_rel = reordered(attended.reshape(8, rows, PAIR), d).reshape(seq, PAIR)
    branch = dot(attended_rel, out_own[:PAIR], ((1,), (0,))).reshape(8, rows, width)
    branch_shared = dot(kept_shared[1], out_own[PAIR:], ((1,), (0,)))
    middle = x_own + scatter_plane(branch) + branch_shared + out_bias.astype(F32)

    centered2, inverse2 = norm_parts(middle)
    normed2_own = (centered2 * gain2 + shift2).astype(BF)
    normed2 = gather_plane(normed2_own).reshape(seq, width)
    pre = dot(normed2, up_own, ((1,), (1,))) + up_bias_own
    inner = jnp.tanh(ROOT * (pre + 0.044715 * pre * pre * pre))
    activated = (0.5 * pre * (1.0 + inner)).astype(BF)
    slope = 0.5 * (1.0 + inner) + 0.5 * pre * (1.0 - inner * inner) * ROOT * (1.0 + 3.0 * 0.044715 * pre * pre)
    grad_pre = (dot(g_rel, down_own, ((1,), (1,))) * slope).astype(BF)
    grad_normed2 = scatter_plane(dot(grad_pre, up_own, ((1,), (0,))).reshape(8, rows, width))
    feed = dot(activated, down_own, ((1,), (0,))).reshape(8, rows, width)
    result = middle + scatter_plane(feed) + down_bias.astype(F32)
    grad_down = dot(activated, g_rel, ((0,), (0,)))
    grad_up = dot(grad_pre, normed2, ((0,), (0,)))
    grad_up_bias = jnp.sum(grad_pre.astype(F32), axis=0)

    grad_middle = g_own + norm_pull(grad_normed2, centered2, inverse2, gain2)
    grad_branch_own = grad_middle.astype(BF)
    grad_branch = gather_plane(grad_branch_own).reshape(seq, width)

    grad_attended_rel = dot(grad_branch, out_own[:PAIR], ((1,), (1,))).astype(BF)
    grad_attended = reordered(grad_attended_rel.reshape(8, rows, PAIR), d).reshape(seq, PAIR)
    grad_shared = dot(grad_branch_own, out_own[PAIR:], ((1,), (1,))).astype(BF)
    grad_out = jnp.concatenate(
        [dot(attended_rel, grad_branch, ((0,), (0,))), dot(kept_shared[1], grad_branch_own, ((0,), (0,)))], 0
    )
    backs = [
        head_backward(*heads[h], kept[h][0], grad_attended[:, h * HEAD_DIM : (h + 1) * HEAD_DIM]) for h in range(2)
    ]
    back_shared = head_backward(*shared, kept_shared[0], grad_shared)
    grad_pairs = jnp.concatenate([backs[h][t] for t in range(3) for h in range(2)], 1).astype(BF)
    grad_query_shared = back_shared[0].astype(BF)
    grad_kv_shared = jnp.concatenate([back_shared[1], back_shared[2]], 1).astype(BF)
    grad_pairs_kv = jnp.concatenate([grad_pairs, grad_kv_shared], 1)
    pairs_rel = reordered(grad_pairs_kv.reshape(8, rows, -1), d).reshape(seq, -1)
    cols_kv = jnp.concatenate([qkv_own[:, : 3 * PAIR], qkv_own[:, 3 * PAIR + HEAD_DIM :]], 1)
    grad_first = dot(pairs_rel, cols_kv, ((1,), (1,))).reshape(8, rows, width)
    grad_first_own = dot(grad_query_shared, qkv_own[:, 3 * PAIR :][:, :HEAD_DIM], ((1,), (1,)))
    grad_normed1 = scatter_plane(grad_first) + grad_first_own
    centered1, inverse1 = norm_parts(x_own)
    grad_in = grad_middle + norm_pull(grad_normed1, centered1, inverse1, gain1)
    normed1_own = lax.dynamic_slice_in_dim(normed1, first_row, rows, 0)
    grad_qkv_kv = dot(normed1, grad_pairs_kv, ((0,), (0,)))
    grad_qkv_q = dot(normed1_own, grad_query_shared, ((0,), (0,)))
    grad_qkv = jnp.concatenate([grad_qkv_kv[:, : 3 * PAIR], grad_qkv_q, grad_qkv_kv[:, 3 * PAIR :]], 1)

    outer = lax.axis_size("do") > 1

    def over_outer(value):
        return lax.psum(value, "do") if outer else value

    sent = jnp.concatenate([grad_up.reshape(4, part, width), grad_down.reshape(4, part, width)], 1).astype(BF)
    summed = over_outer(lax.psum_scatter(sent, "gy", scatter_dimension=0, tiled=False))
    lanes = summed.reshape(2 * part, 4, 2 * block).transpose(1, 0, 2)
    mine = exchange_gx(lanes, g)
    theirs = swap_core(mine)
    both = jnp.where(low, jnp.stack([mine, theirs]), jnp.stack([theirs, mine])).reshape(8, 2, part, 2 * block)
    total_up = both[:, 0].reshape(8 * part, 2 * block).T.astype(F32)
    total_down = both[:, 1].reshape(8 * part, 2 * block).astype(F32)

    sent = grad_out.astype(BF).reshape(-1, 4, 2, block).transpose(2, 1, 0, 3).reshape(8, -1, block)
    got = lax.all_to_all(sent, PLANE, split_axis=0, concat_axis=0, tiled=True)
    shared_rows = jnp.sum(got[:, PAIR:].astype(F32), axis=0).astype(BF)
    placed = jnp.concatenate([got[:, :PAIR].reshape(shared_at, block), shared_rows], 0)
    mine = over_outer(lax.psum_scatter(placed, "gy", scatter_dimension=0, tiled=True))
    theirs = swap_core(mine)
    total_out = jnp.concatenate([jnp.where(low, mine, theirs), jnp.where(low, theirs, mine)], 1).astype(F32)

    sent = grad_qkv.astype(BF).reshape(4, 2, block, own_cols).transpose(1, 0, 2, 3).reshape(8, block, own_cols)
    got = lax.all_to_all(sent, PLANE, split_axis=0, concat_axis=0, tiled=True)
    shared_cols = jnp.sum(got[:, :, 3 * PAIR :].astype(F32), axis=0).astype(BF)
    wide = []
    for t in range(3):
        wide.append(got[:, :, t * PAIR : (t + 1) * PAIR].transpose(1, 0, 2).reshape(block, shared_at))
        wide.append(shared_cols[:, t * HEAD_DIM : (t + 1) * HEAD_DIM])
    placed = jnp.concatenate(wide, 1).reshape(block, 4, qkv_cols).transpose(1, 0, 2)
    mine = over_outer(lax.psum_scatter(placed, "gy", scatter_dimension=0, tiled=False))
    theirs = swap_core(mine)
    total_qkv = jnp.concatenate([jnp.where(low, mine, theirs), jnp.where(low, theirs, mine)], 0).astype(F32)

    def spread(pair_sums, shared_sums):
        return lax.dynamic_update_slice_in_dim(
            jnp.concatenate([jnp.zeros((shared_at,), F32), shared_sums]), pair_sums, d * PAIR, 0
        )

    sums = jnp.sum(grad_pairs_kv.astype(F32), axis=0)
    up_sums = lax.dynamic_update_slice_in_dim(
        jnp.zeros((4, 8, part), F32), grad_up_bias.reshape(4, 1, part), d, 1
    ).reshape(hidden)
    smalls = lax.psum(
        (
            jnp.sum(grad_normed1 * centered1, axis=0),
            jnp.sum(grad_normed1, axis=0),
            spread(sums[:PAIR], jnp.sum(grad_query_shared.astype(F32), axis=0)),
            spread(sums[2 * PAIR : 3 * PAIR], sums[3 * PAIR + HEAD_DIM :]),
            jnp.sum(grad_branch_own.astype(F32), axis=0),
            jnp.sum(grad_normed2 * centered2, axis=0),
            jnp.sum(grad_normed2, axis=0),
            up_sums,
            jnp.sum(g_own, axis=0),
        ),
        ("do", "c", "gx", "gy"),
    )

    def to_output(own):
        blocks = own.astype(BF).reshape(rows, 4, 2 * block).transpose(1, 0, 2)
        return from_plane(exchange_gx(blocks, g).reshape(4 * rows, 2 * block), z)

    return (
        to_output(result),
        to_output(grad_in),
        smalls[0],
        smalls[1],
        total_qkv,
        smalls[2],
        smalls[3],
        total_out,
        smalls[4],
        smalls[5],
        smalls[6],
        total_up,
        smalls[7],
        total_down,
        smalls[8],
    )


def solution(mesh):
    devices = mesh.devices
    split = Mesh(
        devices.reshape(devices.shape[0] // 2, 2, devices.shape[1], devices.shape[2]), ("do", "c", "gx", "gy")
    )
    stream = P(None, ("do", "c", "gy"), "gx")
    flat = P()
    tall = P("gx", "gy")
    wide = P("gy", "gx")
    return jax.shard_map(
        shards,
        mesh=split,
        in_specs=(
            stream,
            P(None, ("do", "c")),
            stream,
            flat,
            flat,
            tall,
            flat,
            flat,
            wide,
            flat,
            flat,
            flat,
            tall,
            flat,
            wide,
            flat,
        ),
        out_specs=(
            stream,
            stream,
            flat,
            flat,
            tall,
            flat,
            flat,
            wide,
            flat,
            flat,
            flat,
            tall,
            flat,
            wide,
            flat,
        ),
        check_vma=False,
    )
```

time: 2170 us -> 572 us (0.26)
  waiting for transfers between devices: 1240 us -> 95.9 us
  blocking collectives: 395 us -> 75.7 us
  matrix products: 247 us -> 58.1 us
  starting transfers between devices: 15.3 us -> 76.4 us
    unnamed x45 -> x6, waiting for transfers between devices: 508 us -> 0.11 us
    reduce_scatter x16 -> x1, waiting for transfers between devices: 417 us -> 0.02 us  [shards(): lax.psum_scatter(sent, 'gy', scatter_dimension=0, tiled=False)]
    all_gather x12 -> x1, waiting for transfers between devices: 315 us -> 0.01 us  [shards(): mlp = lax.all_gather(mlp, 'gy', axis=0, tiled=False)]
    all_gather x12 -> x2, blocking collectives: 244 us -> 36.1 us  [the longest x1 20.8 us: shards(): qkv_all = lax.all_gather(qkv_half, 'gy', axis=1, tiled=True)]
    dot_general x262 -> x35, matrix products: 247 us -> 58.1 us  [dot(): lax.dot_general(left, right, (dims, ((), ())), preferred_element_type=F32)]
    ppermute x0 -> x56, waiting for transfers between devices: none -> 89.7 us  [the longest x36 76.1 us: from_peer(): return lax.ppermute(value, 'gx', [(i, i ^ step) for i in range(4)])]
    dynamic_update_slice x102 -> x2, local copies, waits for them, and re-layouts: 81.9 us -> 0.14 us  [the longest x1 0.09 us: spread(): lax.dynamic_update_slice_in_dim(jnp.concatenate([jnp.zeros((shared_at,),...]
    all_to_all x5 -> x0, blocking collectives: 70.3 us -> none  [the longest x3 36.6 us: to_columns(): lax.all_to_all(token_block, 'gy', split_axis=1, concat_axis=0, tiled=True)]
  transfers between devices with their start and end apart: 40 -> 64, of which waited for: 30 -> 23; matrix products, arithmetic and copies ran while one was open for 20% -> 46% of each run, Pallas kernels for 0% -> 0%
where the time goes in v1:
time: 572 us; the launch traced here: 562 us
  local copies, waits for them, and re-layouts  175 us (31%)
  waiting for transfers between devices  95.9 us (17%)
  starting transfers between devices  76.4 us (13%)
  blocking collectives  75.7 us (13%)
  other arithmetic  64.3 us (11%)
  matrix products  58.1 us (10%)
  between operations  16.5 us (3%)
    ppermute x36, waiting for transfers between devices, from_peer(): return lax.ppermute(value, 'gx', [(i, i ^ step) for i in range(4)])  76.1 us
    dot_general x35, matrix products, dot(): lax.dot_general(left, right, (dims, ((), ())), preferred_element_type=F32)  58.1 us
    ppermute x36, starting transfers between devices, from_peer(): return lax.ppermute(value, 'gx', [(i, i ^ step) for i in range(4)])  42.2 us
    psum x1, blocking collectives, shards(): lax.psum((jnp.sum(grad_normed1 * centered1, axis=0), jnp.sum(grad_normed1...  39.7 us
    unnamed x284, local copies, waits for them, and re-layouts  35.2 us
    slice x9, local copies, waits for them, and re-layouts, scatter_plane(): summed = partial[:4].astype(F32) + other.astype(F32)  23.5 us
    all_gather x1, blocking collectives, shards(): qkv_all = lax.all_gather(qkv_half, 'gy', axis=1, tiled=True)  20.8 us
    all_gather x1, blocking collectives, shards(): out_all = lax.all_gather(out_half, 'gy', axis=0, tiled=True)  15.3 us
  transfers between devices with their start and end apart: 64, of which 23 were waited for; matrix products, arithmetic and copies ran while one was open for 46% of the time, Pallas kernels for 0%

profile of v1, /device:TPU:0, one launch (start us, length us, event | category | flops | bytes accessed | tf_op | source)
XLA Modules:
  0.0 561.7 jit_solution(9679077862024750630)
XLA Ops:
  9.0 2.8 collective-permute-start
  11.8 3.2 collective-permute-start.1
  16.7 2.8 collective-permute-start.27
  19.5 2.8 collective-permute-start.28
  23.5 15.3 %all-gather.2 = bf16[4,272,136]{1,2,0:T(8,128)(2,1)S(1)} all-gather(bf16[1,272,136]{1,2,0:T(8,128)(2,1)S(1)} %bitcast.514), channel_id=1, replica_groups=mesh['dp'=2,'gx'=4,'gy'=4] {'gy'}, dimensions={0}, use_global_device_ids=true | all-gather | bytes 369920 | tf_op jit(solution)/shard_map/all_gather | solution.py:187
  40.4 3.7 all-to-all-start.1
  44.2 20.8 %all-gather.1 = bf16[4,816,136]{1,2,0:T(8,128)(2,1)S(1)} all-gather(bf16[1,816,136]{1,2,0:T(8,128)(2,1)S(1)} %dynamic-slice_bitcast_fusion.4), channel_id=1, replica_groups=mesh['dp'=2,'gx'=4,'gy'=4] {'gy'}, dimensions={0}, use_global_device_ids=true | all-gather | bytes 1109760 | tf_op jit(solution)/shard_map/all_gather | solution.py:174
  77.5 3.1 concatenate.135
  92.6 5.7 %collective-permute-done.16 = bf16[272,272]{1,0:T(8,128)(2,1)S(1)} collective-permute-done((bf16[272,272]{1,0:T(8,128)(2,1)}, bf16[272,272]{1,0:T(8,128)(2,1)S(1)}, u32[]{:S(2)}, u32[]{:S(2)}) %collective-permute-start.16) | collective-permute-done | bytes 148000 | tf_op jit(solution)/shard_map/ppermute | solution.py:28
  100.6 4.5 all-to-all-start
  105.8 2.9 collective-permute-start.4
  112.3 3.0 collective-permute-done.3
  115.3 16.5 %collective-permute-done.4 = bf16[512,272]{0,1:T(8,128)(2,1)} collective-permute-done((bf16[512,272]{0,1:T(8,128)(2,1)}, bf16[512,272]{0,1:T(8,128)(2,1)}, u32[]{:S(2)}, u32[]{:S(2)}) %collective-permute-start.4) | collective-permute-done | bytes 278560 | tf_op jit(solution)/shard_map/ppermute | solution.py:28
  140.1 2.4 broadcast_select_fusion.1
  173.6 5.3 collective-permute-done.10
  178.9 4.7 collective-permute-done.8
  190.9 2.1 slice.383
  194.9 2.4 constant_dynamic-update-slice_fusion.13
  197.3 6.9 %copy.324 = bf16[8,128,1088]{1,0,2:T(8,128)(2,1)} copy(bf16[8,128,1088]{1,2,0:T(8,128)(2,1)} %constant_dynamic-update-slice_fusion.13) | data formatting | bytes 4456448 | tf_op jit(solution)/shard_map/concatenate | solution.py:167
  204.2 4.7 reshape.393
  212.3 3.5 fusion.162
  217.5 3.9 squeeze.175
  221.4 3.3 copy.314
  224.7 4.1 squeeze.176
  228.8 2.3 constant_dynamic-update-slice_fusion.8
  231.1 3.7 fusion.32
  234.8 6.4 %convert_reduce_fusion.1 = (f32[544]{0:T(1024)S(1)}, bf16[1024,544]{0,1:T(8,128)(2,1)S(1)}, f32[1024,544]{0,1:T(8,128)}) fusion(f32[1024,544]{0,1:T(8,128)S(1)} %fusion.32, f32[544]{0:T(1024)S(1)} %reshape.382, bf16[544,1088]{1,0:T(8,128)(2,1)S(1)} %copy-done.27, bf16[8,128,1088]{1,2,0:T(8,128)(2,1)} %constant_dynamic-update-slice_fusion.13), kind=kOutput, calls=%fused_computation.68 | convolution fusion | flops 1224408576 | bytes 8986880 | tf_op jit(solution)/shard_map/dot_general | solution.py:20
  250.7 7.0 %copy.310 = bf16[8,128,1088]{1,0,2:T(8,128)(2,1)} copy(bf16[8,128,1088]{1,2,0:T(8,128)(2,1)} %constant_dynamic-update-slice_fusion.8) | data formatting | bytes 4456448 | tf_op jit(solution)/shard_map/concatenate | solution.py:45
  257.8 4.4 fusion.43
  266.5 4.7 reshape.392
  271.2 3.4 copy.315
  274.6 3.1 copy.318
  280.8 3.0 copy.325
  283.9 3.0 copy.328
  287.8 5.6 %fusion.25 = (bf16[544,1024]{1,0:T(8,128)(2,1)}, bf16[544,1024]{1,0:T(8,128)(2,1)}) fusion(f32[1024,544]{0,1:T(8,128)} %get-tuple-element.251, f32[1024,544]{0,1:T(8,128)} %copy-done.21, f32[544]{0:T(1024)S(1)} %copy-done.75), kind=kLoop, calls=%fused_computation.51 | loop fusion | flops 12255232 | bytes 6686848 | tf_op jit(solution)/shard_map/convert_element_type | solution.py:242
  301.1 3.5 collective-permute-done.34
  306.0 5.9 %collective-permute-done.35 = bf16[128,1088]{0,1:T(8,128)(2,1)S(1)} collective-permute-done((bf16[128,1088]{0,1:T(8,128)(2,1)S(1)}, bf16[128,1088]{0,1:T(8,128)(2,1)S(1)}, u32[]{:S(2)}, u32[]{:S(2)}) %collective-permute-start.35) | collective-permute-done | bytes 278560 | tf_op jit(solution)/shard_map/ppermute | solution.py:28
  313.2 3.5 collective-permute-done.19
  316.7 6.5 %collective-permute-done.20 = bf16[128,1088]{0,1:T(8,128)(2,1)S(1)} collective-permute-done((bf16[128,1088]{0,1:T(8,128)(2,1)S(1)}, bf16[128,1088]{0,1:T(8,128)(2,1)S(1)}, u32[]{:S(2)}, u32[]{:S(2)}) %collective-permute-start.20) | collective-permute-done | bytes 278560 | tf_op jit(solution)/shard_map/ppermute | solution.py:28
  334.5 4.8 collective-permute-done.38
  345.8 3.5 all-to-all-start.3
  349.4 4.7 convolution_convert_fusion.1
  354.0 4.8 all-to-all-done.3
  360.2 3.7 convolution_convert_fusion
  382.8 2.1 collective-permute-start.26
  387.0 11.9 %collective-permute-done.26 = bf16[256,272]{0,1:T(8,128)(2,1)S(1)} collective-permute-done((bf16[256,272]{0,1:T(8,128)(2,1)S(1)}, bf16[256,272]{0,1:T(8,128)(2,1)S(1)}, u32[]{:S(2)}, u32[]{:S(2)}) %collective-permute-start.26) | collective-permute-done | bytes 139296 | tf_op jit(solution)/shard_map/ppermute | solution.py:77
  401.8 2.2 multiply_reduce_fusion
  414.8 3.1 constant_dynamic-slice_fusion.15
  417.8 6.5 %stack.248 = bf16[8,128,512]{1,0,2:T(8,128)(2,1)} concatenate(bf16[1,128,512]{1,0,2:T(2,128)(2,1)} %get-tuple-element.174, bf16[1,128,512]{1,0,2:T(2,128)(2,1)} %get-tuple-element.173, bf16[1,128,512]{1,0,2:T(2,128)(2,1)} %get-tuple-element.172, bf16[1,128,512]{1,0,2:T(2,128)(2,1)} %get-tuple-element.171, bf16[1,128,512]{1,0,2:T(2,128)(2,1)} %get-tuple-element.170, ...), dimensions={0} | concatenate | bytes 2097152 | tf_op jit(solution)/shard_map/stack | solution.py:32
  424.3 2.9 fusion.45
  427.2 2.1 copy-done.17
  430.5 2.4 copy.333
  432.9 2.4 copy.334
  436.0 3.7 convolution_convert_fusion.2
  442.9 4.3 all-to-all-start.2
  448.8 3.0 copy.332
  451.8 3.0 copy.335
  456.6 3.6 fusion.155
  468.2 3.6 collective-permute-done.42
  471.8 4.9 collective-permute-done.43
  487.8 2.3 reshape_reduce_scatter.3
  500.0 2.8 collective-permute-done.53
  505.4 39.7 %all-reduce.3 = (f32[1088]{0:T(1024)}, f32[1088]{0:T(1024)}, f32[1088]{0:T(1024)}, f32[1088]{0:T(1024)}, f32[1088]{0:T(1024)}, /*index=5*/f32[1088]{0:T(1024)}, f32[1088]{0:T(1024)}, f32[4352]{0:T(1024)}, f32[1088]{0:T(1024)}) all-reduce(f32[1088]{0:T(1024)S(1)} %get-tuple-element.90, ...), channel_id=1, replica_groups=mesh['dp'=2,'gx'=4,'gy'=4] {'dp','gx','gy'}, use_global_device_ids=true, to_apply=%region_20.21 | all-reduce | flops 13056 | bytes 104448 | tf_op jit(solution)/shard_map/psum | solution.py:323
  550.7 3.0 copy.353
  (593 shorter events, 217.7 us)
Async XLA Ops:
  9.0 75.6 %collective-permute-start = (bf16[256,272]{0,1:T(8,128)(2,1)}, bf16[256,272]{0,1:T(8,128)(2,1)}, u32[]{:S(2)}, u32[]{:S(2)}) collective-permute-start(bf16[256,272]{0,1:T(8,128)(2,1)} %get-tuple-element.236), channel_id=1, source_target_pairs={{0,0},{1,2},{2,16},{3,18},{16,1},{17,3},{18,17},{19,19},{4,4},{5,6... | collective-permute-start | bytes 417800 | tf_op jit(solution)/shard_map/ppermute | solution.py:67
  11.8 74.3 %collective-permute-start.1 = (bf16[256,272]{0,1:T(8,128)(2,1)}, bf16[256,272]{0,1:T(8,128)(2,1)}, u32[]{:S(2)}, u32[]{:S(2)}) collective-permute-start(bf16[256,272]{0,1:T(8,128)(2,1)} %get-tuple-element.237), channel_id=1, source_target_pairs={{0,2},{1,0},{2,18},{3,16},{16,3},{17,1},{18,19},{19,17},{4,6},{5,4... | collective-permute-start | bytes 417800 | tf_op jit(solution)/shard_map/ppermute | solution.py:68
  16.7 69.8 %collective-permute-start.27 = (bf16[256,272]{0,1:T(8,128)(2,1)}, bf16[256,272]{0,1:T(8,128)(2,1)}, u32[]{:S(2)}, u32[]{:S(2)}) collective-permute-start(bf16[256,272]{0,1:T(8,128)(2,1)} %get-tuple-element.218), channel_id=1, source_target_pairs={{0,0},{1,2},{2,16},{3,18},{16,1},{17,3},{18,17},{19,19},{4,4},{5,6... | collective-permute-start | bytes 417800 | tf_op jit(solution)/shard_map/ppermute | solution.py:67
  19.5 67.0 %collective-permute-start.28 = (bf16[256,272]{0,1:T(8,128)(2,1)}, bf16[256,272]{0,1:T(8,128)(2,1)}, u32[]{:S(2)}, u32[]{:S(2)}) collective-permute-start(bf16[256,272]{0,1:T(8,128)(2,1)} %get-tuple-element.219), channel_id=1, source_target_pairs={{0,2},{1,0},{2,18},{3,16},{16,3},{17,1},{18,19},{19,17},{4,6},{5,4... | collective-permute-start | bytes 417800 | tf_op jit(solution)/shard_map/ppermute | solution.py:68
  22.3 58.3 %collective-permute-start.5 = (s32[2,1024]{1,0:T(2,128)}, s32[2,1024]{1,0:T(2,128)}, u32[]{:S(2)}, u32[]{:S(2)}) collective-permute-start(s32[2,1024]{1,0:T(2,128)} %param.17), channel_id=1, source_target_pairs={{0,16},{16,0},{1,17},{17,1},{2,18},{18,2},{3,19},{19,3},{4,20},{20... | collective-permute-start | bytes 24584 | tf_op jit(solution)/shard_map/ppermute | solution.py:24
  40.4 60.2 %all-to-all-start.1 = ((bf16[8,192,136]{1,2,0:T(8,128)(2,1)}), bf16[8,192,136]{1,2,0:T(8,128)(2,1)S(1)}, u32[]{:S(2)}, u32[]{:S(2)}) async-start(bf16[8,192,136]{1,2,0:T(8,128)(2,1)} %copy.304), calls=%async_computation.1 | async-start | bytes 1114112 | tf_op jit(solution)/shard_map/all_to_all | solution.py:195
  44.1 168.1 %all-gather.5.cloned.1.call-start = ((), (), s32[]{:S(2)}) async-start(), calls=%async_computation.8 | async-start | bytes 4177920 | tf_op jit(solution)/shard_map/all_gather | solution.py:202
  80.6 11.6 %collective-permute-start.15 = (bf16[272,272]{1,0:T(8,128)(2,1)}, bf16[272,272]{1,0:T(8,128)(2,1)S(1)}, u32[]{:S(2)}, u32[]{:S(2)}) collective-permute-start(bf16[272,272]{1,0:T(8,128)(2,1)} %get-tuple-element.196), channel_id=1, source_target_pairs={{0,4},{4,0},{8,12},{12,8},{1,5},{5,1},{9,13},{13,9},{2,6},{6,2},{1... | collective-permute-start | bytes 443912 | tf_op jit(solution)/shard_map/ppermute | solution.py:28
  84.7 13.7 %collective-permute-start.16 = (bf16[272,272]{1,0:T(8,128)(2,1)}, bf16[272,272]{1,0:T(8,128)(2,1)S(1)}, u32[]{:S(2)}, u32[]{:S(2)}) collective-permute-start(bf16[272,272]{1,0:T(8,128)(2,1)} %get-tuple-element.197), channel_id=1, source_target_pairs={{0,8},{4,12},{8,0},{12,4},{1,9},{5,13},{9,1},{13,5},{2,10},{6,14},... | collective-permute-start | bytes 443912 | tf_op jit(solution)/shard_map/ppermute | solution.py:28
  86.1 12.2 %collective-permute-start.17 = (bf16[272,272]{1,0:T(8,128)(2,1)}, bf16[272,272]{1,0:T(8,128)(2,1)S(1)}, u32[]{:S(2)}, u32[]{:S(2)}) collective-permute-start(bf16[272,272]{1,0:T(8,128)(2,1)} %get-tuple-element.198), channel_id=1, source_target_pairs={{0,12},{4,8},{8,4},{12,0},{1,13},{5,9},{9,5},{13,1},{2,14},{6,10},... | collective-permute-start | bytes 443912 | tf_op jit(solution)/shard_map/ppermute | solution.py:28
  88.4 17.4 %collective-permute-start.29 = (bf16[512,272]{0,1:T(8,128)(2,1)}, bf16[512,272]{0,1:T(8,128)(2,1)S(1)}, u32[]{:S(2)}, u32[]{:S(2)}) collective-permute-start(bf16[512,272]{0,1:T(8,128)(2,1)} %get-tuple-element.215), channel_id=1, source_target_pairs={{0,4},{4,0},{8,12},{12,8},{1,5},{5,1},{9,13},{13,9},{2,6},{6,2},{1... | collective-permute-start | bytes 835592 | tf_op jit(solution)/shard_map/ppermute | solution.py:28
  90.1 19.2 %collective-permute-start.30 = (bf16[512,272]{0,1:T(8,128)(2,1)}, bf16[512,272]{0,1:T(8,128)(2,1)}, u32[]{:S(2)}, u32[]{:S(2)}) collective-permute-start(bf16[512,272]{0,1:T(8,128)(2,1)} %get-tuple-element.215), channel_id=1, source_target_pairs={{0,8},{4,12},{8,0},{12,4},{1,9},{5,13},{9,1},{13,5},{2,10},{6,14},... | collective-permute-start | bytes 835592 | tf_op jit(solution)/shard_map/ppermute | solution.py:28
  92.3 17.0 %collective-permute-start.31 = (bf16[512,272]{0,1:T(8,128)(2,1)}, bf16[512,272]{0,1:T(8,128)(2,1)}, u32[]{:S(2)}, u32[]{:S(2)}) collective-permute-start(bf16[512,272]{0,1:T(8,128)(2,1)} %get-tuple-element.215), channel_id=1, source_target_pairs={{0,12},{4,8},{8,4},{12,0},{1,13},{5,9},{9,5},{13,1},{2,14},{6,10},... | collective-permute-start | bytes 835592 | tf_op jit(solution)/shard_map/ppermute | solution.py:28
  98.3 13.9 %collective-permute-start.2 = (bf16[512,272]{0,1:T(8,128)(2,1)}, bf16[512,272]{0,1:T(8,128)(2,1)}, u32[]{:S(2)}, u32[]{:S(2)}) collective-permute-start(bf16[512,272]{0,1:T(8,128)(2,1)} %get-tuple-element.233), channel_id=1, source_target_pairs={{0,4},{4,0},{8,12},{12,8},{1,5},{5,1},{9,13},{13,9},{2,6},{6,2},{1... | collective-permute-start | bytes 835592 | tf_op jit(solution)/shard_map/ppermute | solution.py:28
  98.4 16.9 %collective-permute-start.3 = (bf16[512,272]{0,1:T(8,128)(2,1)}, bf16[512,272]{0,1:T(8,128)(2,1)}, u32[]{:S(2)}, u32[]{:S(2)}) collective-permute-start(bf16[512,272]{0,1:T(8,128)(2,1)} %get-tuple-element.233), channel_id=1, source_target_pairs={{0,8},{4,12},{8,0},{12,4},{1,9},{5,13},{9,1},{13,5},{2,10},{6,14},... | collective-permute-start | bytes 835592 | tf_op jit(solution)/shard_map/ppermute | solution.py:28
  100.6 38.0 %all-to-all-start = ((bf16[8,136,576]{2,1,0:T(8,128)(2,1)}), bf16[8,136,576]{2,1,0:T(8,128)(2,1)}, u32[]{:S(2)}, u32[]{:S(2)}) async-start(bf16[8,136,576]{2,1,0:T(8,128)(2,1)} %concatenate.135), calls=%async_computation | async-start | bytes 2785280 | tf_op jit(solution)/shard_map/all_to_all | solution.py:182
  105.8 25.9 %collective-permute-start.4 = (bf16[512,272]{0,1:T(8,128)(2,1)}, bf16[512,272]{0,1:T(8,128)(2,1)}, u32[]{:S(2)}, u32[]{:S(2)}) collective-permute-start(bf16[512,272]{0,1:T(8,128)(2,1)} %get-tuple-element.233), channel_id=1, source_target_pairs={{0,12},{4,8},{8,4},{12,0},{1,13},{5,9},{9,5},{13,1},{2,14},{6,10},... | collective-permute-start | bytes 835592 | tf_op jit(solution)/shard_map/ppermute | solution.py:28
  135.3 4.8 collective-permute-start.6
  161.4 6.6 %collective-permute-start.7 = (bf16[4,128,1088]{1,2,0:T(8,128)(2,1)S(1)}, bf16[4,128,1088]{1,2,0:T(8,128)(2,1)S(1)}, u32[]{:S(2)}, u32[]{:S(2)}) collective-permute-start(bf16[4,128,1088]{1,2,0:T(8,128)(2,1)S(1)} %copy_bitcast_fusion), channel_id=1, source_target_pairs={{0,16},{16,0},{1,17},{17,1},{2,18},{18,2},{3,19},{19,3},{4,20},{20... | collective-permute-start | bytes 3342344 | tf_op jit(solution)/shard_map/ppermute | solution.py:24
  163.9 31.0 %collective-permute-start.32 = (bf16[4,128,1088]{1,2,0:T(8,128)(2,1)}, bf16[4,128,1088]{1,2,0:T(8,128)(2,1)}, u32[]{:S(2)}, u32[]{:S(2)}) collective-permute-start(bf16[4,128,1088]{1,2,0:T(8,128)(2,1)} %pad_maximum_fusion.9), channel_id=1, source_target_pairs={{0,16},{16,0},{1,17},{17,1},{2,18},{18,2},{3,19},{19,3},{4,20},{20... | collective-permute-start | bytes 3342344 | tf_op jit(solution)/shard_map/ppermute | solution.py:24
  168.4 10.5 %collective-permute-start.10 = (bf16[128,1088]{0,1:T(8,128)(2,1)S(1)}, bf16[128,1088]{0,1:T(8,128)(2,1)S(1)}, u32[]{:S(2)}, u32[]{:S(2)}) collective-permute-start(bf16[128,1088]{0,1:T(8,128)(2,1)S(1)} %get-tuple-element.161), channel_id=1, source_target_pairs={{0,12},{4,8},{8,4},{12,0},{1,13},{5,9},{9,5},{13,1},{2,14},{6,10},... | collective-permute-start | bytes 835592 | tf_op jit(solution)/shard_map/ppermute | solution.py:28
  169.8 13.8 %collective-permute-start.8 = (bf16[128,1088]{0,1:T(8,128)(2,1)S(1)}, bf16[128,1088]{0,1:T(8,128)(2,1)S(1)}, u32[]{:S(2)}, u32[]{:S(2)}) collective-permute-start(bf16[128,1088]{0,1:T(8,128)(2,1)S(1)} %get-tuple-element.160), channel_id=1, source_target_pairs={{0,4},{4,0},{8,12},{12,8},{1,5},{5,1},{9,13},{13,9},{2,6},{6,2},{1... | collective-permute-start | bytes 835592 | tf_op jit(solution)/shard_map/ppermute | solution.py:28
  170.5 13.9 %collective-permute-start.9 = (bf16[128,1088]{0,1:T(8,128)(2,1)S(1)}, bf16[128,1088]{0,1:T(8,128)(2,1)S(1)}, u32[]{:S(2)}, u32[]{:S(2)}) collective-permute-start(bf16[128,1088]{0,1:T(8,128)(2,1)S(1)} %get-tuple-element.162), channel_id=1, source_target_pairs={{0,8},{4,12},{8,0},{12,4},{1,9},{5,13},{9,1},{13,5},{2,10},{6,14},... | collective-permute-start | bytes 835592 | tf_op jit(solution)/shard_map/ppermute | solution.py:28
  186.5 22.3 %collective-permute-start.11 = (bf16[128,1088]{0,1:T(8,128)(2,1)S(1)}, bf16[128,1088]{0,1:T(8,128)(2,1)S(1)}, u32[]{:S(2)}, u32[]{:S(2)}) collective-permute-start(bf16[128,1088]{0,1:T(8,128)(2,1)S(1)} %get-tuple-element.128), channel_id=1, source_target_pairs={{0,4},{4,0},{8,12},{12,8},{1,5},{5,1},{9,13},{13,9},{2,6},{6,2},{1... | collective-permute-start | bytes 835592 | tf_op jit(solution)/shard_map/ppermute | solution.py:28
  187.8 21.1 %collective-permute-start.12 = (bf16[128,1088]{0,1:T(8,128)(2,1)S(1)}, bf16[128,1088]{0,1:T(8,128)(2,1)S(1)}, u32[]{:S(2)}, u32[]{:S(2)}) collective-permute-start(bf16[128,1088]{0,1:T(8,128)(2,1)S(1)} %get-tuple-element.128), channel_id=1, source_target_pairs={{0,8},{4,12},{8,0},{12,4},{1,9},{5,13},{9,1},{13,5},{2,10},{6,14},... | collective-permute-start | bytes 835592 | tf_op jit(solution)/shard_map/ppermute | solution.py:28
  188.5 20.4 %collective-permute-start.13 = (bf16[128,1088]{0,1:T(8,128)(2,1)S(1)}, bf16[128,1088]{0,1:T(8,128)(2,1)S(1)}, u32[]{:S(2)}, u32[]{:S(2)}) collective-permute-start(bf16[128,1088]{0,1:T(8,128)(2,1)S(1)} %get-tuple-element.128), channel_id=1, source_target_pairs={{0,12},{4,8},{8,4},{12,0},{1,13},{5,9},{9,5},{13,1},{2,14},{6,10},... | collective-permute-start | bytes 835592 | tf_op jit(solution)/shard_map/ppermute | solution.py:28
  210.0 18.7 %collective-permute-start.14 = (bf16[4,128,1088]{1,2,0:T(8,128)(2,1)}, bf16[4,128,1088]{1,2,0:T(8,128)(2,1)}, u32[]{:S(2)}, u32[]{:S(2)}) collective-permute-start(bf16[4,128,1088]{1,2,0:T(8,128)(2,1)} %pad_maximum_fusion.7), channel_id=1, source_target_pairs={{0,16},{16,0},{1,17},{17,1},{2,18},{18,2},{3,19},{19,3},{4,20},{20... | collective-permute-start | bytes 3342344 | tf_op jit(solution)/shard_map/ppermute | solution.py:24
  249.6 43.8 %collective-permute-start.33 = (bf16[4,128,1088]{1,2,0:T(8,128)(2,1)}, bf16[4,128,1088]{1,2,0:T(8,128)(2,1)}, u32[]{:S(2)}, u32[]{:S(2)}) collective-permute-start(bf16[4,128,1088]{1,2,0:T(8,128)(2,1)} %copy.327), channel_id=1, source_target_pairs={{0,16},{16,0},{1,17},{17,1},{2,18},{18,2},{3,19},{19,3},{4,20},{20... | collective-permute-start | bytes 3342344 | tf_op jit(solution)/shard_map/ppermute | solution.py:24
  280.8 17.9 %collective-permute-start.18 = (bf16[4,128,1088]{1,2,0:T(8,128)(2,1)}, bf16[4,128,1088]{1,2,0:T(8,128)(2,1)S(1)}, u32[]{:S(2)}, u32[]{:S(2)}) collective-permute-start(bf16[4,128,1088]{1,2,0:T(8,128)(2,1)} %copy.317), channel_id=1, source_target_pairs={{0,16},{16,0},{1,17},{17,1},{2,18},{18,2},{3,19},{19,3},{4,20},{20... | collective-permute-start | bytes 3342344 | tf_op jit(solution)/shard_map/ppermute | solution.py:24
  295.2 9.5 %collective-permute-start.34 = (bf16[128,1088]{0,1:T(8,128)(2,1)S(1)}, bf16[128,1088]{0,1:T(8,128)(2,1)S(1)}, u32[]{:S(2)}, u32[]{:S(2)}) collective-permute-start(bf16[128,1088]{0,1:T(8,128)(2,1)S(1)} %get-tuple-element.149), channel_id=1, source_target_pairs={{0,4},{4,0},{8,12},{12,8},{1,5},{5,1},{9,13},{13,9},{2,6},{6,2},{1... | collective-permute-start | bytes 835592 | tf_op jit(solution)/shard_map/ppermute | solution.py:28
  296.5 15.5 %collective-permute-start.35 = (bf16[128,1088]{0,1:T(8,128)(2,1)S(1)}, bf16[128,1088]{0,1:T(8,128)(2,1)S(1)}, u32[]{:S(2)}, u32[]{:S(2)}) collective-permute-start(bf16[128,1088]{0,1:T(8,128)(2,1)S(1)} %get-tuple-element.151), channel_id=1, source_target_pairs={{0,8},{4,12},{8,0},{12,4},{1,9},{5,13},{9,1},{13,5},{2,10},{6,14},... | collective-permute-start | bytes 835592 | tf_op jit(solution)/shard_map/ppermute | solution.py:28
  297.2 14.8 %collective-permute-start.36 = (bf16[128,1088]{0,1:T(8,128)(2,1)S(1)}, bf16[128,1088]{0,1:T(8,128)(2,1)S(1)}, u32[]{:S(2)}, u32[]{:S(2)}) collective-permute-start(bf16[128,1088]{0,1:T(8,128)(2,1)S(1)} %get-tuple-element.150), channel_id=1, source_target_pairs={{0,12},{4,8},{8,4},{12,0},{1,13},{5,9},{9,5},{13,1},{2,14},{6,10},... | collective-permute-start | bytes 835592 | tf_op jit(solution)/shard_map/ppermute | solution.py:28
  299.1 17.5 %collective-permute-start.19 = (bf16[128,1088]{0,1:T(8,128)(2,1)S(1)}, bf16[128,1088]{0,1:T(8,128)(2,1)S(1)}, u32[]{:S(2)}, u32[]{:S(2)}) collective-permute-start(bf16[128,1088]{0,1:T(8,128)(2,1)S(1)} %get-tuple-element.157), channel_id=1, source_target_pairs={{0,4},{4,0},{8,12},{12,8},{1,5},{5,1},{9,13},{13,9},{2,6},{6,2},{1... | collective-permute-start | bytes 835592 | tf_op jit(solution)/shard_map/ppermute | solution.py:28
  300.5 22.7 %collective-permute-start.20 = (bf16[128,1088]{0,1:T(8,128)(2,1)S(1)}, bf16[128,1088]{0,1:T(8,128)(2,1)S(1)}, u32[]{:S(2)}, u32[]{:S(2)}) collective-permute-start(bf16[128,1088]{0,1:T(8,128)(2,1)S(1)} %get-tuple-element.159), channel_id=1, source_target_pairs={{0,8},{4,12},{8,0},{12,4},{1,9},{5,13},{9,1},{13,5},{2,10},{6,14},... | collective-permute-start | bytes 835592 | tf_op jit(solution)/shard_map/ppermute | solution.py:28
  304.7 18.5 %collective-permute-start.21 = (bf16[128,1088]{0,1:T(8,128)(2,1)S(1)}, bf16[128,1088]{0,1:T(8,128)(2,1)S(1)}, u32[]{:S(2)}, u32[]{:S(2)}) collective-permute-start(bf16[128,1088]{0,1:T(8,128)(2,1)S(1)} %get-tuple-element.158), channel_id=1, source_target_pairs={{0,12},{4,8},{8,4},{12,0},{1,13},{5,9},{9,5},{13,1},{2,14},{6,10},... | collective-permute-start | bytes 835592 | tf_op jit(solution)/shard_map/ppermute | solution.py:28
  324.9 9.6 %collective-permute-start.37 = (bf16[128,1088]{0,1:T(8,128)(2,1)S(1)}, bf16[128,1088]{0,1:T(8,128)(2,1)S(1)}, u32[]{:S(2)}, u32[]{:S(2)}) collective-permute-start(bf16[128,1088]{0,1:T(8,128)(2,1)S(1)} %get-tuple-element.112), channel_id=1, source_target_pairs={{0,4},{4,0},{8,12},{12,8},{1,5},{5,1},{9,13},{13,9},{2,6},{6,2},{1... | collective-permute-start | bytes 835592 | tf_op jit(solution)/shard_map/ppermute | solution.py:28
  325.7 13.7 %collective-permute-start.38 = (bf16[128,1088]{0,1:T(8,128)(2,1)S(1)}, bf16[128,1088]{0,1:T(8,128)(2,1)S(1)}, u32[]{:S(2)}, u32[]{:S(2)}) collective-permute-start(bf16[128,1088]{0,1:T(8,128)(2,1)S(1)} %get-tuple-element.112), channel_id=1, source_target_pairs={{0,8},{4,12},{8,0},{12,4},{1,9},{5,13},{9,1},{13,5},{2,10},{6,14},... | collective-permute-start | bytes 835592 | tf_op jit(solution)/shard_map/ppermute | solution.py:28
  326.7 12.7 %collective-permute-start.39 = (bf16[128,1088]{0,1:T(8,128)(2,1)S(1)}, bf16[128,1088]{0,1:T(8,128)(2,1)}, u32[]{:S(2)}, u32[]{:S(2)}) collective-permute-start(bf16[128,1088]{0,1:T(8,128)(2,1)S(1)} %get-tuple-element.112), channel_id=1, source_target_pairs={{0,12},{4,8},{8,4},{12,0},{1,13},{5,9},{9,5},{13,1},{2,14},{6,10},... | collective-permute-start | bytes 835592 | tf_op jit(solution)/shard_map/ppermute | solution.py:28
  340.5 2.8 collective-permute-start.40
  345.8 13.1 %all-to-all-start.3 = ((bf16[8,192,136]{1,2,0:T(8,128)(2,1)}), bf16[8,192,136]{1,2,0:T(8,128)(2,1)S(1)}, u32[]{:S(2)}, u32[]{:S(2)}) async-start(bf16[8,192,136]{1,2,0:T(8,128)(2,1)} %bitcast.468), calls=%async_computation.3 | async-start | bytes 1114112 | tf_op jit(solution)/shard_map/all_to_all | solution.py:295
  349.3 105.7 %reduce-scatter.10.cloned.1.call-start = ((), (), s32[]{:S(2)}) async-start(), calls=%async_computation.9 | async-start | bytes 696320
  360.1 127.7 %reduce-scatter.8.cloned.1.call-start = ((), (), s32[]{:S(2)}) async-start(), calls=%async_computation.7 | async-start | bytes 3133440 | tf_op jit(solution)/shard_map/reduce_scatter | solution.py:286
  371.2 6.7 %collective-permute-start.22 = (bf16[128,272]{0,1:T(8,128)(2,1)}, bf16[128,272]{0,1:T(8,128)(2,1)}, u32[]{:S(2)}, u32[]{:S(2)}) collective-permute-start(bf16[128,272]{0,1:T(8,128)(2,1)} %get-tuple-element.231), channel_id=1, source_target_pairs={{0,4},{4,0},{8,12},{12,8},{1,5},{5,1},{9,13},{13,9},{2,6},{6,2},{1... | collective-permute-start | bytes 208904 | tf_op jit(solution)/shard_map/ppermute | solution.py:28
  372.1 5.8 %collective-permute-start.23 = (bf16[128,272]{0,1:T(8,128)(2,1)}, bf16[128,272]{0,1:T(8,128)(2,1)}, u32[]{:S(2)}, u32[]{:S(2)}) collective-permute-start(bf16[128,272]{0,1:T(8,128)(2,1)} %get-tuple-element.230), channel_id=1, source_target_pairs={{0,8},{4,12},{8,0},{12,4},{1,9},{5,13},{9,1},{13,5},{2,10},{6,14},... | collective-permute-start | bytes 208904 | tf_op jit(solution)/shard_map/ppermute | solution.py:28
  372.8 5.5 collective-permute-start.24
  382.0 4.9 collective-permute-start.25
  382.8 16.0 %collective-permute-start.26 = (bf16[256,272]{0,1:T(8,128)(2,1)S(1)}, bf16[256,272]{0,1:T(8,128)(2,1)S(1)}, u32[]{:S(2)}, u32[]{:S(2)}) collective-permute-start(bf16[256,272]{0,1:T(8,128)(2,1)S(1)} %bitcast.535), channel_id=1, source_target_pairs={{2,0},{0,1},{18,2},{16,3},{3,16},{1,17},{19,18},{17,19},{6,4},{4,5... | collective-permute-start | bytes 417800 | tf_op jit(solution)/shard_map/ppermute | solution.py:77
  435.2 21.3 %collective-permute-start.41 = (bf16[4,128,1088]{1,2,0:T(8,128)(2,1)}, bf16[4,128,1088]{1,2,0:T(8,128)(2,1)}, u32[]{:S(2)}, u32[]{:S(2)}) collective-permute-start(bf16[4,128,1088]{1,2,0:T(8,128)(2,1)} %copy.334), channel_id=1, source_target_pairs={{0,16},{16,0},{1,17},{17,1},{2,18},{18,2},{3,19},{19,3},{4,20},{20... | collective-permute-start | bytes 3342344 | tf_op jit(solution)/shard_map/ppermute | solution.py:24
  442.9 22.9 %all-to-all-start.2 = ((bf16[8,136,576]{2,1,0:T(8,128)(2,1)}), bf16[8,136,576]{2,1,0:T(8,128)(2,1)}, u32[]{:S(2)}, u32[]{:S(2)}) async-start(bf16[8,136,576]{2,1,0:T(8,128)(2,1)} %bitcast.452), calls=%async_computation.2 | async-start | bytes 2785280 | tf_op jit(solution)/shard_map/all_to_all | solution.py:303
  447.2 100.5 %reduce-scatter.12.cloned.1.call-start = ((), (), s32[]{:S(2)}) async-start(), calls=%async_computation.10 | async-start | bytes 1218560
  456.0 47.4 %collective-permute-start.51 = (bf16[272,136]{0,1:T(8,128)(2,1)S(1)}, bf16[272,136]{0,1:T(8,128)(2,1)}, u32[]{:S(2)}, u32[]{:S(2)}) collective-permute-start(bf16[272,136]{0,1:T(8,128)(2,1)S(1)} %copy.357), channel_id=1, source_target_pairs={{0,16},{16,0},{1,17},{17,1},{2,18},{18,2},{3,19},{19,3},{4,20},{20... | collective-permute-start | bytes 221960 | tf_op jit(solution)/shard_map/ppermute | solution.py:24
  461.1 10.7 %collective-permute-start.42 = (bf16[128,1088]{0,1:T(8,128)(2,1)}, bf16[128,1088]{0,1:T(8,128)(2,1)}, u32[]{:S(2)}, u32[]{:S(2)}) collective-permute-start(bf16[128,1088]{0,1:T(8,128)(2,1)} %get-tuple-element.146), channel_id=1, source_target_pairs={{0,4},{4,0},{8,12},{12,8},{1,5},{5,1},{9,13},{13,9},{2,6},{6,2},{1... | collective-permute-start | bytes 835592 | tf_op jit(solution)/shard_map/ppermute | solution.py:28
  462.7 14.0 %collective-permute-start.43 = (bf16[128,1088]{0,1:T(8,128)(2,1)}, bf16[128,1088]{0,1:T(8,128)(2,1)}, u32[]{:S(2)}, u32[]{:S(2)}) collective-permute-start(bf16[128,1088]{0,1:T(8,128)(2,1)} %get-tuple-element.148), channel_id=1, source_target_pairs={{0,8},{4,12},{8,0},{12,4},{1,9},{5,13},{9,1},{13,5},{2,10},{6,14},... | collective-permute-start | bytes 835592 | tf_op jit(solution)/shard_map/ppermute | solution.py:28
  464.1 14.1 %collective-permute-start.44 = (bf16[128,1088]{0,1:T(8,128)(2,1)}, bf16[128,1088]{0,1:T(8,128)(2,1)}, u32[]{:S(2)}, u32[]{:S(2)}) collective-permute-start(bf16[128,1088]{0,1:T(8,128)(2,1)} %get-tuple-element.147), channel_id=1, source_target_pairs={{0,12},{4,8},{8,4},{12,0},{1,13},{5,9},{9,5},{13,1},{2,14},{6,10},... | collective-permute-start | bytes 835592 | tf_op jit(solution)/shard_map/ppermute | solution.py:28
  480.7 6.9 %collective-permute-start.45 = (bf16[128,272]{0,1:T(8,128)(2,1)S(1)}, bf16[128,272]{0,1:T(8,128)(2,1)S(1)}, u32[]{:S(2)}, u32[]{:S(2)}) collective-permute-start(bf16[128,272]{0,1:T(8,128)(2,1)S(1)} %get-tuple-element.213), channel_id=1, source_target_pairs={{0,4},{4,0},{8,12},{12,8},{1,5},{5,1},{9,13},{13,9},{2,6},{6,2},{1... | collective-permute-start | bytes 208904 | tf_op jit(solution)/shard_map/ppermute | solution.py:28
  481.4 6.3 %collective-permute-start.46 = (bf16[128,272]{0,1:T(8,128)(2,1)S(1)}, bf16[128,272]{0,1:T(8,128)(2,1)S(1)}, u32[]{:S(2)}, u32[]{:S(2)}) collective-permute-start(bf16[128,272]{0,1:T(8,128)(2,1)S(1)} %get-tuple-element.212), channel_id=1, source_target_pairs={{0,8},{4,12},{8,0},{12,4},{1,9},{5,13},{9,1},{13,5},{2,10},{6,14},... | collective-permute-start | bytes 208904 | tf_op jit(solution)/shard_map/ppermute | solution.py:28
  482.2 5.5 collective-permute-start.47
  491.8 8.2 %collective-permute-start.52 = (bf16[272,272]{1,0:T(8,128)(2,1)S(1)}, bf16[272,272]{1,0:T(8,128)(2,1)S(1)}, u32[]{:S(2)}, u32[]{:S(2)}) collective-permute-start(bf16[272,272]{1,0:T(8,128)(2,1)S(1)} %bitcast.532), channel_id=1, source_target_pairs={{0,4},{4,0},{8,12},{12,8},{1,5},{5,1},{9,13},{13,9},{2,6},{6,2},{1... | collective-permute-start | bytes 443912 | tf_op jit(solution)/shard_map/ppermute | solution.py:28
  493.2 9.6 %collective-permute-start.53 = (bf16[272,272]{1,0:T(8,128)(2,1)S(1)}, bf16[272,272]{1,0:T(8,128)(2,1)S(1)}, u32[]{:S(2)}, u32[]{:S(2)}) collective-permute-start(bf16[272,272]{1,0:T(8,128)(2,1)S(1)} %bitcast.531), channel_id=1, source_target_pairs={{0,8},{4,12},{8,0},{12,4},{1,9},{5,13},{9,1},{13,5},{2,10},{6,14},... | collective-permute-start | bytes 443912 | tf_op jit(solution)/shard_map/ppermute | solution.py:28
  494.4 8.4 %collective-permute-start.54 = (bf16[272,272]{1,0:T(8,128)(2,1)S(1)}, bf16[272,272]{1,0:T(8,128)(2,1)S(1)}, u32[]{:S(2)}, u32[]{:S(2)}) collective-permute-start(bf16[272,272]{1,0:T(8,128)(2,1)S(1)} %bitcast.533), channel_id=1, source_target_pairs={{0,12},{4,8},{8,4},{12,0},{1,13},{5,9},{9,5},{13,1},{2,14},{6,10},... | collective-permute-start | bytes 443912 | tf_op jit(solution)/shard_map/ppermute | solution.py:28
  497.2 47.9 %collective-permute-start.48 = (bf16[256,272]{0,1:T(8,128)(2,1)}, bf16[256,272]{0,1:T(8,128)(2,1)S(1)}, u32[]{:S(2)}, u32[]{:S(2)}) collective-permute-start(bf16[256,272]{0,1:T(8,128)(2,1)} %bitcast.440), channel_id=1, source_target_pairs={{0,0},{2,1},{16,2},{18,3},{1,16},{3,17},{17,18},{19,19},{4,4},{6,5... | collective-permute-start | bytes 417800 | tf_op jit(solution)/shard_map/ppermute | solution.py:76
  500.0 45.1 %collective-permute-start.49 = (bf16[256,272]{0,1:T(8,128)(2,1)}, bf16[256,272]{0,1:T(8,128)(2,1)}, u32[]{:S(2)}, u32[]{:S(2)}) collective-permute-start(bf16[256,272]{0,1:T(8,128)(2,1)} %bitcast.439), channel_id=1, source_target_pairs={{2,0},{0,1},{18,2},{16,3},{3,16},{1,17},{19,18},{17,19},{6,4},{4,5... | collective-permute-start | bytes 417800 | tf_op jit(solution)/shard_map/ppermute | solution.py:77
  503.4 43.4 %collective-permute-start.55 = (bf16[4,272,272]{2,1,0:T(8,128)(2,1)S(1)}, bf16[4,272,272]{2,1,0:T(8,128)(2,1)S(1)}, u32[]{:S(2)}, u32[]{:S(2)}) collective-permute-start(bf16[4,272,272]{2,1,0:T(8,128)(2,1)S(1)} %get-tuple-element.182), channel_id=1, source_target_pairs={{0,16},{16,0},{1,17},{17,1},{2,18},{18,2},{3,19},{19,3},{4,20},{20... | collective-permute-start | bytes 1775624 | tf_op jit(solution)/shard_map/ppermute | solution.py:24
  547.7 6.0 %collective-permute-start.50 = (bf16[136,816]{1,0:T(8,128)(2,1)}, bf16[136,816]{1,0:T(8,128)(2,1)S(1)}, u32[]{:S(2)}, u32[]{:S(2)}) collective-permute-start(bf16[136,816]{1,0:T(8,128)(2,1)} %bitcast.524), channel_id=1, source_target_pairs={{0,16},{16,0},{1,17},{17,1},{2,18},{18,2},{3,19},{19,3},{4,20},{20... | collective-permute-start | bytes 665864 | tf_op jit(solution)/shard_map/ppermute | solution.py:24
  (109 other events, 879.6 us)
Sparse Core Ops, SparseCore 0:
  100.7 65.9 all-gather.4
  360.2 20.0 reduce-scatter.9
  382.7 50.7 reduce-scatter.7
  487.7 26.8 reduce-scatter.11

commit v2 on v1

v2 whole, which is shorter than its diff:
```python
import math

import jax
import jax.numpy as jnp
import numpy as np
from jax import lax
from jax.experimental import pallas as pl
from jax.experimental.pallas import tpu as pltpu
from jax.sharding import Mesh
from jax.sharding import PartitionSpec as P

HEAD_DIM = 64
PAIR = 2 * HEAD_DIM
EPSILON = 1e-05
BLOCKED = -1e30
BF = jnp.bfloat16
F32 = jnp.float32
PLANE = ("c", "gx")
EVERY = ("c", "gx", "gy")
ROOT = math.sqrt(2.0 / math.pi)
WINDOW = 128
TALL = WINDOW + 16
MIB = 1024 * 1024


def dot(left, right, dims):
    return lax.dot_general(left, right, (dims, ((), ())), preferred_element_type=F32)


def kernel(body, outs, scratch, ids, *arrays, us=1.0, limit=40):
    in_specs = [pl.BlockSpec(memory_space=pltpu.SMEM)] + [pl.BlockSpec(memory_space=pltpu.VMEM)] * len(arrays)
    result = pl.pallas_call(
        body,
        out_shape=tuple(jax.ShapeDtypeStruct(shape, kind) for shape, kind in outs),
        in_specs=in_specs,
        out_specs=tuple(pl.BlockSpec(memory_space=pltpu.VMEM) for _ in outs),
        scratch_shapes=[pltpu.VMEM(shape, kind) for shape, kind in scratch],
        compiler_params=pltpu.CompilerParams(vmem_limit_bytes=limit * MIB),
        cost_estimate=pl.CostEstimate(flops=int(us * 6e8), bytes_accessed=int(us * 1e5), transcendentals=0),
    )(ids, *arrays)
    return result if len(outs) > 1 else result[0]


def swap_core(value):
    return lax.ppermute(value, "c", [(0, 1), (1, 0)])


def from_peer(value, step):
    return lax.ppermute(value, "gx", [(i, i ^ step) for i in range(4)])


def from_below(value, step):
    return lax.ppermute(value, "gy", [(i, (i + step) % 4) for i in range(4)])


def gather_plane(own):
    near = [own] + [from_peer(own, k) for k in range(1, 4)]
    return near + [swap_core(piece) for piece in near]


def position(c, g, z):
    return (c * 4 + g) * 4 + z


def token_moves():
    moves = []
    for m in range(4):
        move = []
        for c in range(2):
            for g in range(4):
                for z in range(4):
                    t, mb = (m ^ g) >> 1, (m ^ g) & 1
                    move.append((position(c, g, z), position(z // 2, 2 * (z % 2) + t, 2 * mb + c)))
        moves.append(move)
    return moves


MOVES = token_moves()
BACK = [[(b, a) for a, b in move] for move in MOVES]


def run_table(width, cols):
    table = np.zeros((8, 4, 3), np.int32)
    for d in range(8):
        filled = 0
        for z in range(4):
            for t in range(3):
                low = max(width * t + PAIR * d, cols * z)
                high = min(width * t + PAIR * (d + 1), cols * (z + 1))
                if high > low:
                    table[d, z] = (low - cols * z, high - low, filled)
                    filled += high - low
            if table[d, z, 1] == 0:
                table[d, z, 2] = filled
    return table.reshape(-1)


def aligned(value, step):
    return pl.multiple_of(value, step)


def normed(rows):
    average = jnp.mean(rows, axis=1, keepdims=True)
    centered = rows - average
    inverse = lax.rsqrt(jnp.mean(centered * centered, axis=1, keepdims=True) + EPSILON)
    return centered * inverse, inverse


def norm_pull(upstream, centered, inverse, gain):
    scaled = upstream * gain
    return inverse * (
        scaled
        - jnp.mean(scaled, axis=1, keepdims=True)
        - centered * jnp.mean(scaled * centered, axis=1, keepdims=True)
    )


def column_sum(rows):
    return jnp.sum(rows, axis=0, keepdims=True)


def place(ids):
    return ids[0], ids[1], ids[2], ids[3]


def run_of(ids, d, z):
    at = 4 + d * 12 + z * 3
    return ids[at], ids[at + 1], ids[at + 2]


def send_tokens(ids, src, *outs):
    g = ids[1]
    for m in range(4):
        v = m ^ g
        outs[m][...] = src[v & 1, v >> 1].T


def own_rows(ids, blocks, held):
    e = 2 * (ids[1] & 1) + (ids[2] >> 1)
    for m in range(4):
        held[m ^ e] = blocks[m][...]
    return held[...].astype(F32).reshape(-1, held.shape[2]).T


def take_tokens(ids, b0, b1, b2, b3, out, held):
    out[...] = own_rows(ids, (b0, b1, b2, b3), held).astype(BF)


def take_normed(ids, b0, b1, b2, b3, gain, shift, out, low, held):
    rows = own_rows(ids, (b0, b1, b2, b3), held)
    out[...] = rows.astype(BF)
    low[...] = (normed(rows)[0] * gain[...].astype(F32) + shift[...].astype(F32)).astype(BF)


def split_features(ids, rows, held, outs):
    e = 2 * (ids[1] & 1) + (ids[2] >> 1)
    held[...] = rows.T.reshape(held.shape).astype(BF)
    for m in range(4):
        outs[m][...] = held[m ^ e]


def land_tokens(ids, b0, b1, b2, b3, out):
    g = ids[1]
    for m, block in enumerate((b0, b1, b2, b3)):
        v = m ^ g
        out[v & 1, v >> 1] = block[...].T


def qkv_windows(ids, w, *rest):
    outs, tall = rest[:4], rest[4]
    c, g, z, d = place(ids)
    rows = w.shape[1]
    tall[:rows] = w[...].astype(F32).T
    tall[rows:] = jnp.zeros((tall.shape[0] - rows, tall.shape[1]), F32)
    for k in range(4):
        to = c * 4 + (g ^ k)
        start, _, _ = run_of(ids, to, z)
        outs[k][:WINDOW] = tall[pl.ds(aligned(start, 16), WINDOW)].astype(BF)
        shared = jnp.maximum(272 * z - HEAD_DIM + 8 * to, 0)
        outs[k][WINDOW:] = jnp.concatenate(
            [tall[pl.ds(aligned(shared, 8), 8)], jnp.zeros((8, tall.shape[1]), F32)], 0
        ).astype(BF)


def join_lanes(ids, b0, b1, b2, b3, out, held):
    g = ids[1]
    for k, block in enumerate((b0, b1, b2, b3)):
        held[g ^ k] = block[...]
    part = held.shape[2]
    for i in range(4):
        out[:, i * part : (i + 1) * part] = held[i]


def qkv_assemble(ids, b0, b1, b2, b3, out, shared, held, tall):
    c, g, z, d = place(ids)
    for s, block in enumerate((b0, b1, b2, b3)):
        held[(z + 4 - s) & 3] = block[...]
    for i in range(4):
        _, _, filled = run_of(ids, d, i)
        tall[pl.ds(aligned(filled, 16), WINDOW)] = held[i, :WINDOW]
    out[...] = tall[: out.shape[0]]
    parts = [held[1 + t, WINDOW:].astype(F32)[:8] for t in range(3)]
    shared[...] = jnp.concatenate(parts + [jnp.zeros_like(parts[0])], 0).astype(BF)


def mlp_blocks(ids, up, down, *outs):
    c, g, z, d = place(ids)
    for k in range(4):
        to = c * 4 + (g ^ k)
        outs[k][0] = up[to]
        outs[k][1] = down[to]


def mlp_join(ids, b0, b1, b2, b3, up, down, held):
    g = ids[1]
    for k, block in enumerate((b0, b1, b2, b3)):
        held[g ^ k] = block[...]
    part = held.shape[3]
    for i in range(4):
        up[:, i * part : (i + 1) * part] = held[i, 0]
        down[:, i * part : (i + 1) * part] = held[i, 1]


def out_half(ids, w, out, tall):
    tall[...] = w[...].astype(F32).T
    rows = out.shape[0]
    out[...] = tall[pl.ds(aligned(ids[0] * rows, 8), rows)].astype(BF)


def out_blocks(ids, b0, b1, b2, b3, out, held, wide):
    z = ids[2]
    for s, block in enumerate((b0, b1, b2, b3)):
        held[(z + 4 - s) & 3] = block[...]
    part = held.shape[2]
    for i in range(4):
        wide[:, i * part : (i + 1) * part] = held[i]
    for to in range(8):
        out[to, :, :PAIR] = wide[:, to * PAIR : (to + 1) * PAIR]
        out[to, :, PAIR:] = wide[:, 8 * PAIR :]


def out_weights(w):
    parts = [w[core * 4 + quarter] for quarter in range(4) for core in range(2)]
    return jnp.concatenate([part.astype(F32) for part in parts], 0).astype(BF)


def lane_head(shape):
    return lax.broadcasted_iota(jnp.int32, shape, len(shape) - 1) < HEAD_DIM


def only_head(value, head):
    low = lane_head(value.shape)
    zero = jnp.zeros_like(value)
    return jnp.where(low, value, zero) if head == 0 else jnp.where(low, zero, value)


def softmax_down(scores, allowed):
    masked = jnp.where(allowed, scores, BLOCKED)
    weights = jnp.exp(masked - jnp.max(masked, axis=0, keepdims=True))
    return (weights * (1.0 / jnp.sum(weights, axis=0, keepdims=True))).astype(BF)


def attend(ids, *refs):
    n, refs = refs[:8], refs[8:]
    w, refs = refs[0], refs[1:]
    sh, refs = refs[:8], refs[8:]
    q_bias, v_bias, segments, w_out = refs[:4]
    n_abs, q_out, k_out, v_out, kv_out, qs_out, probs, probs_s, att_rel, att_s, w16, far, near = refs[4:17]
    w16_f, att_abs = refs[17:]
    d = ids[3]
    rows = n_abs.shape[1]
    seq = 8 * rows
    for r in range(8):
        n_abs[r ^ d] = n[r][...]
        for t in range(3):
            w16_f[t, r ^ d] = sh[r][...].astype(F32)[t * 8 : (t + 1) * 8]
    tokens = n_abs[...].reshape(seq, n_abs.shape[2])
    w16_rows = w16_f[...].reshape(3 * HEAD_DIM, n_abs.shape[2]).astype(BF)
    w16[...] = w16_rows
    pair = aligned(d * PAIR, PAIR)
    projected = dot(tokens, w[...], ((1,), (1,)))
    q = (projected[:, :PAIR] + q_bias[:, pl.ds(pair, PAIR)].astype(F32)).astype(BF) * BF(HEAD_DIM**-0.5)
    k = projected[:, PAIR : 2 * PAIR].astype(BF)
    v = (projected[:, 2 * PAIR :] + v_bias[:, pl.ds(pair, PAIR)].astype(F32)).astype(BF)
    q_out[...] = q
    k_out[...] = k
    v_out[...] = v
    nothing = jnp.zeros((1, HEAD_DIM), F32)
    shared_v = jnp.concatenate([nothing, v_bias[:, 8 * PAIR :].astype(F32)], 1)
    shared_q = q_bias[:, 8 * PAIR :].astype(F32)
    kv = (dot(tokens, w16_rows[HEAD_DIM:], ((1,), (1,))) + shared_v).astype(BF)
    qs = (dot(n[0][...], w16_rows[:HEAD_DIM], ((1,), (1,))) + shared_q).astype(BF) * BF(HEAD_DIM**-0.5)
    qs = jnp.concatenate([qs, jnp.zeros_like(qs)], 1)
    kv_out[...] = kv
    qs_out[...] = qs

    seg_row = segments[...]
    seg_col = jnp.broadcast_to(seg_row, (8, seq)).T[:, :1]
    v_t = v.astype(F32).T.astype(BF)
    keys = [only_head(k, h) for h in range(2)]
    step = 2 * rows
    for b in range(4):
        seen = (b + 1) * step
        at = slice(b * step, seen)
        shape = (seen, step)
        causal = lax.broadcasted_iota(jnp.int32, shape, 0) <= lax.broadcasted_iota(jnp.int32, shape, 1) + b * step
        allowed = (seg_col[:seen] == seg_row[:, at]) & causal
        turned = []
        for h in range(2):
            p = softmax_down(dot(keys[h][:seen], q[at], ((1,), (1,))), allowed)
            probs[h, :seen, at] = p
            turned.append(dot(v_t[h * HEAD_DIM : (h + 1) * HEAD_DIM, :seen], p, ((1,), (0,))))
        attended = jnp.concatenate(turned, 0).T.astype(BF)
        att_abs[2 * b] = attended[:rows]
        att_abs[2 * b + 1] = attended[rows:]

    first = aligned(d * rows, rows)
    shape = (seq, rows)
    causal = lax.broadcasted_iota(jnp.int32, shape, 0) <= lax.broadcasted_iota(jnp.int32, shape, 1) + first
    allowed = (seg_col == segments[:, pl.ds(first, rows)]) & causal
    p = softmax_down(dot(only_head(kv, 0), qs, ((1,), (1,))), allowed)
    probs_s[...] = p
    kv_t = kv.astype(F32).T.astype(BF)
    attended_s = dot(kv_t[HEAD_DIM:], p, ((1,), (0,))).T.astype(BF)
    att_s[...] = attended_s

    for r in range(8):
        att_rel[r] = att_abs[r ^ d]
    wo = out_weights(w_out)
    for half, out in ((1, far), (0, near)):
        block = att_rel[4 * half : 4 * half + 4].reshape(4 * rows, PAIR)
        branch = dot(block, wo[:, :PAIR], ((1,), (1,)))
        out[...] = branch.astype(BF).reshape(out.shape)
        if half == 0:
            out[0] = (branch[:rows] + dot(attended_s, wo[:, PAIR:], ((1,), (1,)))).astype(BF)


def attend_back(ids, *refs):
    gb, refs = refs[:8], refs[8:]
    w_out, q_in, k_in, v_in, kv_in, qs_in, probs, probs_s, w, w16 = refs[:10]
    gb_rel, grads, grad_qs, sums, far = refs[10:15]
    g_abs, grads_rel = refs[15:]
    d = ids[3]
    rows = gb_rel.shape[1]
    seq = 8 * rows
    width = gb_rel.shape[2]
    for r in range(8):
        gb_rel[r] = gb[r][...]
    wo = out_weights(w_out)
    back = dot(gb_rel[...].reshape(seq, width), wo[:, :PAIR], ((1,), (0,))).astype(BF)
    for r in range(8):
        g_abs[r ^ d] = back[r * rows : (r + 1) * rows]
    g_all = g_abs[...].reshape(seq, PAIR)
    g_s = dot(gb[0][...], wo[:, PAIR:], ((1,), (0,))).astype(BF)
    q, k, v, kv, qs = q_in[...], k_in[...], v_in[...], kv_in[...], qs_in[...]
    scale = HEAD_DIM**-0.5
    k_t = k.astype(F32).T.astype(BF)
    values = [only_head(v, h) for h in range(2)]
    step = 2 * rows
    grad_q = []
    grad_k = [[jnp.zeros((step, PAIR), F32) for _ in range(4)] for _ in range(2)]
    grad_v = [[jnp.zeros((step, PAIR), F32) for _ in range(4)] for _ in range(2)]
    for b in range(4):
        seen = (b + 1) * step
        at = slice(b * step, seen)
        turned = []
        for h in range(2):
            p_low = probs[h, :seen, at]
            p = p_low.astype(F32)
            gp = dot(values[h][:seen], g_all[at], ((1,), (1,)))
            inner = jnp.sum(p * gp, axis=0, keepdims=True)
            gs = (p * (gp - inner)).astype(BF)
            turned.append(dot(k_t[h * HEAD_DIM : (h + 1) * HEAD_DIM, :seen], gs, ((1,), (0,))) * scale)
            dk = dot(gs, q[at], ((1,), (0,)))
            dv = dot(p_low, g_all[at], ((1,), (0,)))
            for i in range(b + 1):
                grad_k[h][i] = grad_k[h][i] + dk[i * step : (i + 1) * step]
                grad_v[h][i] = grad_v[h][i] + dv[i * step : (i + 1) * step]
        grad_q.append(jnp.concatenate(turned, 0).T)
    low = lane_head((step, PAIR))
    qsum = jnp.zeros((1, PAIR), F32)
    vsum = jnp.zeros((1, PAIR), F32)
    for i in range(4):
        dq = grad_q[i].astype(BF)
        dk = jnp.where(low, grad_k[0][i], grad_k[1][i]).astype(BF)
        dv = jnp.where(low, grad_v[0][i], grad_v[1][i]).astype(BF)
        qsum = qsum + column_sum(dq.astype(F32))
        vsum = vsum + column_sum(dv.astype(F32))
        for j in range(2):
            part = slice(j * rows, (j + 1) * rows)
            grads[2 * i + j, :, :PAIR] = dq[part]
            grads[2 * i + j, :, PAIR : 2 * PAIR] = dk[part]
            grads[2 * i + j, :, 2 * PAIR : 3 * PAIR] = dv[part]

    p_low = probs_s[...]
    p = p_low.astype(F32)
    v_s = jnp.concatenate([kv[:, HEAD_DIM:], jnp.zeros((seq, HEAD_DIM), BF)], 1)
    g_pad = jnp.concatenate([g_s, jnp.zeros((rows, HEAD_DIM), BF)], 1)
    gp = dot(v_s, g_pad, ((1,), (1,)))
    inner = jnp.sum(p * gp, axis=0, keepdims=True)
    gs = (p * (gp - inner)).astype(BF)
    kv_t = kv.astype(F32).T.astype(BF)
    dq = (dot(kv_t[:HEAD_DIM], gs, ((1,), (0,))) * scale).T.astype(BF)
    grad_qs[...] = dq
    dk = dot(gs, qs, ((1,), (0,)))[:, :HEAD_DIM]
    dv = dot(p_low, g_pad, ((1,), (0,)))[:, :HEAD_DIM]
    dkv = jnp.concatenate([dk, dv], 1).astype(BF)
    for r in range(8):
        grads[r, :, 3 * PAIR :] = dkv[r * rows : (r + 1) * rows]
    last = jnp.concatenate([column_sum(dq.astype(F32)), column_sum(dv.astype(BF).astype(F32))], 1)
    sums[...] = jnp.concatenate([qsum, vsum, last, jnp.zeros((5, PAIR), F32)], 0)

    for r in range(4):
        grads_rel[r] = grads[(r + 4) ^ d]
    joined = jnp.concatenate([w[...], w16[HEAD_DIM:]], 0)
    out = dot(grads_rel[...].reshape(4 * rows, 4 * PAIR), joined, ((1,), (0,)))
    far[...] = out.astype(BF).reshape(far.shape)


def qkv_grads(ids, grads, n_abs, grad_qs, n_own, *refs):
    o0, o1, o2, o3, shared_far, shared_near = refs[:6]
    tall, s32 = refs[6:]
    c, g, z, d = place(ids)
    rows, width = n_abs.shape[1], n_abs.shape[2]
    seq = 8 * rows
    tokens = n_abs[...].reshape(seq, width)
    out = dot(grads[...].reshape(seq, 4 * PAIR), tokens, ((0,), (0,)))
    tall[: 3 * PAIR] = out[: 3 * PAIR]
    tall[3 * PAIR :] = jnp.zeros((WINDOW, width), F32)
    line = lax.broadcasted_iota(jnp.int32, (WINDOW, width), 0)
    for s, ref in enumerate((o0, o1, o2, o3)):
        to = (z + s) & 3
        _, length, filled = run_of(ids, d, to)
        window = tall[pl.ds(aligned(filled, 16), WINDOW)]
        ref[...] = jnp.where(line < length, window, 0.0).astype(BF)
    q_part = dot(grad_qs[...], n_own[...], ((0,), (0,)))
    s32[...] = jnp.zeros(s32.shape, F32)
    for a in range(8):
        s32[a, :8] = q_part[a * 8 : (a + 1) * 8]
        s32[a, 8:16] = out[3 * PAIR + a * 8 : 3 * PAIR + (a + 1) * 8]
        s32[a, 16:24] = out[3 * PAIR + HEAD_DIM + a * 8 : 3 * PAIR + HEAD_DIM + (a + 1) * 8]
    for r in range(4):
        shared_near[r] = s32[r ^ d].astype(BF)
        shared_far[r] = s32[(r + 4) ^ d].astype(BF)


def first_near(ids, grads, w, w16, grad_qs, near, grads_rel):
    d = ids[3]
    rows = near.shape[1]
    for r in range(4):
        grads_rel[r] = grads[r ^ d]
    joined = jnp.concatenate([w[...], w16[HEAD_DIM:]], 0)
    out = dot(grads_rel[...].reshape(4 * rows, 4 * PAIR), joined, ((1,), (0,)))
    near[...] = out.astype(BF).reshape(near.shape)
    near[0] = (out[:rows] + dot(grad_qs[...], w16[:HEAD_DIM], ((1,), (0,)))).astype(BF)


def out_grads(ids, gb_rel, att_rel, att_s, out):
    rows, width = gb_rel.shape[1], gb_rel.shape[2]
    tokens = gb_rel[...].reshape(8 * rows, width)
    pair = dot(att_rel[...].reshape(8 * rows, PAIR), tokens, ((0,), (0,))).T
    shared = dot(att_s[...], gb_rel[0], ((0,), (0,))).T
    part = out.shape[1]
    for core in range(2):
        for quarter in range(4):
            at = slice((2 * quarter + core) * part, (2 * quarter + core + 1) * part)
            out[core * 4 + quarter] = jnp.concatenate([pair[at], shared[at]], 1).astype(BF)


def add_far(ids, near, far, s0, s1, s2, s3):
    s0[...] = near[0].astype(F32) + far[0].astype(F32)
    for k, ref in ((1, s1), (2, s2), (3, s3)):
        ref[...] = (near[k].astype(F32) + far[k].astype(F32)).astype(BF)


def add_far_shared(ids, near, far, shared_near, shared_far, s0, s1, s2, s3, t0, t1, t2, t3):
    add_far(ids, near, far, s0, s1, s2, s3)
    add_far(ids, shared_near, shared_far, t0, t1, t2, t3)


def total_of(s0, r1, r2, r3):
    return s0[...] + r1[...].astype(F32) + r2[...].astype(F32) + r3[...].astype(F32)


def middle_norm(ids, s0, r1, r2, r3, x_own, bias, gain, shift, middle, low):
    rows = x_own[...].astype(F32) + (total_of(s0, r1, r2, r3) + bias[...].astype(F32))
    middle[...] = rows
    low[...] = (normed(rows)[0] * gain[...].astype(F32) + shift[...].astype(F32)).astype(BF)


def middle_back(ids, s0, r1, r2, r3, middle, g_own, gain, grad_middle, low, sums):
    upstream = total_of(s0, r1, r2, r3)
    centered, inverse = normed(middle[...])
    g = g_own[...].astype(F32)
    grad = g + norm_pull(upstream, centered, inverse, gain[...].astype(F32))
    grad_middle[...] = grad
    rounded = grad.astype(BF)
    low[...] = rounded
    sums[...] = jnp.concatenate(
        [
            column_sum(rounded.astype(F32)),
            column_sum(upstream * centered),
            column_sum(upstream),
            column_sum(g),
        ],
        0,
    )


def finish_out(ids, s0, r1, r2, r3, middle, bias, o0, o1, o2, o3, held):
    rows = middle[...] + (total_of(s0, r1, r2, r3) + bias[...].astype(F32))
    split_features(ids, rows, held, (o0, o1, o2, o3))


def finish_in(ids, s0, r1, r2, r3, t0, u1, u2, u3, grad_middle, x_own, gain, *refs):
    o0, o1, o2, o3, sums, w0, w1, w2, w3 = refs[:9]
    held, s32 = refs[9:]
    z = ids[2]
    upstream = total_of(s0, r1, r2, r3)
    centered, inverse = normed(x_own[...].astype(F32))
    rows = grad_middle[...] + norm_pull(upstream, centered, inverse, gain[...].astype(F32))
    split_features(ids, rows, held, (o0, o1, o2, o3))
    sums[...] = jnp.concatenate([column_sum(upstream * centered), column_sum(upstream)], 0)
    shared = total_of(t0, u1, u2, u3)
    blank = jnp.zeros((16, shared.shape[1]), F32)
    s32[0] = blank
    for t in range(3):
        s32[1 + t] = jnp.concatenate([shared[t * 8 : (t + 1) * 8], blank[:8]], 0)
    for s, ref in enumerate((w0, w1, w2, w3)):
        ref[...] = s32[(z + s) & 3].astype(BF)


def grad_activated(ids, *refs):
    g, down, g_rel, out = refs[:8], refs[8], refs[9], refs[10]
    rows = g_rel.shape[1]
    for r in range(8):
        g_rel[r] = g[r][...]
    for b in range(4):
        block = g_rel[2 * b : 2 * b + 2].reshape(2 * rows, g_rel.shape[2])
        out[b * 2 * rows : (b + 1) * 2 * rows] = dot(block, down[...], ((1,), (1,)))


def feed_forward(ids, *refs):
    n, refs = refs[:8], refs[8:]
    up, grad_act, bias, n_rel, act, grad_pre, bias_sum, far, near = refs
    rows = n_rel.shape[1]
    for r in range(8):
        n_rel[r] = n[r][...]
    total = jnp.zeros(bias_sum.shape, F32)
    for b in (2, 3, 0, 1):
        at = slice(b * 2 * rows, (b + 1) * 2 * rows)
        block = n_rel[2 * b : 2 * b + 2].reshape(2 * rows, n_rel.shape[2])
        pre = dot(block, up[...], ((1,), (1,))) + bias[...]
        square = pre * pre
        bent = jnp.tanh(ROOT * pre * (1.0 + 0.044715 * square))
        half = 0.5 * (1.0 + bent)
        act[at] = (pre * half).astype(BF)
        slope = half + 0.5 * pre * (1.0 - bent * bent) * (ROOT + ROOT * 3.0 * 0.044715 * square)
        low = (grad_act[at] * slope).astype(BF)
        grad_pre[at] = low
        total = total + column_sum(low.astype(F32))
        out = dot(low, up[...], ((1,), (0,))).astype(BF)
        ref = far if b >= 2 else near
        for j in range(2):
            ref[2 * (b % 2) + j] = out[j * rows : (j + 1) * rows]
    bias_sum[...] = total


def feed_out(ids, act, down, far, near):
    rows = near.shape[1]
    for b in (2, 3, 0, 1):
        out = dot(act[b * 2 * rows : (b + 1) * 2 * rows], down[...], ((1,), (0,))).astype(BF)
        ref = far if b >= 2 else near
        for j in range(2):
            ref[2 * (b % 2) + j] = out[j * rows : (j + 1) * rows]


def mlp_grads(ids, act, grad_pre, n_rel, g_rel, out):
    rows, width = n_rel.shape[1], n_rel.shape[2]
    part = out.shape[2]
    up = dot(grad_pre[...], n_rel[...].reshape(8 * rows, width), ((0,), (0,)))
    for i in range(4):
        out[i, 0] = up[i * part : (i + 1) * part].astype(BF)
    down = dot(act[...], g_rel[...].reshape(8 * rows, width), ((0,), (0,)))
    for i in range(4):
        out[i, 1] = down[i * part : (i + 1) * part].astype(BF)


def mlp_lanes(ids, summed, o0, o1, o2, o3, held):
    g = ids[1]
    part = held.shape[3]
    for i in range(4):
        held[i] = summed[:, :, i * part : (i + 1) * part]
    for k, ref in enumerate((o0, o1, o2, o3)):
        ref[...] = held[g ^ k]


def mlp_land(ids, *refs):
    blocks, up, down, held = refs[:8], refs[8], refs[9], refs[10]
    d = ids[3]
    for r in range(8):
        held[r ^ d] = blocks[r][...].astype(F32)
    up[...] = held[:, 0].reshape(-1, held.shape[3]).T
    down[...] = held[:, 1].reshape(-1, held.shape[3])


def qkv_lanes(ids, b0, b1, b2, b3, w0, w1, w2, w3, o0, o1, o2, o3, held):
    g = ids[1]
    part = held.shape[2]
    window = sum(ref[...].astype(F32) for ref in (b0, b1, b2, b3))
    shared = sum(ref[...].astype(F32) for ref in (w0, w1, w2, w3))
    for i in range(4):
        held[i, :WINDOW] = window[:, i * part : (i + 1) * part].astype(BF)
        held[i, WINDOW:] = shared[:, i * part : (i + 1) * part].astype(BF)
    for k, ref in enumerate((o0, o1, o2, o3)):
        ref[...] = held[g ^ k]


def qkv_land(ids, *refs):
    blocks, out, tall = refs[:8], refs[8], refs[9]
    c, g, z, d = place(ids)
    tall[...] = jnp.zeros(tall.shape, F32)
    keep = jnp.where(z > 0, 1.0, 0.0)
    for r in range(8):
        owner = r ^ d
        start, _, _ = run_of(ids, owner, z)
        start = aligned(start, 16)
        block = blocks[r][...].astype(F32)
        tall[pl.ds(start, WINDOW)] = tall[pl.ds(start, WINDOW)] + block[:WINDOW]
        at = aligned(jnp.maximum(272 * z - HEAD_DIM + 8 * owner, 0), 8)
        tall[pl.ds(at, 8)] = tall[pl.ds(at, 8)] + block[WINDOW : WINDOW + 8] * keep
    out[...] = tall[: out.shape[1]].T


def out_split(ids, got, o0, o1, o2, o3, wide, held):
    z = ids[2]
    part = held.shape[2]
    shared = jnp.zeros((got.shape[1], HEAD_DIM), F32)
    for a in range(8):
        wide[:, a * PAIR : (a + 1) * PAIR] = got[a, :, :PAIR].astype(F32)
        shared = shared + got[a, :, PAIR:].astype(F32)
    wide[:, 8 * PAIR :] = shared
    for i in range(4):
        held[i] = wide[:, i * part : (i + 1) * part].astype(BF)
    for s, ref in enumerate((o0, o1, o2, o3)):
        ref[...] = held[(z + s) & 3]


def sum_four(ids, b0, b1, b2, b3, out):
    out[...] = sum(ref[...].astype(F32) for ref in (b0, b1, b2, b3)).astype(BF)


def out_land(ids, mine, theirs, out, held):
    c = ids[0]
    held[c] = mine[...].astype(F32)
    held[1 - c] = theirs[...].astype(F32)
    out[...] = held[...].reshape(-1, held.shape[2]).T


def shards(
    hidden_in,
    segment_ids,
    cotangent,
    norm1_gain,
    norm1_shift,
    w_qkv,
    q_bias,
    v_bias,
    w_out,
    out_bias,
    norm2_gain,
    norm2_shift,
    w_up,
    up_bias,
    w_down,
    down_bias,
):
    c = lax.axis_index("c")
    g = lax.axis_index("gx")
    z = lax.axis_index("gy")
    d = c * 4 + g
    width = norm1_gain.shape[0]
    hidden = up_bias.shape[0]
    quarter = hidden_in.shape[2]
    half = quarter // 2
    part = hidden // 32
    own_hidden = hidden // 8
    cols = w_qkv.shape[1]
    seq = segment_ids.shape[1]
    rows = seq // 8
    outer = lax.axis_size("do") > 1
    ids = jnp.concatenate(
        [jnp.stack([c, g, z, d]).astype(jnp.int32), jnp.asarray(run_table(width, cols))]
    )

    def row(vector):
        return vector.reshape(1, -1)

    def over_outer(value):
        return lax.psum(value, "do") if outer else value

    block = ((quarter, rows), BF)
    own_bf, own_f32 = ((rows, width), BF), ((rows, width), F32)
    held_tokens = ((4, quarter, rows), BF)

    def move_in(tokens):
        sent = kernel(send_tokens, [block] * 4, [], ids, tokens.reshape(2, 2, rows, quarter), us=1.0)
        return [lax.ppermute(sent[m], EVERY, MOVES[m]) for m in range(4)]

    def move_out(blocks):
        got = [lax.ppermute(blocks[m], EVERY, BACK[m]) for m in range(4)]
        out = kernel(land_tokens, [((2, 2, rows, quarter), BF)], [], ids, *got, us=1.0)
        return out.reshape(2, 2 * rows, quarter)

    x_blocks = move_in(hidden_in)

    window = ((TALL, quarter), BF)
    windows = kernel(qkv_windows, [window] * 4, [((cols + WINDOW, quarter), F32)], ids, w_qkv, us=1.5)
    windows = [windows[0]] + [from_peer(windows[k], k) for k in range(1, 4)]
    joined = kernel(join_lanes, [((TALL, width), BF)], [((4, TALL, quarter), BF)], ids, *windows, us=1.0)
    x_own, n1_own = kernel(
        take_normed, [own_bf, own_bf], [held_tokens], ids, *x_blocks, row(norm1_gain), row(norm1_shift), us=1.5
    )
    n1 = gather_plane(n1_own)
    joined = [joined] + [from_below(joined, s) for s in range(1, 4)]
    w_own, w_shared = kernel(
        qkv_assemble,
        [((3 * PAIR, width), BF), ((32, width), BF)],
        [((4, TALL, width), BF), ((3 * PAIR + WINDOW, width), BF)],
        ids,
        *joined,
        us=1.0,
    )
    w_shared = gather_plane(w_shared)

    out_piece = kernel(out_half, [((half, quarter), BF)], [((quarter, quarter), F32)], ids, w_out, us=0.7)
    out_pieces = [out_piece] + [from_below(out_piece, s) for s in range(1, 4)]
    out_sent = kernel(
        out_blocks,
        [((8, half, PAIR + HEAD_DIM), BF)],
        [((4, half, quarter), BF), ((half, width), BF)],
        ids,
        *out_pieces,
        us=0.7,
    )
    wo = lax.all_to_all(out_sent, PLANE, split_axis=0, concat_axis=0, tiled=True)

    mlp_sent = kernel(
        mlp_blocks,
        [((2, part, quarter), BF)] * 4,
        [],
        ids,
        w_up.T.reshape(8, part, quarter),
        w_down.reshape(8, part, quarter),
        us=1.0,
    )
    mlp_got = [mlp_sent[0]] + [from_peer(mlp_sent[k], k) for k in range(1, 4)]
    up_part, down_part = kernel(
        mlp_join, [((part, width), BF)] * 2, [((4, 2, part, quarter), BF)], ids, *mlp_got, us=1.0
    )
    up_own = lax.all_gather(up_part, "gy", axis=0, tiled=False).reshape(own_hidden, width)
    down_own = lax.all_gather(down_part, "gy", axis=0, tiled=False).reshape(own_hidden, width)
    up_bias_own = lax.dynamic_index_in_dim(up_bias.reshape(4, 8, part), d, 1, False).reshape(1, -1).astype(F32)

    g_own = kernel(take_tokens, [own_bf], [held_tokens], ids, *move_in(cotangent), us=1.0)
    g_all = gather_plane(g_own)

    ids_other = swap_core(segment_ids)
    segments = lax.dynamic_index_in_dim(jnp.where(z % 2 == c, segment_ids, ids_other), z // 2, 0, False)
    segments = row(segments.astype(F32))

    half_rows = ((4, rows, width), BF)
    pair_seq = ((seq, PAIR), BF)
    n_abs, q, k, v, kv, qs, probs, probs_s, att_rel, att_s, w16, far, near = kernel(
        attend,
        [
            ((8, rows, width), BF),
            pair_seq,
            pair_seq,
            pair_seq,
            pair_seq,
            ((rows, PAIR), BF),
            ((2, seq, seq), BF),
            ((seq, rows), BF),
            ((8, rows, PAIR), BF),
            ((rows, HEAD_DIM), BF),
            ((3 * HEAD_DIM, width), BF),
            half_rows,
            half_rows,
        ],
        [((3, 8, 8, width), F32), ((8, rows, PAIR), BF)],
        ids,
        *n1,
        w_own,
        *w_shared,
        row(q_bias),
        row(v_bias),
        segments,
        wo,
        us=12.0,
        limit=56,
    )
    summed = [own_f32, own_bf, own_bf, own_bf]

    def scatter(near, far):
        s = kernel(add_far, summed, [], ids, near, swap_core(far), us=1.2)
        return [s[0]] + [from_peer(s[k], k) for k in range(1, 4)]

    middle, n2_own = kernel(
        middle_norm,
        [own_f32, own_bf],
        [],
        ids,
        *scatter(near, far),
        x_own,
        row(out_bias),
        row(norm2_gain),
        row(norm2_shift),
        us=1.0,
    )
    n2 = gather_plane(n2_own)

    all_bf = ((8, rows, width), BF)
    g_rel, grad_act = kernel(
        grad_activated, [all_bf, ((seq, own_hidden), F32)], [], ids, *g_all, down_own, us=3.0
    )
    n_rel, act, grad_pre, up_sum, far, near = kernel(
        feed_forward,
        [
            all_bf,
            ((seq, own_hidden), BF),
            ((seq, own_hidden), BF),
            ((1, own_hidden), F32),
            half_rows,
            half_rows,
        ],
        [],
        ids,
        *n2,
        up_own,
        grad_act,
        up_bias_own,
        us=7.0,
    )
    parts = scatter(near, far)
    feed_far, feed_near = kernel(feed_out, [half_rows, half_rows], [], ids, act, down_own, us=2.5)
    mlp_partial = kernel(mlp_grads, [((4, 2, part, width), BF)], [], ids, act, grad_pre, n_rel, g_rel, us=5.0)
    mlp_summed = over_outer(lax.psum_scatter(mlp_partial, "gy", scatter_dimension=0, tiled=False))
    grad_middle, gb_own, middle_sums = kernel(
        middle_back,
        [own_f32, own_bf, ((4, width), F32)],
        [],
        ids,
        *parts,
        middle,
        g_own,
        row(norm2_gain),
        us=1.2,
    )
    gb = gather_plane(gb_own)
    result = kernel(
        finish_out,
        [block] * 4,
        [held_tokens],
        ids,
        *scatter(feed_near, feed_far),
        middle,
        row(down_bias),
        us=1.2,
    )
    hidden_out = move_out(result)

    gb_rel, grads, grad_qs, qkv_sums, far = kernel(
        attend_back,
        [all_bf, ((8, rows, 4 * PAIR), BF), ((rows, HEAD_DIM), BF), ((8, PAIR), F32), half_rows],
        [((8, rows, PAIR), BF), ((4, rows, 4 * PAIR), BF)],
        ids,
        *gb,
        wo,
        q,
        k,
        v,
        kv,
        qs,
        probs,
        probs_s,
        w_own,
        w16,
        us=14.0,
        limit=56,
    )
    far = swap_core(far)
    shared_rows = ((4, 32, width), BF)
    window_wide = ((WINDOW, width), BF)
    windows = kernel(
        qkv_grads,
        [window_wide] * 4 + [shared_rows] * 2,
        [((3 * PAIR + WINDOW, width), F32), ((8, 32, width), F32)],
        ids,
        grads,
        n_abs,
        grad_qs,
        n1_own,
        us=4.0,
    )
    shared_far, shared_near = swap_core(windows[4]), windows[5]
    windows = [windows[0]] + [from_below(windows[s], s) for s in range(1, 4)]
    near = kernel(
        first_near, [half_rows], [((4, rows, 4 * PAIR), BF)], ids, grads, w_own, w16, grad_qs, us=1.2
    )
    small_bf, small_f32 = ((32, width), BF), ((32, width), F32)
    s = kernel(
        add_far_shared,
        summed + [small_f32, small_bf, small_bf, small_bf],
        [],
        ids,
        near,
        far,
        shared_near,
        shared_far,
        us=1.4,
    )
    parts = [s[0]] + [from_peer(s[k], k) for k in range(1, 4)]
    shared_parts = [s[4]] + [from_peer(s[4 + k], k) for k in range(1, 4)]
    done = kernel(
        finish_in,
        [block] * 4 + [((2, width), F32)] + [((16, width), BF)] * 4,
        [held_tokens, ((4, 16, width), F32)],
        ids,
        *parts,
        *shared_parts,
        grad_middle,
        x_own,
        row(norm1_gain),
        us=1.5,
    )
    grad_in = move_out(done[:4])
    first_sums = done[4]
    shared_windows = [done[5]] + [from_below(done[5 + s], s) for s in range(1, 4)]

    lanes = kernel(
        mlp_lanes, [((2, part, quarter), BF)] * 4, [((4, 2, part, quarter), BF)], ids, mlp_summed, us=1.0
    )
    near = [lanes[0]] + [from_peer(lanes[k], k) for k in range(1, 4)]
    total_up, total_down = kernel(
        mlp_land,
        [((quarter, hidden // 4), F32), ((hidden // 4, quarter), F32)],
        [((8, 2, part, quarter), F32)],
        ids,
        *near,
        *[swap_core(piece) for piece in near],
        us=2.0,
    )

    out_sent = kernel(out_grads, [((8, half, PAIR + HEAD_DIM), BF)], [], ids, gb_rel, att_rel, att_s, us=2.5)
    out_got = lax.all_to_all(out_sent, PLANE, split_axis=0, concat_axis=0, tiled=True)
    out_split_parts = kernel(
        out_split,
        [((half, quarter), BF)] * 4,
        [((half, width), F32), ((4, half, quarter), BF)],
        ids,
        out_got,
        us=1.0,
    )
    out_split_parts = [out_split_parts[0]] + [from_below(out_split_parts[s], s) for s in range(1, 4)]
    mine = kernel(sum_four, [((half, quarter), BF)], [], ids, *out_split_parts, us=0.6)
    total_out = kernel(
        out_land, [((quarter, quarter), F32)], [((2, half, quarter), F32)], ids, mine, swap_core(mine), us=0.7
    )
    total_out = over_outer(total_out)

    lanes = kernel(
        qkv_lanes, [window] * 4, [((4, TALL, quarter), BF)], ids, *windows, *shared_windows, us=1.0
    )
    near = [lanes[0]] + [from_peer(lanes[k], k) for k in range(1, 4)]
    total_qkv = kernel(
        qkv_land,
        [((quarter, cols), F32)],
        [((cols + WINDOW, quarter), F32)],
        ids,
        *near,
        *[swap_core(piece) for piece in near],
        us=2.0,
    )
    total_qkv = over_outer(total_qkv)

    def spread(pair_sums, shared_sums):
        base = jnp.concatenate([jnp.zeros((8 * PAIR,), F32), shared_sums])
        return row(lax.dynamic_update_slice_in_dim(base, pair_sums, d * PAIR, 0))

    up_rows = lax.dynamic_update_slice_in_dim(
        jnp.zeros((4, 8, part), F32), up_sum.reshape(4, 1, part), d, 1
    ).reshape(4, 8 * part)
    smalls = jnp.concatenate(
        [
            first_sums,
            spread(qkv_sums[0], qkv_sums[2, :HEAD_DIM]),
            spread(qkv_sums[1], qkv_sums[2, HEAD_DIM:]),
            middle_sums,
            up_rows,
        ],
        0,
    )
    smalls = smalls + swap_core(smalls)
    smalls = smalls + from_peer(smalls, 1)
    smalls = smalls + from_peer(smalls, 2)
    smalls = smalls + lax.ppermute(smalls, "gy", [(i, i ^ 1) for i in range(4)])
    smalls = smalls + lax.ppermute(smalls, "gy", [(i, i ^ 2) for i in range(4)])
    smalls = over_outer(smalls)

    return (
        hidden_out,
        grad_in,
        smalls[0],
        smalls[1],
        total_qkv,
        smalls[2],
        smalls[3],
        total_out,
        smalls[4],
        smalls[5],
        smalls[6],
        total_up,
        smalls[8:12].reshape(hidden),
        total_down,
        smalls[7],
    )


def solution(mesh):
    devices = mesh.devices
    split = Mesh(
        devices.reshape(devices.shape[0] // 2, 2, devices.shape[1], devices.shape[2]), ("do", "c", "gx", "gy")
    )
    stream = P(None, ("do", "c", "gy"), "gx")
    flat = P()
    tall = P("gx", "gy")
    wide = P("gy", "gx")
    grads = (flat, flat, tall, flat, flat, wide, flat, flat, flat, tall, flat, wide, flat)
    return jax.shard_map(
        shards,
        mesh=split,
        in_specs=(stream, P(None, ("do", "c")), stream, *grads),
        out_specs=(stream, stream, *grads),
        check_vma=False,
    )
```

time: 572 us -> 451 us (0.79)
  starting transfers between devices: 76.4 us -> 193 us
  local copies, waits for them, and re-layouts: 175 us -> 65.7 us
  Pallas kernels: 0 us -> 82.3 us
  blocking collectives: 75.7 us -> 0 us
  other arithmetic: 64.3 us -> 1.59 us
  matrix products: 58.1 us -> 0 us
  waiting for transfers between devices: 95.9 us -> 87.6 us
    pallas_call x0 -> x37, Pallas kernels: none -> 82.3 us  [kernel(): pl.pallas_call(body, out_shape=tuple((jax.ShapeDtypeStruct(shape, kind) f...]
    ppermute x8 -> x33, starting transfers between devices: 16.1 us -> 79.6 us  [the longest x15 31.4 us: from_below(): return lax.ppermute(value, 'gy', [(i, (i + step) % 4) for i in range(4)])]
    dot_general x35 -> x0, matrix products: 58.1 us -> none  [dot(): lax.dot_general(left, right, (dims, ((), ())), preferred_element_type=F32)]
    slice x35 -> x3, local copies, waits for them, and re-layouts: 49.3 us -> 0.7 us  [the longest x1 0.7 us: shards(): smalls[7]]
    psum x1 -> x0, blocking collectives: 39.7 us -> none  [shards(): lax.psum((jnp.sum(grad_normed1 * centered1, axis=0), jnp.sum(grad_normed1...]
    ppermute x36 -> x44, starting transfers between devices: 42.2 us -> 80.7 us  [from_peer(): return lax.ppermute(value, 'gx', [(i, i ^ step) for i in range(4)])]
    all_gather x2 -> x0, blocking collectives: 36.1 us -> none  [the longest x1 20.8 us: shards(): qkv_all = lax.all_gather(qkv_half, 'gy', axis=1, tiled=True)]
    concatenate x21 -> x4, local copies, waits for them, and re-layouts: 32.8 us -> 0.8 us  [the longest x1 0.74 us: shards(): jnp.concatenate([jnp.stack([c, g, z, d]).astype(jnp.int32), jnp.asarray(r...]
  transfers between devices with their start and end apart: 64 -> 118, of which waited for: 23 -> 24; matrix products, arithmetic and copies ran while one was open for 46% -> 5% of each run, Pallas kernels for 0% -> 16%
where the time goes in v2:
time: 451 us; the launch traced here: 445 us
  starting transfers between devices  193 us (43%)
  waiting for transfers between devices  87.6 us (19%)
  Pallas kernels  82.3 us (18%)
  local copies, waits for them, and re-layouts  65.7 us (15%)
  between operations  15.3 us (3%)
    pallas_call x37, Pallas kernels, kernel(): pl.pallas_call(body, out_shape=tuple((jax.ShapeDtypeStruct(shape, kind) f...  82.3 us
    ppermute x44, starting transfers between devices, from_peer(): return lax.ppermute(value, 'gx', [(i, i ^ step) for i in range(4)])  80.7 us
    ppermute x44, waiting for transfers between devices, from_peer(): return lax.ppermute(value, 'gx', [(i, i ^ step) for i in range(4)])  69.2 us
    unnamed x200, local copies, waits for them, and re-layouts  46.8 us
    ppermute x15, starting transfers between devices, from_below(): return lax.ppermute(value, 'gy', [(i, (i + step) % 4) for i in range(4)])  31.4 us
    ppermute x8, starting transfers between devices, move_in(): return [lax.ppermute(sent[m], EVERY, MOVES[m]) for m in range(4)]  24.1 us
    ppermute x8, starting transfers between devices, move_out(): got = [lax.ppermute(blocks[m], EVERY, BACK[m]) for m in range(4)]  22.6 us
    ppermute x36, starting transfers between devices, swap_core(): return lax.ppermute(value, 'c', [(0, 1), (1, 0)])  21.9 us
  transfers between devices with their start and end apart: 118, of which 24 were waited for; matrix products, arithmetic and copies ran while one was open for 5% of the time, Pallas kernels for 16%

profile of v2, /device:TPU:0, one launch (start us, length us, event | category | flops | bytes accessed | tf_op | source)
XLA Modules:
  0.0 445.0 jit_solution(18370332627828941946)
XLA Ops:
  9.8 3.0 collective-permute-start.11
  16.0 4.4 collective-permute-start.1
  22.9 3.7 collective-permute-start.39
  28.1 2.0 collective-permute-start.2
  31.9 7.0 %collective-permute-done.2.b2 = bf16[272,128]{1,0:T(8,128)(2,1)S(1)} collective-permute-done((bf16[272,128]{1,0:T(8,128)(2,1)S(1)}, bf16[272,128]{1,0:T(8,128)(2,1)S(1)}, u32[]{:S(2)}, u32[]{:S(2)}) %collective-permute-start.2) | collective-permute-done | bytes 69664 | tf_op jit(solution)/shard_map/ppermute | solution.py:708
  39.8 6.2 %collective-permute-start.3 = (bf16[272,128]{1,0:T(8,128)(2,1)S(1)}, bf16[272,128]{1,0:T(8,128)(2,1)S(1)}, u32[]{:S(2)}, u32[]{:S(2)}) collective-permute-start(bf16[272,128]{1,0:T(8,128)(2,1)S(1)} %get-tuple-element.126), channel_id=1, source_target_pairs={{0,6},{1,14},{2,22},{3,30},{4,4},{5,12},{6,20},{7,28},{8,2},{9,10}... | collective-permute-start | bytes 208904 | tf_op jit(solution)/shard_map/ppermute | solution.py:708
  46.0 3.8 collective-permute-start.16
  51.6 8.9 %collective-permute-start.26 = (bf16[136,272]{1,0:T(8,128)(2,1)S(1)}, bf16[136,272]{1,0:T(8,128)(2,1)S(1)}, u32[]{:S(2)}, u32[]{:S(2)}) collective-permute-start(bf16[136,272]{1,0:T(8,128)(2,1)S(1)} %shard_map.285.b0), channel_id=1, source_target_pairs={{0,2},{1,3},{2,0},{3,1},{4,6},{5,7},{6,4},{7,5},{8,10},{9,11},{10,... | collective-permute-start | bytes 221960 | tf_op jit(solution)/shard_map/ppermute | solution.py:53
  60.5 3.0 collective-permute-start.27
  64.5 28.1 %collective-permute-start.6 = (bf16[128,1088]{1,0:T(8,128)(2,1)S(1)}, bf16[128,1088]{1,0:T(8,128)(2,1)S(1)}, u32[]{:S(2)}, u32[]{:S(2)}) collective-permute-start(bf16[128,1088]{1,0:T(8,128)(2,1)S(1)} %get-tuple-element.127.refs_0_.n_own), channel_id=1, source_target_pairs={{0,12},{4,8},{8,4},{12,0},{1,13},{5,9},{9,5},{13,1},{2,14},{6,10},... | collective-permute-start | bytes 835592 | tf_op jit(solution)/shard_map/ppermute | solution.py:49
  94.9 4.2 all-to-all-start
  103.8 2.6 collective-permute-done.4.refs_1_
  107.9 5.1 %collective-permute-done.17.refs_10_ = bf16[32,1088]{1,0:T(8,128)(2,1)S(1)} collective-permute-done((bf16[32,1088]{1,0:T(8,128)(2,1)S(1)}, bf16[32,1088]{1,0:T(8,128)(2,1)S(1)}, u32[]{:S(2)}, u32[]{:S(2)}) %collective-permute-start.17) | collective-permute-done | bytes 69664 | tf_op jit(solution)/shard_map/ppermute | solution.py:49
  113.2 5.1 %collective-permute-done.19.refs_12_ = bf16[32,1088]{1,0:T(8,128)(2,1)S(1)} collective-permute-done((bf16[32,1088]{1,0:T(8,128)(2,1)S(1)}, bf16[32,1088]{1,0:T(8,128)(2,1)S(1)}, u32[]{:S(2)}, u32[]{:S(2)}) %collective-permute-start.19) | collective-permute-done | bytes 69664 | tf_op jit(solution)/shard_map/ppermute | solution.py:49
  122.2 13.1 %shard_map.287 = (bf16[8,128,1088]{2,1,0:T(8,128)(2,1)}, bf16[1024,128]{1,0:T(8,128)(2,1)}, bf16[1024,128]{1,0:T(8,128)(2,1)}, bf16[1024,128]{1,0:T(8,128)(2,1)}...) custom-call(s32[100]{0:T(128)} %copy-done.5, ...), custom_call_target="tpu_custom_call" | custom-call | flops 7200000000 | bytes 1200000 | tf_op jit(solution)/shard_map/pallas_call | solution.py:32
  139.0 4.2 collective-permute-start.43
  144.0 5.2 %collective-permute-start.45 = (bf16[272,128]{1,0:T(8,128)(2,1)S(1)}, bf16[272,128]{1,0:T(8,128)(2,1)S(1)}, u32[]{:S(2)}, u32[]{:S(2)}) collective-permute-start(bf16[272,128]{1,0:T(8,128)(2,1)S(1)} %get-tuple-element.150), channel_id=1, source_target_pairs={{0,6},{1,14},{2,22},{3,30},{4,4},{5,12},{6,20},{7,28},{8,2},{9,10}... | collective-permute-start | bytes 208904 | tf_op jit(solution)/shard_map/ppermute | solution.py:708
  149.3 3.5 collective-permute-done.45.b3
  153.6 5.8 %collective-permute-start.47 = (bf16[128,1088]{1,0:T(8,128)(2,1)S(1)}, bf16[128,1088]{1,0:T(8,128)(2,1)S(1)}, u32[]{:S(2)}, u32[]{:S(2)}) collective-permute-start(bf16[128,1088]{1,0:T(8,128)(2,1)S(1)} %shard_map.293.refs_0_.g_own), channel_id=1, source_target_pairs={{0,8},{4,12},{8,0},{12,4},{1,9},{5,13},{9,1},{13,5},{2,10},{6,14},... | collective-permute-start | bytes 835592 | tf_op jit(solution)/shard_map/ppermute | solution.py:49
  163.4 3.4 collective-permute-start.31
  166.8 1.9 collective-permute-start.48
  170.2 2.2 collective-permute-done.29.r1
  174.1 12.0 %collective-permute-start.51 = (bf16[128,1088]{1,0:T(8,128)(2,1)S(1)}, bf16[128,1088]{1,0:T(8,128)(2,1)S(1)}, u32[]{:S(2)}, u32[]{:S(2)}) collective-permute-start(bf16[128,1088]{1,0:T(8,128)(2,1)S(1)} %collective-permute-done.47.refs_2_), channel_id=1, source_target_pairs={{0,16},{16,0},{1,17},{17,1},{2,18},{18,2},{3,19},{19,3},{4,20},{20... | collective-permute-start | bytes 835592 | tf_op jit(solution)/shard_map/ppermute | solution.py:45
  191.9 5.8 %collective-permute-done.32.refs_1_ = bf16[128,1088]{1,0:T(8,128)(2,1)S(1)} collective-permute-done((bf16[128,1088]{1,0:T(8,128)(2,1)S(1)}, bf16[128,1088]{1,0:T(8,128)(2,1)S(1)}, u32[]{:S(2)}, u32[]{:S(2)}) %collective-permute-start.32) | collective-permute-done | bytes 278560 | tf_op jit(solution)/shard_map/ppermute | solution.py:49
  197.7 4.9 %collective-permute-done.33.refs_2_ = bf16[128,1088]{1,0:T(8,128)(2,1)S(1)} collective-permute-done((bf16[128,1088]{1,0:T(8,128)(2,1)S(1)}, bf16[128,1088]{1,0:T(8,128)(2,1)S(1)}, u32[]{:S(2)}, u32[]{:S(2)}) %collective-permute-start.33) | collective-permute-done | bytes 278560 | tf_op jit(solution)/shard_map/ppermute | solution.py:49
  202.6 1.9 collective-permute-done.34.refs_3_
  206.1 3.2 shard_map.294
  213.7 1.7 copy-done.58
  215.4 6.6 %shard_map.295 = (bf16[8,128,1088]{2,1,0:T(8,128)(2,1)S(1)}, bf16[1024,544]{1,0:T(8,128)(2,1)S(1)}, bf16[1024,544]{1,0:T(8,128)(2,1)S(1)}, f32[1,544]{1,0:T(1,12...) custom-call(s32[100]{0:T(128)S(1)} %copy-done.6, ...), custom_call_target="tpu_custom_call" | custom-call | flops 4200000000 | bytes 700000 | tf_op jit(solution)/shard_map/pallas_call | solution.py:32
  234.4 5.1 %shard_map.314 = bf16[4,2,136,1088]{3,2,1,0:T(8,128)(2,1)} custom-call(s32[100]{0:T(128)S(1)} %copy-done.6, bf16[1024,544]{1,0:T(8,128)(2,1)S(1)} %copy-done.50, bf16[1024,544]{1,0:T(8,128)(2,1)S(1)} %copy-done.53, bf16[8,128,1088]{2,1,0:T(8,128)(2,1)S(1)} %copy-done.48, bf16[8,128,1088]{2,1,0:T(8,128)(2,1)S(1)} %copy-done.46), custom_call_target="tpu_custom_call" | custom-call | flops 3000000000 | bytes 500000 | tf_op jit(solution)/shard_map/pallas_call | solution.py:32
  239.6 2.0 copy.57.far
  243.1 1.7 collective-permute-start.63
  246.0 6.4 %collective-permute-done.62.r1 = bf16[128,1088]{1,0:T(8,128)(2,1)S(1)} collective-permute-done((bf16[128,1088]{1,0:T(8,128)(2,1)S(1)}, bf16[128,1088]{1,0:T(8,128)(2,1)S(1)}, u32[]{:S(2)}, u32[]{:S(2)}) %collective-permute-start.62) | collective-permute-done | bytes 278560 | tf_op jit(solution)/shard_map/ppermute | solution.py:49
  252.4 6.2 %collective-permute-done.63.r2 = bf16[128,1088]{1,0:T(8,128)(2,1)S(1)} collective-permute-done((bf16[128,1088]{1,0:T(8,128)(2,1)S(1)}, bf16[128,1088]{1,0:T(8,128)(2,1)S(1)}, u32[]{:S(2)}, u32[]{:S(2)}) %collective-permute-start.63) | collective-permute-done | bytes 278560 | tf_op jit(solution)/shard_map/ppermute | solution.py:49
  264.2 6.5 %collective-permute-done.65.refs_1_ = bf16[128,1088]{1,0:T(8,128)(2,1)S(1)} collective-permute-done((bf16[128,1088]{1,0:T(8,128)(2,1)S(1)}, bf16[128,1088]{1,0:T(8,128)(2,1)S(1)}, u32[]{:S(2)}, u32[]{:S(2)}) %collective-permute-start.65) | collective-permute-done | bytes 278560 | tf_op jit(solution)/shard_map/ppermute | solution.py:49
  270.6 6.2 %collective-permute-done.66.refs_2_ = bf16[128,1088]{1,0:T(8,128)(2,1)S(1)} collective-permute-done((bf16[128,1088]{1,0:T(8,128)(2,1)S(1)}, bf16[128,1088]{1,0:T(8,128)(2,1)S(1)}, u32[]{:S(2)}, u32[]{:S(2)}) %collective-permute-start.66) | collective-permute-done | bytes 278560 | tf_op jit(solution)/shard_map/ppermute | solution.py:49
  277.3 2.7 shard_map.296
  281.9 12.4 %shard_map.302 = (bf16[8,128,1088]{2,1,0:T(8,128)(2,1)}, bf16[8,128,512]{2,1,0:T(8,128)(2,1)}, bf16[128,64]{1,0:T(8,128)(2,1)}, f32[8,128]{1,0:T(8,128)}, bf16[4,128,1088]{2,1,0:T(8,128)(2,1)}) custom-call(s32[100]{0:T(128)} %copy-done.5, bf16[128,1088]{1,0:T(8,128)(2,1)} %copy-done.19, bf16[128,1088]{1,0:T(8,128)(2,1)} %copy-done.88, ...), custom_call_target="tpu_custom_call" | custom-call | flops 8400000000 | bytes 1400000 | tf_op jit(solution)/shard_map/pallas_call | solution.py:32
  294.3 2.4 copy.58
  297.1 2.1 copy.55.far
  308.0 3.2 shard_map.304
  315.0 3.5 collective-permute-done.55.r2
  322.6 3.6 collective-permute-start.58
  327.0 2.1 shard_map.310
  329.1 5.5 %all-to-all-start.1 = ((bf16[8,136,192]{2,1,0:T(8,128)(2,1)}), bf16[8,136,192]{2,1,0:T(8,128)(2,1)}, u32[]{:S(2)}, u32[]{:S(2)}) async-start(bf16[8,136,192]{2,1,0:T(8,128)(2,1)} %shard_map.310), calls=%async_computation.1 | async-start | bytes 1114112 | tf_op jit(solution)/shard_map/all_to_all | solution.py:956
  337.1 4.8 %collective-permute-start.60 = (bf16[272,128]{1,0:T(8,128)(2,1)}, bf16[272,128]{1,0:T(8,128)(2,1)}, u32[]{:S(2)}, u32[]{:S(2)}) collective-permute-start(bf16[272,128]{1,0:T(8,128)(2,1)} %get-tuple-element.164), channel_id=1, source_target_pairs={{6,0},{14,1},{22,2},{30,3},{4,4},{12,5},{20,6},{28,7},{2,8},{10,9}... | collective-permute-start | bytes 208904 | tf_op jit(solution)/shard_map/ppermute | solution.py:711
  346.0 2.0 shard_map.305
  349.7 3.4 collective-permute-start.79
  356.9 2.7 collective-permute-start.76
  362.1 4.2 collective-permute-done.74.r1
  367.4 4.2 collective-permute-start.103
  371.7 1.9 collective-permute-start.104
  375.6 1.9 shard_map.306
  379.6 2.3 collective-permute-done.103.b2
  381.9 2.8 collective-permute-start.94
  387.8 3.3 collective-permute-start.81
  391.1 2.5 collective-permute-start.82
  394.4 4.7 %collective-permute-done.85 = f32[12,1088]{1,0:T(8,128)S(1)} collective-permute-done((f32[12,1088]{1,0:T(8,128)S(1)}, f32[12,1088]{1,0:T(8,128)S(1)}, u32[]{:S(2)}, u32[]{:S(2)}) %collective-permute-start.85) | collective-permute-done | bytes 52256 | tf_op jit(solution)/shard_map/ppermute | solution.py:49
  399.3 1.9 collective-permute-start.86
  402.9 3.8 collective-permute-done.86
  406.7 4.5 %collective-permute-start.83 = (bf16[272,128]{1,0:T(8,128)(2,1)S(1)}, bf16[272,128]{1,0:T(8,128)(2,1)S(1)}, u32[]{:S(2)}, u32[]{:S(2)}) collective-permute-start(bf16[272,128]{1,0:T(8,128)(2,1)S(1)} %copy-done.23), channel_id=1, source_target_pairs={{6,0},{14,1},{22,2},{30,3},{4,4},{12,5},{20,6},{28,7},{2,8},{10,9}... | collective-permute-start | bytes 208904 | tf_op jit(solution)/shard_map/ppermute | solution.py:711
  427.4 2.2 shard_map.309
  429.5 3.5 collective-permute-done.88
  434.4 2.3 shard_map.316
  (456 shorter events, 137.0 us)
Async XLA Ops:
  7.2 197.6 %all-gather.7.cloned.1.call-start = ((), (), s32[]{:S(2)}) async-start(), calls=%async_computation.5 | async-start | bytes 1566720 | tf_op jit(solution)/shard_map/all_gather | solution.py:762
  9.8 16.8 %collective-permute-start.11 = (bf16[144,272]{1,0:T(8,128)(2,1)S(1)}, bf16[144,272]{1,0:T(8,128)(2,1)S(1)}, u32[]{:S(2)}, u32[]{:S(2)}) collective-permute-start(bf16[144,272]{1,0:T(8,128)(2,1)S(1)} %get-tuple-element.129), channel_id=1, source_target_pairs={{0,4},{4,0},{8,12},{12,8},{1,5},{5,1},{9,13},{13,9},{2,6},{6,2},{1... | collective-permute-start | bytes 235016 | tf_op jit(solution)/shard_map/ppermute | solution.py:49
  12.9 13.8 %collective-permute-start.12 = (bf16[144,272]{1,0:T(8,128)(2,1)S(1)}, bf16[144,272]{1,0:T(8,128)(2,1)S(1)}, u32[]{:S(2)}, u32[]{:S(2)}) collective-permute-start(bf16[144,272]{1,0:T(8,128)(2,1)S(1)} %get-tuple-element.130), channel_id=1, source_target_pairs={{0,8},{4,12},{8,0},{12,4},{1,9},{5,13},{9,1},{13,5},{2,10},{6,14},... | collective-permute-start | bytes 235016 | tf_op jit(solution)/shard_map/ppermute | solution.py:49
  14.4 13.7 %collective-permute-start.13 = (bf16[144,272]{1,0:T(8,128)(2,1)S(1)}, bf16[144,272]{1,0:T(8,128)(2,1)S(1)}, u32[]{:S(2)}, u32[]{:S(2)}) collective-permute-start(bf16[144,272]{1,0:T(8,128)(2,1)S(1)} %get-tuple-element.131), channel_id=1, source_target_pairs={{0,12},{4,8},{8,4},{12,0},{1,13},{5,9},{9,5},{13,1},{2,14},{6,10},... | collective-permute-start | bytes 235016 | tf_op jit(solution)/shard_map/ppermute | solution.py:49
  16.0 14.9 %collective-permute-start.1 = (bf16[272,128]{1,0:T(8,128)(2,1)S(1)}, bf16[272,128]{1,0:T(8,128)(2,1)S(1)}, u32[]{:S(2)}, u32[]{:S(2)}) collective-permute-start(bf16[272,128]{1,0:T(8,128)(2,1)S(1)} %get-tuple-element.124), channel_id=1, source_target_pairs={{0,2},{1,10},{2,18},{3,26},{4,0},{5,8},{6,16},{7,24},{8,6},{9,14},... | collective-permute-start | bytes 208904 | tf_op jit(solution)/shard_map/ppermute | solution.py:708
  22.9 16.9 %collective-permute-start.39 = (bf16[2,136,272]{2,1,0:T(8,128)(2,1)S(1)}, bf16[2,136,272]{2,1,0:T(8,128)(2,1)S(1)}, u32[]{:S(2)}, u32[]{:S(2)}) collective-permute-start(bf16[2,136,272]{2,1,0:T(8,128)(2,1)S(1)} %get-tuple-element.143), channel_id=1, source_target_pairs={{0,4},{4,0},{8,12},{12,8},{1,5},{5,1},{9,13},{13,9},{2,6},{6,2},{1... | collective-permute-start | bytes 443912 | tf_op jit(solution)/shard_map/ppermute | solution.py:49
  26.6 19.3 %collective-permute-start.40 = (bf16[2,136,272]{2,1,0:T(8,128)(2,1)S(1)}, bf16[2,136,272]{2,1,0:T(8,128)(2,1)S(1)}, u32[]{:S(2)}, u32[]{:S(2)}) collective-permute-start(bf16[2,136,272]{2,1,0:T(8,128)(2,1)S(1)} %get-tuple-element.144), channel_id=1, source_target_pairs={{0,8},{4,12},{8,0},{12,4},{1,9},{5,13},{9,1},{13,5},{2,10},{6,14},... | collective-permute-start | bytes 443912 | tf_op jit(solution)/shard_map/ppermute | solution.py:49
  26.6 19.4 %collective-permute-start.41 = (bf16[2,136,272]{2,1,0:T(8,128)(2,1)S(1)}, bf16[2,136,272]{2,1,0:T(8,128)(2,1)S(1)}, u32[]{:S(2)}, u32[]{:S(2)}) collective-permute-start(bf16[2,136,272]{2,1,0:T(8,128)(2,1)S(1)} %get-tuple-element.145), channel_id=1, source_target_pairs={{0,12},{4,8},{8,4},{12,0},{1,13},{5,9},{9,5},{13,1},{2,14},{6,10},... | collective-permute-start | bytes 443912 | tf_op jit(solution)/shard_map/ppermute | solution.py:49
  30.9 61.7 %collective-permute-start.14 = (bf16[144,1088]{1,0:T(8,128)(2,1)S(1)}, bf16[144,1088]{1,0:T(8,128)(2,1)S(1)}, u32[]{:S(2)}, u32[]{:S(2)}) collective-permute-start(bf16[144,1088]{1,0:T(8,128)(2,1)S(1)} %shard_map.283.b0), channel_id=1, source_target_pairs={{0,1},{1,2},{2,3},{3,0},{4,5},{5,6},{6,7},{7,4},{8,9},{9,10},{10,1... | collective-permute-start | bytes 940040 | tf_op jit(solution)/shard_map/ppermute | solution.py:53
  38.9 54.3 %collective-permute-start.15 = (bf16[144,1088]{1,0:T(8,128)(2,1)S(1)}, bf16[144,1088]{1,0:T(8,128)(2,1)S(1)}, u32[]{:S(2)}, u32[]{:S(2)}) collective-permute-start(bf16[144,1088]{1,0:T(8,128)(2,1)S(1)} %shard_map.283.b0), channel_id=1, source_target_pairs={{0,2},{1,3},{2,0},{3,1},{4,6},{5,7},{6,4},{7,5},{8,10},{9,11},{10,... | collective-permute-start | bytes 940040 | tf_op jit(solution)/shard_map/ppermute | solution.py:53
  45.9 14.5 %collective-permute-start.25 = (bf16[136,272]{1,0:T(8,128)(2,1)S(1)}, bf16[136,272]{1,0:T(8,128)(2,1)S(1)}, u32[]{:S(2)}, u32[]{:S(2)}) collective-permute-start(bf16[136,272]{1,0:T(8,128)(2,1)S(1)} %shard_map.285.b0), channel_id=1, source_target_pairs={{0,1},{1,2},{2,3},{3,0},{4,5},{5,6},{6,7},{7,4},{8,9},{9,10},{10,1... | collective-permute-start | bytes 221960 | tf_op jit(solution)/shard_map/ppermute | solution.py:53
  46.0 53.8 %collective-permute-start.16 = (bf16[144,1088]{1,0:T(8,128)(2,1)S(1)}, bf16[144,1088]{1,0:T(8,128)(2,1)S(1)}, u32[]{:S(2)}, u32[]{:S(2)}) collective-permute-start(bf16[144,1088]{1,0:T(8,128)(2,1)S(1)} %shard_map.283.b0), channel_id=1, source_target_pairs={{0,3},{1,0},{2,1},{3,2},{4,7},{5,4},{6,5},{7,6},{8,11},{9,8},{10,9... | collective-permute-start | bytes 940040 | tf_op jit(solution)/shard_map/ppermute | solution.py:53
  51.6 12.9 %collective-permute-start.26 = (bf16[136,272]{1,0:T(8,128)(2,1)S(1)}, bf16[136,272]{1,0:T(8,128)(2,1)S(1)}, u32[]{:S(2)}, u32[]{:S(2)}) collective-permute-start(bf16[136,272]{1,0:T(8,128)(2,1)S(1)} %shard_map.285.b0), channel_id=1, source_target_pairs={{0,2},{1,3},{2,0},{3,1},{4,6},{5,7},{6,4},{7,5},{8,10},{9,11},{10,... | collective-permute-start | bytes 221960 | tf_op jit(solution)/shard_map/ppermute | solution.py:53
  60.5 32.1 %collective-permute-start.27 = (bf16[136,272]{1,0:T(8,128)(2,1)S(1)}, bf16[136,272]{1,0:T(8,128)(2,1)S(1)}, u32[]{:S(2)}, u32[]{:S(2)}) collective-permute-start(bf16[136,272]{1,0:T(8,128)(2,1)S(1)} %shard_map.285.b0), channel_id=1, source_target_pairs={{0,3},{1,0},{2,1},{3,2},{4,7},{5,4},{6,5},{7,6},{8,11},{9,8},{10,9... | collective-permute-start | bytes 221960 | tf_op jit(solution)/shard_map/ppermute | solution.py:53
  64.5 39.2 %collective-permute-start.6 = (bf16[128,1088]{1,0:T(8,128)(2,1)S(1)}, bf16[128,1088]{1,0:T(8,128)(2,1)S(1)}, u32[]{:S(2)}, u32[]{:S(2)}) collective-permute-start(bf16[128,1088]{1,0:T(8,128)(2,1)S(1)} %get-tuple-element.127.refs_0_.n_own), channel_id=1, source_target_pairs={{0,12},{4,8},{8,4},{12,0},{1,13},{5,9},{9,5},{13,1},{2,14},{6,10},... | collective-permute-start | bytes 835592 | tf_op jit(solution)/shard_map/ppermute | solution.py:49
  92.6 13.8 %collective-permute-start.4 = (bf16[128,1088]{1,0:T(8,128)(2,1)S(1)}, bf16[128,1088]{1,0:T(8,128)(2,1)S(1)}, u32[]{:S(2)}, u32[]{:S(2)}) collective-permute-start(bf16[128,1088]{1,0:T(8,128)(2,1)S(1)} %get-tuple-element.127.refs_0_.n_own), channel_id=1, source_target_pairs={{0,4},{4,0},{8,12},{12,8},{1,5},{5,1},{9,13},{13,9},{2,6},{6,2},{1... | collective-permute-start | bytes 835592 | tf_op jit(solution)/shard_map/ppermute | solution.py:49
  92.6 13.8 %collective-permute-start.5 = (bf16[128,1088]{1,0:T(8,128)(2,1)S(1)}, bf16[128,1088]{1,0:T(8,128)(2,1)}, u32[]{:S(2)}, u32[]{:S(2)}) collective-permute-start(bf16[128,1088]{1,0:T(8,128)(2,1)S(1)} %get-tuple-element.127.refs_0_.n_own), channel_id=1, source_target_pairs={{0,8},{4,12},{8,0},{12,4},{1,9},{5,13},{9,1},{13,5},{2,10},{6,14},... | collective-permute-start | bytes 835592 | tf_op jit(solution)/shard_map/ppermute | solution.py:49
  93.2 13.7 %collective-permute-start.7 = (bf16[128,1088]{1,0:T(8,128)(2,1)S(1)}, bf16[128,1088]{1,0:T(8,128)(2,1)}, u32[]{:S(2)}, u32[]{:S(2)}) collective-permute-start(bf16[128,1088]{1,0:T(8,128)(2,1)S(1)} %get-tuple-element.127.refs_0_.n_own), channel_id=1, source_target_pairs={{0,16},{16,0},{1,17},{17,1},{2,18},{18,2},{3,19},{19,3},{4,20},{20... | collective-permute-start | bytes 835592 | tf_op jit(solution)/shard_map/ppermute | solution.py:45
  94.9 25.8 %all-to-all-start = ((bf16[8,136,192]{2,1,0:T(8,128)(2,1)}), bf16[8,136,192]{2,1,0:T(8,128)(2,1)S(1)}, u32[]{:S(2)}, u32[]{:S(2)}) async-start(bf16[8,136,192]{2,1,0:T(8,128)(2,1)} %shard_map.286), calls=%async_computation | async-start | bytes 1114112 | tf_op jit(solution)/shard_map/all_to_all | solution.py:746
  99.2 113.1 %all-gather.5.cloned.1.call-start = ((), (), s32[]{:S(2)}) async-start(), calls=%async_computation.4 | async-start | bytes 1566720 | tf_op jit(solution)/shard_map/all_gather | solution.py:761
  103.8 17.5 %collective-permute-start.10 = (bf16[128,1088]{1,0:T(8,128)(2,1)S(1)}, bf16[128,1088]{1,0:T(8,128)(2,1)S(1)}, u32[]{:S(2)}, u32[]{:S(2)}) collective-permute-start(bf16[128,1088]{1,0:T(8,128)(2,1)S(1)} %collective-permute-done.6.refs_3_), channel_id=1, source_target_pairs={{0,16},{16,0},{1,17},{17,1},{2,18},{18,2},{3,19},{19,3},{4,20},{20... | collective-permute-start | bytes 835592 | tf_op jit(solution)/shard_map/ppermute | solution.py:45
  106.4 14.9 %collective-permute-start.8 = (bf16[128,1088]{1,0:T(8,128)(2,1)S(1)}, bf16[128,1088]{1,0:T(8,128)(2,1)S(1)}, u32[]{:S(2)}, u32[]{:S(2)}) collective-permute-start(bf16[128,1088]{1,0:T(8,128)(2,1)S(1)} %collective-permute-done.4.refs_1_), channel_id=1, source_target_pairs={{0,16},{16,0},{1,17},{17,1},{2,18},{18,2},{3,19},{19,3},{4,20},{20... | collective-permute-start | bytes 835592 | tf_op jit(solution)/shard_map/ppermute | solution.py:45
  106.4 14.9 %collective-permute-start.9 = (bf16[128,1088]{1,0:T(8,128)(2,1)}, bf16[128,1088]{1,0:T(8,128)(2,1)S(1)}, u32[]{:S(2)}, u32[]{:S(2)}) collective-permute-start(bf16[128,1088]{1,0:T(8,128)(2,1)} %collective-permute-done.5.refs_2_), channel_id=1, source_target_pairs={{0,16},{16,0},{1,17},{17,1},{2,18},{18,2},{3,19},{19,3},{4,20},{20... | collective-permute-start | bytes 835592 | tf_op jit(solution)/shard_map/ppermute | solution.py:45
  137.1 22.4 %collective-permute-start.28 = (bf16[4,128,1088]{1,2,0:T(8,128)(2,1)S(1)}, bf16[4,128,1088]{1,2,0:T(8,128)(2,1)}, u32[]{:S(2)}, u32[]{:S(2)}) collective-permute-start(bf16[4,128,1088]{1,2,0:T(8,128)(2,1)S(1)} %copy.49), channel_id=1, source_target_pairs={{0,16},{16,0},{1,17},{17,1},{2,18},{18,2},{3,19},{19,3},{4,20},{20... | collective-permute-start | bytes 3342344 | tf_op jit(solution)/shard_map/ppermute | solution.py:45
  137.3 275.0 %reduce-scatter.2.cloned.1.call-start = ((), (), s32[]{:S(2)}) async-start(), calls=%async_computation.3 | async-start | bytes 3133440 | tf_op jit(solution)/shard_map/reduce_scatter | solution.py:848
  153.5 13.3 %collective-permute-start.46 = (bf16[128,1088]{1,0:T(8,128)(2,1)S(1)}, bf16[128,1088]{1,0:T(8,128)(2,1)S(1)}, u32[]{:S(2)}, u32[]{:S(2)}) collective-permute-start(bf16[128,1088]{1,0:T(8,128)(2,1)S(1)} %shard_map.293.refs_0_.g_own), channel_id=1, source_target_pairs={{0,4},{4,0},{8,12},{12,8},{1,5},{5,1},{9,13},{13,9},{2,6},{6,2},{1... | collective-permute-start | bytes 835592 | tf_op jit(solution)/shard_map/ppermute | solution.py:49
  153.6 15.1 %collective-permute-start.47 = (bf16[128,1088]{1,0:T(8,128)(2,1)S(1)}, bf16[128,1088]{1,0:T(8,128)(2,1)S(1)}, u32[]{:S(2)}, u32[]{:S(2)}) collective-permute-start(bf16[128,1088]{1,0:T(8,128)(2,1)S(1)} %shard_map.293.refs_0_.g_own), channel_id=1, source_target_pairs={{0,8},{4,12},{8,0},{12,4},{1,9},{5,13},{9,1},{13,5},{2,10},{6,14},... | collective-permute-start | bytes 835592 | tf_op jit(solution)/shard_map/ppermute | solution.py:49
  163.4 22.7 %collective-permute-start.31 = (bf16[128,1088]{1,0:T(8,128)(2,1)S(1)}, bf16[128,1088]{1,0:T(8,128)(2,1)S(1)}, u32[]{:S(2)}, u32[]{:S(2)}) collective-permute-start(bf16[128,1088]{1,0:T(8,128)(2,1)S(1)} %get-tuple-element.139), channel_id=1, source_target_pairs={{0,12},{4,8},{8,4},{12,0},{1,13},{5,9},{9,5},{13,1},{2,14},{6,10},... | collective-permute-start | bytes 835592 | tf_op jit(solution)/shard_map/ppermute | solution.py:49
  166.8 22.6 %collective-permute-start.48 = (bf16[128,1088]{1,0:T(8,128)(2,1)S(1)}, bf16[128,1088]{1,0:T(8,128)(2,1)S(1)}, u32[]{:S(2)}, u32[]{:S(2)}) collective-permute-start(bf16[128,1088]{1,0:T(8,128)(2,1)S(1)} %shard_map.293.refs_0_.g_own), channel_id=1, source_target_pairs={{0,12},{4,8},{8,4},{12,0},{1,13},{5,9},{9,5},{13,1},{2,14},{6,10},... | collective-permute-start | bytes 835592 | tf_op jit(solution)/shard_map/ppermute | solution.py:49
  168.6 21.3 %collective-permute-start.49 = (bf16[128,1088]{1,0:T(8,128)(2,1)S(1)}, bf16[128,1088]{1,0:T(8,128)(2,1)S(1)}, u32[]{:S(2)}, u32[]{:S(2)}) collective-permute-start(bf16[128,1088]{1,0:T(8,128)(2,1)S(1)} %shard_map.293.refs_0_.g_own), channel_id=1, source_target_pairs={{0,16},{16,0},{1,17},{17,1},{2,18},{18,2},{3,19},{19,3},{4,20},{20... | collective-permute-start | bytes 835592 | tf_op jit(solution)/shard_map/ppermute | solution.py:45
  172.4 19.0 %collective-permute-start.50 = (bf16[128,1088]{1,0:T(8,128)(2,1)S(1)}, bf16[128,1088]{1,0:T(8,128)(2,1)S(1)}, u32[]{:S(2)}, u32[]{:S(2)}) collective-permute-start(bf16[128,1088]{1,0:T(8,128)(2,1)S(1)} %collective-permute-done.46.refs_1_), channel_id=1, source_target_pairs={{0,16},{16,0},{1,17},{17,1},{2,18},{18,2},{3,19},{19,3},{4,20},{20... | collective-permute-start | bytes 835592 | tf_op jit(solution)/shard_map/ppermute | solution.py:45
  174.1 17.3 %collective-permute-start.51 = (bf16[128,1088]{1,0:T(8,128)(2,1)S(1)}, bf16[128,1088]{1,0:T(8,128)(2,1)S(1)}, u32[]{:S(2)}, u32[]{:S(2)}) collective-permute-start(bf16[128,1088]{1,0:T(8,128)(2,1)S(1)} %collective-permute-done.47.refs_2_), channel_id=1, source_target_pairs={{0,16},{16,0},{1,17},{17,1},{2,18},{18,2},{3,19},{19,3},{4,20},{20... | collective-permute-start | bytes 835592 | tf_op jit(solution)/shard_map/ppermute | solution.py:45
  189.4 13.2 %collective-permute-start.33 = (bf16[128,1088]{1,0:T(8,128)(2,1)S(1)}, bf16[128,1088]{1,0:T(8,128)(2,1)S(1)}, u32[]{:S(2)}, u32[]{:S(2)}) collective-permute-start(bf16[128,1088]{1,0:T(8,128)(2,1)S(1)} %get-tuple-element.141.refs_0_), channel_id=1, source_target_pairs={{0,8},{4,12},{8,0},{12,4},{1,9},{5,13},{9,1},{13,5},{2,10},{6,14},... | collective-permute-start | bytes 835592 | tf_op jit(solution)/shard_map/ppermute | solution.py:49
  189.9 14.6 %collective-permute-start.34 = (bf16[128,1088]{1,0:T(8,128)(2,1)S(1)}, bf16[128,1088]{1,0:T(8,128)(2,1)S(1)}, u32[]{:S(2)}, u32[]{:S(2)}) collective-permute-start(bf16[128,1088]{1,0:T(8,128)(2,1)S(1)} %get-tuple-element.141.refs_0_), channel_id=1, source_target_pairs={{0,12},{4,8},{8,4},{12,0},{1,13},{5,9},{9,5},{13,1},{2,14},{6,10},... | collective-permute-start | bytes 835592 | tf_op jit(solution)/shard_map/ppermute | solution.py:49
  191.4 13.4 %collective-permute-start.52 = (bf16[128,1088]{1,0:T(8,128)(2,1)S(1)}, bf16[128,1088]{1,0:T(8,128)(2,1)}, u32[]{:S(2)}, u32[]{:S(2)}) collective-permute-start(bf16[128,1088]{1,0:T(8,128)(2,1)S(1)} %collective-permute-done.48.refs_3_), channel_id=1, source_target_pairs={{0,16},{16,0},{1,17},{17,1},{2,18},{18,2},{3,19},{19,3},{4,20},{20... | collective-permute-start | bytes 835592 | tf_op jit(solution)/shard_map/ppermute | solution.py:45
  191.4 20.9 %collective-permute-start.35 = (bf16[128,1088]{1,0:T(8,128)(2,1)S(1)}, bf16[128,1088]{1,0:T(8,128)(2,1)}, u32[]{:S(2)}, u32[]{:S(2)}) collective-permute-start(bf16[128,1088]{1,0:T(8,128)(2,1)S(1)} %get-tuple-element.141.refs_0_), channel_id=1, source_target_pairs={{0,16},{16,0},{1,17},{17,1},{2,18},{18,2},{3,19},{19,3},{4,20},{20... | collective-permute-start | bytes 835592 | tf_op jit(solution)/shard_map/ppermute | solution.py:45
  197.7 14.6 %collective-permute-start.36 = (bf16[128,1088]{1,0:T(8,128)(2,1)S(1)}, bf16[128,1088]{1,0:T(8,128)(2,1)}, u32[]{:S(2)}, u32[]{:S(2)}) collective-permute-start(bf16[128,1088]{1,0:T(8,128)(2,1)S(1)} %collective-permute-done.32.refs_1_), channel_id=1, source_target_pairs={{0,16},{16,0},{1,17},{17,1},{2,18},{18,2},{3,19},{19,3},{4,20},{20... | collective-permute-start | bytes 835592 | tf_op jit(solution)/shard_map/ppermute | solution.py:45
  243.1 15.5 %collective-permute-start.63 = (bf16[128,1088]{1,0:T(8,128)(2,1)S(1)}, bf16[128,1088]{1,0:T(8,128)(2,1)S(1)}, u32[]{:S(2)}, u32[]{:S(2)}) collective-permute-start(bf16[128,1088]{1,0:T(8,128)(2,1)S(1)} %get-tuple-element.169), channel_id=1, source_target_pairs={{0,8},{4,12},{8,0},{12,4},{1,9},{5,13},{9,1},{13,5},{2,10},{6,14},... | collective-permute-start | bytes 835592 | tf_op jit(solution)/shard_map/ppermute | solution.py:49
  244.8 13.7 %collective-permute-start.64 = (bf16[128,1088]{1,0:T(8,128)(2,1)S(1)}, bf16[128,1088]{1,0:T(8,128)(2,1)S(1)}, u32[]{:S(2)}, u32[]{:S(2)}) collective-permute-start(bf16[128,1088]{1,0:T(8,128)(2,1)S(1)} %get-tuple-element.170), channel_id=1, source_target_pairs={{0,12},{4,8},{8,4},{12,0},{1,13},{5,9},{9,5},{13,1},{2,14},{6,10},... | collective-permute-start | bytes 835592 | tf_op jit(solution)/shard_map/ppermute | solution.py:49
  262.1 14.7 %collective-permute-start.66 = (bf16[128,1088]{1,0:T(8,128)(2,1)S(1)}, bf16[128,1088]{1,0:T(8,128)(2,1)S(1)}, u32[]{:S(2)}, u32[]{:S(2)}) collective-permute-start(bf16[128,1088]{1,0:T(8,128)(2,1)S(1)} %get-tuple-element.171.refs_0_), channel_id=1, source_target_pairs={{0,8},{4,12},{8,0},{12,4},{1,9},{5,13},{9,1},{13,5},{2,10},{6,14},... | collective-permute-start | bytes 835592 | tf_op jit(solution)/shard_map/ppermute | solution.py:49
  262.8 14.0 %collective-permute-start.67 = (bf16[128,1088]{1,0:T(8,128)(2,1)S(1)}, bf16[128,1088]{1,0:T(8,128)(2,1)}, u32[]{:S(2)}, u32[]{:S(2)}) collective-permute-start(bf16[128,1088]{1,0:T(8,128)(2,1)S(1)} %get-tuple-element.171.refs_0_), channel_id=1, source_target_pairs={{0,12},{4,8},{8,4},{12,0},{1,13},{5,9},{9,5},{13,1},{2,14},{6,10},... | collective-permute-start | bytes 835592 | tf_op jit(solution)/shard_map/ppermute | solution.py:49
  264.2 17.8 %collective-permute-start.68 = (bf16[128,1088]{1,0:T(8,128)(2,1)S(1)}, bf16[128,1088]{1,0:T(8,128)(2,1)}, u32[]{:S(2)}, u32[]{:S(2)}) collective-permute-start(bf16[128,1088]{1,0:T(8,128)(2,1)S(1)} %get-tuple-element.171.refs_0_), channel_id=1, source_target_pairs={{0,16},{16,0},{1,17},{17,1},{2,18},{18,2},{3,19},{19,3},{4,20},{20... | collective-permute-start | bytes 835592 | tf_op jit(solution)/shard_map/ppermute | solution.py:45
  281.8 15.4 %collective-permute-start.53 = (bf16[4,128,1088]{1,2,0:T(8,128)(2,1)S(1)}, bf16[4,128,1088]{1,2,0:T(8,128)(2,1)}, u32[]{:S(2)}, u32[]{:S(2)}) collective-permute-start(bf16[4,128,1088]{1,2,0:T(8,128)(2,1)S(1)} %copy.54), channel_id=1, source_target_pairs={{0,16},{16,0},{1,17},{17,1},{2,18},{18,2},{3,19},{19,3},{4,20},{20... | collective-permute-start | bytes 3342344 | tf_op jit(solution)/shard_map/ppermute | solution.py:45
  296.7 40.4 %collective-permute-start.72 = (bf16[4,128,1088]{1,2,0:T(8,128)(2,1)}, bf16[4,128,1088]{1,2,0:T(8,128)(2,1)}, u32[]{:S(2)}, u32[]{:S(2)}) collective-permute-start(bf16[4,128,1088]{1,2,0:T(8,128)(2,1)} %copy.58), channel_id=1, source_target_pairs={{0,16},{16,0},{1,17},{17,1},{2,18},{18,2},{3,19},{19,3},{4,20},{20... | collective-permute-start | bytes 3342344 | tf_op jit(solution)/shard_map/ppermute | solution.py:45
  302.8 12.2 %collective-permute-start.54 = (bf16[128,1088]{1,0:T(8,128)(2,1)}, bf16[128,1088]{1,0:T(8,128)(2,1)S(1)}, u32[]{:S(2)}, u32[]{:S(2)}) collective-permute-start(bf16[128,1088]{1,0:T(8,128)(2,1)} %get-tuple-element.157), channel_id=1, source_target_pairs={{0,4},{4,0},{8,12},{12,8},{1,5},{5,1},{9,13},{13,9},{2,6},{6,2},{1... | collective-permute-start | bytes 835592 | tf_op jit(solution)/shard_map/ppermute | solution.py:49
  303.2 15.3 %collective-permute-start.55 = (bf16[128,1088]{1,0:T(8,128)(2,1)}, bf16[128,1088]{1,0:T(8,128)(2,1)S(1)}, u32[]{:S(2)}, u32[]{:S(2)}) collective-permute-start(bf16[128,1088]{1,0:T(8,128)(2,1)} %get-tuple-element.158), channel_id=1, source_target_pairs={{0,8},{4,12},{8,0},{12,4},{1,9},{5,13},{9,1},{13,5},{2,10},{6,14},... | collective-permute-start | bytes 835592 | tf_op jit(solution)/shard_map/ppermute | solution.py:49
  304.9 13.5 %collective-permute-start.56 = (bf16[128,1088]{1,0:T(8,128)(2,1)}, bf16[128,1088]{1,0:T(8,128)(2,1)S(1)}, u32[]{:S(2)}, u32[]{:S(2)}) collective-permute-start(bf16[128,1088]{1,0:T(8,128)(2,1)} %get-tuple-element.159), channel_id=1, source_target_pairs={{0,12},{4,8},{8,4},{12,0},{1,13},{5,9},{9,5},{13,1},{2,14},{6,10},... | collective-permute-start | bytes 835592 | tf_op jit(solution)/shard_map/ppermute | solution.py:49
  314.1 29.5 %collective-permute-start.73 = (bf16[4,32,1088]{2,1,0:T(8,128)(2,1)}, bf16[4,32,1088]{2,1,0:T(8,128)(2,1)}, u32[]{:S(2)}, u32[]{:S(2)}) collective-permute-start(bf16[4,32,1088]{2,1,0:T(8,128)(2,1)} %get-tuple-element.185), channel_id=1, source_target_pairs={{0,16},{16,0},{1,17},{17,1},{2,18},{18,2},{3,19},{19,3},{4,20},{20... | collective-permute-start | bytes 835592 | tf_op jit(solution)/shard_map/ppermute | solution.py:45
  321.0 28.5 %collective-permute-start.57 = (bf16[272,128]{1,0:T(8,128)(2,1)}, bf16[272,128]{1,0:T(8,128)(2,1)S(1)}, u32[]{:S(2)}, u32[]{:S(2)}) collective-permute-start(bf16[272,128]{1,0:T(8,128)(2,1)} %get-tuple-element.161), channel_id=1, source_target_pairs={{0,0},{8,1},{16,2},{24,3},{2,4},{10,5},{18,6},{26,7},{4,8},{12,9},... | collective-permute-start | bytes 208904 | tf_op jit(solution)/shard_map/ppermute | solution.py:711
  322.6 27.0 %collective-permute-start.58 = (bf16[272,128]{1,0:T(8,128)(2,1)}, bf16[272,128]{1,0:T(8,128)(2,1)}, u32[]{:S(2)}, u32[]{:S(2)}) collective-permute-start(bf16[272,128]{1,0:T(8,128)(2,1)} %get-tuple-element.162), channel_id=1, source_target_pairs={{2,0},{10,1},{18,2},{26,3},{0,4},{8,5},{16,6},{24,7},{6,8},{14,9},... | collective-permute-start | bytes 208904 | tf_op jit(solution)/shard_map/ppermute | solution.py:711
  326.2 23.5 %collective-permute-start.59 = (bf16[272,128]{1,0:T(8,128)(2,1)}, bf16[272,128]{1,0:T(8,128)(2,1)}, u32[]{:S(2)}, u32[]{:S(2)}) collective-permute-start(bf16[272,128]{1,0:T(8,128)(2,1)} %get-tuple-element.163), channel_id=1, source_target_pairs={{4,0},{12,1},{20,2},{28,3},{6,4},{14,5},{22,6},{30,7},{0,8},{8,9},... | collective-permute-start | bytes 208904 | tf_op jit(solution)/shard_map/ppermute | solution.py:711
  329.1 30.9 %all-to-all-start.1 = ((bf16[8,136,192]{2,1,0:T(8,128)(2,1)}), bf16[8,136,192]{2,1,0:T(8,128)(2,1)}, u32[]{:S(2)}, u32[]{:S(2)}) async-start(bf16[8,136,192]{2,1,0:T(8,128)(2,1)} %shard_map.310), calls=%async_computation.1 | async-start | bytes 1114112 | tf_op jit(solution)/shard_map/all_to_all | solution.py:956
  337.1 16.0 %collective-permute-start.60 = (bf16[272,128]{1,0:T(8,128)(2,1)}, bf16[272,128]{1,0:T(8,128)(2,1)}, u32[]{:S(2)}, u32[]{:S(2)}) collective-permute-start(bf16[272,128]{1,0:T(8,128)(2,1)} %get-tuple-element.164), channel_id=1, source_target_pairs={{6,0},{14,1},{22,2},{30,3},{4,4},{12,5},{20,6},{28,7},{2,8},{10,9}... | collective-permute-start | bytes 208904 | tf_op jit(solution)/shard_map/ppermute | solution.py:711
  353.1 25.1 %collective-permute-start.90 = (bf16[128,1088]{1,0:T(8,128)(2,1)S(1)}, bf16[128,1088]{1,0:T(8,128)(2,1)S(1)}, u32[]{:S(2)}, u32[]{:S(2)}) collective-permute-start(bf16[128,1088]{1,0:T(8,128)(2,1)S(1)} %copy-done.18), channel_id=1, source_target_pairs={{0,2},{1,3},{2,0},{3,1},{4,6},{5,7},{6,4},{7,5},{8,10},{9,11},{10,... | collective-permute-start | bytes 835592 | tf_op jit(solution)/shard_map/ppermute | solution.py:53
  355.3 31.0 %collective-permute-start.91 = (bf16[128,1088]{1,0:T(8,128)(2,1)S(1)}, bf16[128,1088]{1,0:T(8,128)(2,1)S(1)}, u32[]{:S(2)}, u32[]{:S(2)}) collective-permute-start(bf16[128,1088]{1,0:T(8,128)(2,1)S(1)} %copy-done.16), channel_id=1, source_target_pairs={{0,3},{1,0},{2,1},{3,2},{4,7},{5,4},{6,5},{7,6},{8,11},{9,8},{10,9... | collective-permute-start | bytes 835592 | tf_op jit(solution)/shard_map/ppermute | solution.py:53
  356.9 14.7 %collective-permute-start.76 = (bf16[128,1088]{1,0:T(8,128)(2,1)}, bf16[128,1088]{1,0:T(8,128)(2,1)S(1)}, u32[]{:S(2)}, u32[]{:S(2)}) collective-permute-start(bf16[128,1088]{1,0:T(8,128)(2,1)} %get-tuple-element.189), channel_id=1, source_target_pairs={{0,12},{4,8},{8,4},{12,0},{1,13},{5,9},{9,5},{13,1},{2,14},{6,10},... | collective-permute-start | bytes 835592 | tf_op jit(solution)/shard_map/ppermute | solution.py:49
  367.4 14.4 %collective-permute-start.103 = (bf16[136,272]{1,0:T(8,128)(2,1)S(1)}, bf16[136,272]{1,0:T(8,128)(2,1)S(1)}, u32[]{:S(2)}, u32[]{:S(2)}) collective-permute-start(bf16[136,272]{1,0:T(8,128)(2,1)S(1)} %get-tuple-element.220), channel_id=1, source_target_pairs={{0,2},{1,3},{2,0},{3,1},{4,6},{5,7},{6,4},{7,5},{8,10},{9,11},{10,... | collective-permute-start | bytes 221960 | tf_op jit(solution)/shard_map/ppermute | solution.py:53
  386.2 13.2 %collective-permute-start.105 = (bf16[136,272]{1,0:T(8,128)(2,1)S(1)}, bf16[136,272]{1,0:T(8,128)(2,1)S(1)}, u32[]{:S(2)}, u32[]{:S(2)}) collective-permute-start(bf16[136,272]{1,0:T(8,128)(2,1)S(1)} %shard_map.312.mine), channel_id=1, source_target_pairs={{0,16},{16,0},{1,17},{17,1},{2,18},{18,2},{3,19},{19,3},{4,20},{20... | collective-permute-start | bytes 221960 | tf_op jit(solution)/shard_map/ppermute | solution.py:45
  386.3 15.0 %collective-permute-start.80 = (bf16[272,128]{1,0:T(8,128)(2,1)}, bf16[272,128]{1,0:T(8,128)(2,1)S(1)}, u32[]{:S(2)}, u32[]{:S(2)}) collective-permute-start(bf16[272,128]{1,0:T(8,128)(2,1)} %get-tuple-element.195), channel_id=1, source_target_pairs={{0,0},{8,1},{16,2},{24,3},{2,4},{10,5},{18,6},{26,7},{4,8},{12,9},... | collective-permute-start | bytes 208904 | tf_op jit(solution)/shard_map/ppermute | solution.py:711
  387.8 14.8 %collective-permute-start.81 = (bf16[272,128]{1,0:T(8,128)(2,1)}, bf16[272,128]{1,0:T(8,128)(2,1)S(1)}, u32[]{:S(2)}, u32[]{:S(2)}) collective-permute-start(bf16[272,128]{1,0:T(8,128)(2,1)} %get-tuple-element.196), channel_id=1, source_target_pairs={{2,0},{10,1},{18,2},{26,3},{0,4},{8,5},{16,6},{24,7},{6,8},{14,9},... | collective-permute-start | bytes 208904 | tf_op jit(solution)/shard_map/ppermute | solution.py:711
  399.1 12.2 %collective-permute-start.96 = (bf16[144,272]{1,0:T(8,128)(2,1)S(1)}, bf16[144,272]{1,0:T(8,128)(2,1)S(1)}, u32[]{:S(2)}, u32[]{:S(2)}) collective-permute-start(bf16[144,272]{1,0:T(8,128)(2,1)S(1)} %get-tuple-element.213), channel_id=1, source_target_pairs={{0,8},{4,12},{8,0},{12,4},{1,9},{5,13},{9,1},{13,5},{2,10},{6,14},... | collective-permute-start | bytes 235016 | tf_op jit(solution)/shard_map/ppermute | solution.py:49
  401.2 14.9 %collective-permute-start.97 = (bf16[144,272]{1,0:T(8,128)(2,1)S(1)}, bf16[144,272]{1,0:T(8,128)(2,1)S(1)}, u32[]{:S(2)}, u32[]{:S(2)}) collective-permute-start(bf16[144,272]{1,0:T(8,128)(2,1)S(1)} %get-tuple-element.214), channel_id=1, source_target_pairs={{0,12},{4,8},{8,4},{12,0},{1,13},{5,9},{9,5},{13,1},{2,14},{6,10},... | collective-permute-start | bytes 235016 | tf_op jit(solution)/shard_map/ppermute | solution.py:49
  402.6 13.9 %collective-permute-start.95 = (bf16[144,272]{1,0:T(8,128)(2,1)S(1)}, bf16[144,272]{1,0:T(8,128)(2,1)S(1)}, u32[]{:S(2)}, u32[]{:S(2)}) collective-permute-start(bf16[144,272]{1,0:T(8,128)(2,1)S(1)} %get-tuple-element.212), channel_id=1, source_target_pairs={{0,4},{4,0},{8,12},{12,8},{1,5},{5,1},{9,13},{13,9},{2,6},{6,2},{1... | collective-permute-start | bytes 235016 | tf_op jit(solution)/shard_map/ppermute | solution.py:49
  402.9 15.2 %collective-permute-start.98 = (bf16[144,272]{1,0:T(8,128)(2,1)S(1)}, bf16[144,272]{1,0:T(8,128)(2,1)S(1)}, u32[]{:S(2)}, u32[]{:S(2)}) collective-permute-start(bf16[144,272]{1,0:T(8,128)(2,1)S(1)} %get-tuple-element.211.refs_0_), channel_id=1, source_target_pairs={{0,16},{16,0},{1,17},{17,1},{2,18},{18,2},{3,19},{19,3},{4,20},{20... | collective-permute-start | bytes 235016 | tf_op jit(solution)/shard_map/ppermute | solution.py:45
  (151 other events, 1169.4 us)
Sparse Core Ops, SparseCore 0:
  51.7 42.1 all-gather.6
  137.4 34.3 all-gather.4
  239.7 49.4 reduce-scatter.1
